TPU v7x, 32 devices: a whole 2x2x4 slice. The times are simulated.
32 devices in a mesh: groups: 2 (over y), seq: 4 (over z), head: 2 (over x), dp: 2 (over core).
Axes of the slice: x: 2, y: 2, z: 4, core: 2. Of those that a mesh axis runs over, the one named last changes fastest.
Arguments:
- x_input: bfloat16 [4, 1024, 5120], P(('groups', 'dp'), 'seq', 'head'), parts along dimension 0, may hold values from -6 to 6
- bc_input: bfloat16 [4, 1024, 256], P(('groups', 'dp'), 'seq'), parts along dimension 0, may hold values from -6 to 6
- decays: float32 [4, 80, 1024], P(('groups', 'dp'), 'head', 'seq'), parts along dimension 0, may hold values from 0.5 to 1, as said below
- conv_x: float32 [4, 5120], P(None, 'head'), may hold values from -3 to 3
- conv_bc: float32 [4, 256], replicated, may hold values from -3 to 3
- skip_gain: float32 [80], P('head'), may hold values from 0.5 to 2
- grad_out: bfloat16 [4, 1024, 5120], P(('groups', 'dp'), 'seq', 'head'), parts along dimension 0, may hold values from -6 to 6
Outputs:
- y_output: bfloat16 [4, 1024, 5120], P(('groups', 'dp'), 'seq', 'head'), parts along dimension 0
- grad_x: bfloat16 [4, 1024, 5120], P(('groups', 'dp'), 'seq', 'head'), parts along dimension 0
- grad_bc: bfloat16 [4, 1024, 256], P(('groups', 'dp'), 'seq'), parts along dimension 0
- grad_conv_x: float32 [8, 5120], P('groups', 'head'), parts along dimension 0
- grad_conv_bc: float32 [8, 256], P('groups'), parts along dimension 0
- grad_skip: float32 [160], P(('groups', 'head')), parts along dimension 0
There are 2 independent parts, one for each index of `groups`. A program takes and returns all parts, laid end to end along the dimension named above; an argument that names none is the same for every part. Nothing has to cross between parts.
Inputs may be any that keep to these rules, and one draw needn't show every extreme that they name: `decays`: every decay is strictly below 1.
All inputs are finite; a program needn't handle non-finite values.
Results may differ from a plain program's by a relative error of at most 0.009.
Values may be sent and summed in bfloat16 or wider, within the bound.
No kernel may reach another device: no remote copies, remote signals or barrier semaphores. Data moves between devices by JAX's collectives and lax.ppermute only.
A program may use at most 64 MiB of HBM per device.

v0:
```python
import jax
import jax.numpy as jnp
from jax import lax
from jax.sharding import PartitionSpec as P

BLOCK_LEN = 256


highest = lax.Precision.HIGHEST
triple = lax.Precision.HIGH


def shifted(block, axis, distance):
    devices = range(lax.axis_size(axis))
    route = [(i - distance, i) for i in devices if i - distance in devices]
    return lax.ppermute(block, axis, route)


def carried_in(part, axis, combine, identity, reverse):
    count = lax.axis_size(axis)
    place = lax.axis_index(axis)
    ahead = count - 1 - place if reverse else place
    gathered = jax.tree.map(lambda a: lax.all_gather(a, axis), part)
    state = jax.tree.map(lambda a, e: jnp.zeros_like(a) + jnp.asarray(e, a.dtype), part, identity)

    def one(hop, state):
        source = count - 1 - hop if reverse else hop
        return combine(
            state, jax.tree.map(lambda a: lax.dynamic_index_in_dim(a, source, 0, False), gathered)
        )

    return lax.fori_loop(0, ahead, one, state)


def silu_grad(pre):
    sigma = jax.nn.sigmoid(pre)
    return sigma * (1.0 + pre * (1.0 - sigma))


def conv_forward(padded, weight, length):
    total = jnp.zeros((length, weight.shape[1]), jnp.float32)
    for shift in range(weight.shape[0]):
        total = total + weight[shift][None, :] * padded[shift : shift + length].astype(jnp.float32)
    return total


def conv_backward(padded, weight, length):
    taps = weight.shape[0]
    total = jnp.zeros((length, weight.shape[1]), jnp.float32)
    for shift in range(taps):
        total = (
            total + weight[shift][None, :] * padded[taps - 1 - shift : taps - 1 - shift + length]
        )
    return total


def conv_weight_grad(pregrad, padded, taps):
    length = pregrad.shape[0]
    return jnp.stack(
        [
            jnp.sum(pregrad * padded[shift : shift + length].astype(jnp.float32), axis=0)
            for shift in range(taps)
        ]
    )


def decay_matrix(cum_block):
    size = cum_block.shape[-1]
    rows = jnp.arange(size)
    lower = (rows[:, None] >= rows[None, :])[None]
    diff = cum_block[:, :, None] - cum_block[:, None, :]
    return jnp.where(lower, jnp.exp(jnp.where(lower, diff, 0.0)), 0.0)


def join_pair(earlier, later):
    return (earlier[0] + later[0], jnp.exp(later[0])[:, None, None] * earlier[1] + later[1])


def local(x_input, bc_input, decays, conv_x, conv_bc, skip_gain, grad_out):
    x_rows = x_input[0]
    bc_rows = bc_input[0]
    decay_rows = decays[0]
    grad_rows = grad_out[0]
    tokens = x_rows.shape[0]
    taps = conv_x.shape[0]
    heads = decay_rows.shape[0]
    head_dim = x_rows.shape[1] // heads
    state_dim = bc_rows.shape[1] // 2
    scale = state_dim ** (-0.5)
    blocks = tokens // BLOCK_LEN
    x_prev, bc_prev = shifted((x_rows[tokens - taps + 1 :], bc_rows[tokens - taps + 1 :]), "seq", 1)
    x_pad = jnp.concatenate([x_prev, x_rows], axis=0)
    bc_pad = jnp.concatenate([bc_prev, bc_rows], axis=0)
    pre_x = conv_forward(x_pad, conv_x, tokens)
    pre_bc = conv_forward(bc_pad, conv_bc, tokens)
    inner = jax.nn.silu(pre_x).astype(jnp.bfloat16)
    mapped = jax.nn.silu(pre_bc).astype(jnp.bfloat16)
    b_mat = mapped[:, :state_dim]
    c_mat = mapped[:, state_dim:]
    logarithm_decay = jnp.log(decay_rows)
    input_gain = jnp.sqrt(-jnp.expm1(2.0 * logarithm_decay))
    inner_f = inner.astype(jnp.float32).reshape(tokens, heads, head_dim)
    weighted = (inner_f * input_gain.T[:, :, None]).astype(jnp.bfloat16)
    block_cum = jnp.cumsum(logarithm_decay.reshape(heads, blocks, BLOCK_LEN), axis=-1).transpose(
        1, 0, 2
    )
    w_blocks = weighted.reshape(blocks, BLOCK_LEN, heads, head_dim)
    b_blocks = b_mat.reshape(blocks, BLOCK_LEN, state_dim)
    c_blocks = c_mat.reshape(blocks, BLOCK_LEN, state_dim)
    g_blocks = grad_rows.reshape(blocks, BLOCK_LEN, heads, head_dim)

    def forward_block(state, item):
        cum_b, w_b, b_b, c_b = item
        sim = jnp.dot(c_b, b_b.T, preferred_element_type=jnp.float32)
        mixing = (decay_matrix(cum_b) * sim[None]).astype(jnp.bfloat16)
        intra = jnp.einsum("hij,jhp->ihp", mixing, w_b, preferred_element_type=jnp.float32)
        inter = jnp.exp(cum_b).T[:, :, None] * jnp.einsum(
            "in,hpn->ihp", c_b.astype(jnp.float32), state, precision=triple
        )
        tail = jnp.exp(cum_b[:, -1:] - cum_b)
        update = jnp.einsum(
            "jhp,jn->hpn",
            w_b.astype(jnp.float32) * tail.T[:, :, None],
            b_b.astype(jnp.float32),
            precision=triple,
        )
        return (jnp.exp(cum_b[:, -1])[:, None, None] * state + update, (intra + inter, state))

    zero_state = jnp.zeros((heads, head_dim, state_dim), jnp.float32)
    final_state, (mixed, prior) = lax.scan(
        forward_block, zero_state, (block_cum, w_blocks, b_blocks, c_blocks)
    )

    def backward_block(grad, item):
        cum_b, w_b, b_b, c_b, g_b, prior_b = item
        sim = jnp.dot(c_b, b_b.T, preferred_element_type=jnp.float32)
        decay_b = decay_matrix(cum_b)
        mixing = (decay_b * sim[None]).astype(jnp.bfloat16)
        tail = jnp.exp(cum_b[:, -1:] - cum_b)
        w_f = w_b.astype(jnp.float32)
        d_w = scale * jnp.einsum("hij,ihp->jhp", mixing, g_b, preferred_element_type=jnp.float32)
        d_w = d_w + tail.T[:, :, None] * jnp.einsum(
            "jn,hpn->jhp", b_b.astype(jnp.float32), grad, precision=triple
        )
        d_mix = scale * jnp.einsum("ihp,jhp->hij", g_b, w_b, preferred_element_type=jnp.float32)
        d_sim = jnp.sum(d_mix * decay_b, axis=0)
        lead = scale * g_b.astype(jnp.float32) * jnp.exp(cum_b).T[:, :, None]
        d_c = jnp.dot(d_sim, b_b.astype(jnp.float32), precision=highest)
        d_c = d_c + jnp.einsum("ihp,hpn->in", lead, prior_b, precision=triple)
        d_b = jnp.dot(d_sim.T, c_b.astype(jnp.float32), precision=highest)
        d_b = d_b + jnp.einsum("jhp,hpn->jn", w_f * tail.T[:, :, None], grad, precision=triple)
        new_grad = jnp.exp(cum_b[:, -1])[:, None, None] * grad + jnp.einsum(
            "ihp,in->hpn", lead, c_b.astype(jnp.float32), precision=triple
        )
        return (new_grad, (d_w, d_b, d_c))

    start_grad, (d_weighted, d_bmat, d_cmat) = lax.scan(
        backward_block,
        zero_state,
        (block_cum, w_blocks, b_blocks, c_blocks, g_blocks, prior),
        reverse=True,
    )
    totals = jnp.sum(logarithm_decay, axis=1)
    zero_totals = jnp.zeros((heads,), jnp.float32)
    incoming = carried_in(
        (totals, final_state), "seq", join_pair, (zero_totals, zero_state), False
    )[1]
    outgoing = carried_in((totals, start_grad), "seq", join_pair, (zero_totals, zero_state), True)[
        1
    ]
    run_decay = jnp.cumsum(logarithm_decay, axis=1)
    lead_factor = jnp.exp(run_decay).T[:, :, None]
    tail_factor = jnp.exp(run_decay[:, -1:] - run_decay).T[:, :, None]
    b_f = b_mat.astype(jnp.float32)
    c_f = c_mat.astype(jnp.float32)
    grad_f = grad_rows.astype(jnp.float32).reshape(tokens, heads, head_dim)
    y_extra = lead_factor * jnp.einsum("tn,hpn->thp", c_f, incoming, precision=triple)
    skip_rep = jnp.repeat(skip_gain, head_dim)[None, :]
    y_sum = scale * (mixed.reshape(tokens, heads, head_dim) + y_extra)
    y_rows = (
        y_sum.reshape(tokens, heads * head_dim) + skip_rep * inner.astype(jnp.float32)
    ).astype(jnp.bfloat16)
    d_w_all = d_weighted.reshape(tokens, heads, head_dim) + tail_factor * jnp.einsum(
        "tn,hpn->thp", b_f, outgoing, precision=triple
    )
    w_tail = weighted.astype(jnp.float32) * tail_factor
    d_b_all = d_bmat.reshape(tokens, state_dim) + jnp.einsum(
        "thp,hpn->tn", w_tail, outgoing, precision=triple
    )
    d_c_all = d_cmat.reshape(tokens, state_dim) + jnp.einsum(
        "thp,hpn->tn", scale * grad_f * lead_factor, incoming, precision=triple
    )
    d_local = jnp.concatenate([d_b_all, d_c_all], axis=1)
    d_inner = (input_gain.T[:, :, None] * d_w_all).reshape(
        tokens, heads * head_dim
    ) + skip_rep * grad_rows.astype(jnp.float32)
    d_pre_x = d_inner * silu_grad(pre_x)
    share = 2 * state_dim // lax.axis_size("head")
    offset = lax.axis_index("head") * share
    d_local_t = d_local.T
    d_share = lax.psum_scatter(d_local_t, "head", scatter_dimension=0, tiled=True).T
    pre_part = lax.dynamic_slice_in_dim(pre_bc, offset, share, 1)
    taps_part = lax.dynamic_slice_in_dim(conv_bc, offset, share, 1)
    pad_part = lax.dynamic_slice_in_dim(bc_pad, offset, share, 1)
    d_pre_bc = d_share * silu_grad(pre_part)
    next_x, next_bc = shifted((d_pre_x[: taps - 1], d_pre_bc[: taps - 1]), "seq", -1)
    grad_x_rows = conv_backward(jnp.concatenate([d_pre_x, next_x], axis=0), conv_x, tokens).astype(
        jnp.bfloat16
    )
    grad_bc_part = conv_backward(
        jnp.concatenate([d_pre_bc, next_bc], axis=0), taps_part, tokens
    ).astype(jnp.bfloat16)
    taps_x = conv_weight_grad(d_pre_x, x_pad, taps)
    taps_bc_part = conv_weight_grad(d_pre_bc, pad_part, taps)
    grad_bc_rows = lax.all_gather(grad_bc_part, "head", axis=1, tiled=True)
    taps_bc = lax.all_gather(taps_bc_part, "head", axis=1, tiled=True)
    skip_term = jnp.sum(grad_f * inner_f, axis=(0, 2))
    sum_x, sum_bc, sum_skip = lax.psum((taps_x, taps_bc, skip_term), ("seq", "dp"))
    token_count = tokens * lax.axis_size("seq") * lax.axis_size("dp")
    norm_tokens = float(token_count) ** (-0.5)
    norm_skip = float(token_count * head_dim) ** (-0.5)
    return (
        y_rows[None],
        grad_x_rows[None],
        grad_bc_rows[None],
        sum_x * norm_tokens,
        sum_bc * norm_tokens,
        sum_skip * norm_skip,
    )


def solution(mesh):
    return jax.shard_map(
        local,
        mesh=mesh,
        in_specs=(
            P(("groups", "dp"), "seq", "head"),
            P(("groups", "dp"), "seq", None),
            P(("groups", "dp"), "head", "seq"),
            P(None, "head"),
            P(),
            P("head"),
            P(("groups", "dp"), "seq", "head"),
        ),
        out_specs=(
            P(("groups", "dp"), "seq", "head"),
            P(("groups", "dp"), "seq", "head"),
            P(("groups", "dp"), "seq", None),
            P("groups", "head"),
            P("groups", None),
            P(("groups", "head")),
        ),
        check_vma=False,
    )
```

profile of v0, /device:TPU:0, one launch (start us, length us, event | category | flops | bytes accessed | tf_op | source)
XLA Modules:
  0.0 329.8 jit_solution(5727681315043839589)
XLA Ops:
  7.9 4.9 %collective-permute-start.1 = (bf16[3,256]{1,0:T(4,128)(2,1)S(1)}, bf16[3,256]{1,0:T(4,128)(2,1)S(1)}, u32[]{:S(2)}, u32[]{:S(2)}) collective-permute-start(bf16[3,256]{1,0:T(4,128)(2,1)S(1)} %slice_bitcast_fusion.1), channel_id=1, source_target_pairs={{0,4},{4,8},{8,12},{1,5},{5,9},{9,13},{2,6},{6,10},{10,14},{3,7},{... | collective-permute-start | bytes 4616 | tf_op jit(solution)/shard_map/ppermute | solution.py:16
  19.8 3.5 %collective-permute-start = (bf16[3,2560]{1,0:T(4,128)(2,1)S(1)}, bf16[3,2560]{1,0:T(4,128)(2,1)S(1)}, u32[]{:S(2)}, u32[]{:S(2)}) collective-permute-start(bf16[3,2560]{1,0:T(4,128)(2,1)S(1)} %slice_bitcast_fusion), channel_id=1, source_target_pairs={{0,4},{4,8},{8,12},{1,5},{5,9},{9,13},{2,6},{6,10},{10,14},{3,7},{... | collective-permute-start | bytes 46088 | tf_op jit(solution)/shard_map/ppermute | solution.py:16
  24.9 10.1 %all-reduce = f32[160]{0:T(256)S(1)} all-reduce(f32[160]{0:T(256)S(1)} %dynamic-update-slice), channel_id=2, replica_groups=mesh['groups'=2,'seq'=4,'head'=2,'dp'=2] {'seq'}, use_global_device_ids=true, to_apply=%add | all-reduce | flops 160 | bytes 1280
  40.9 4.7 %fusion.1 = f32[40,256,64]{1,2,0:T(8,128)} fusion(bf16[256,40,64]{0,2,1:T(8,128)(2,1)S(1)} %bitcast.154, f32[256,256]{0,1:T(8,128)S(1)} %fusion.81, f32[40,256]{1,0:T(8,128)S(1)} %get-tuple-element.233, pred[256,256]{0,1:T(8,128)(4,1)S(1)} %iota_compare_fusion), kind=kOutput, calls=%fused_computation.8 | convolution fusion | flops 348651520 | bytes 4300800 | tf_op jit(solution)/shard_map/while/body/eval_jaxpr/hij,ihp->jhp/dot_general | solution.py:141
  45.6 72.7 %all-gather.8.cloned.1.call-done = f32[160,64,128]{2,1,0:T(8,128)} async-done(((f32[40,64,128]{2,1,0:T(8,128)}), f32[160,64,128]{2,1,0:T(8,128)}) %all-gather.8.cloned.1.call-update) | async-done | bytes 5242896 | tf_op jit(solution)/shard_map/all_gather | solution.py:23
  118.4 6.9 %while.17 = (s32[]{:T(128)}, f32[40,64,128]{2,1,0:T(8,128)S(1)}, s32[]{:T(128)}, f32[4,40]{1,0:T(4,128)}, f32[4,40,64,128]{3,2,1,0:T(8,128)}, /*index=5*/s32[]{:T(128)}, s32[]{:T(128)}, s32[]{:T(128)}, s32[]{:T(128)}) while((s32[]{:T(128)}, f32[40,64,128]{2,1,0:T(8,128)S(1)}, s32[]{:T(128)}, f32[4,40]{1,0:T(4,128)}, ...), condition=%wide.region_8.9_spmd, body=%wide.region_7.8_spmd.sunk | while | flops 655366 | bytes 3932787 | solution.py:32
  125.3 5.1 %fusion.29 = f32[256,40,64]{0,2,1:T(8,128)} fusion(f32[256,40,64]{0,2,1:T(8,128)} %fusion.53, f32[40,256,64]{1,2,0:T(8,128)} %fusion.1, f32[40,64,128]{2,1,0:T(8,128)S(1)} %get-tuple-element.192, f32[256,40]{0,1:T(8,128)S(1)} %get-tuple-element.237, f32[256,40]{0,1:T(8,128)S(1)} %get-tuple-element.240, f32[256,40]{0,1:T(8,128)S(1)} %get-tuple-element.242, ...), kind=kOutput, calls=%fused_computation.54 | convolution fusion | flops 507248640 | bytes 9363456 | tf_op jit(solution)/shard_map/tn,hpn->thp/dot_general | solution.py:183
  130.4 3.2 copy.103
  133.7 5.1 %fusion.10 = (f32[2560]{0:T(1024)S(1)}, f32[2560]{0:T(1024)S(1)}, f32[2560]{0:T(1024)S(1)}, f32[2560]{0:T(1024)S(1)}, f32[256,2560]{1,0:T(8,128)S(1)}) fusion(bf16[256,2560]{1,0:T(8,128)(2,1)S(1)} %bitcast.151, bf16[3,2560]{1,0:T(4,128)(2,1)S(1)} %collective-permute-done, bf16[1,256,2560]{2,1,0:T(8,128)(2,1)S(1)} %copy-done.1, ...), kind=kLoop, calls=%fused_computation.33 | loop fusion | flops 31447040 | bytes 9282560 | tf_op jit(solution)/shard_map/reduce_sum | solution.py:61
  140.1 4.6 %collective-permute-done.2 = f32[3,2560]{1,0:T(4,128)S(1)} collective-permute-done((f32[3,2560]{1,0:T(4,128)S(1)}, f32[3,2560]{1,0:T(4,128)S(1)}, u32[]{:S(2)}, u32[]{:S(2)}) %collective-permute-start.2) | collective-permute-done | bytes 30752 | tf_op jit(solution)/shard_map/ppermute | solution.py:16
  144.7 4.6 %fusion.18 = (f32[2560]{0:T(1024)S(1)}, f32[256,2560]{1,0:T(8,128)}, bf16[1,256,2560]{2,1,0:T(8,128)(2,1)}) fusion(bf16[1,256,2560]{2,1,0:T(8,128)(2,1)S(1)} %copy-done.6, bf16[256,2560]{1,0:T(8,128)(2,1)S(1)} %bitcast.152, f32[2560]{0:T(1024)S(1)} %get-tuple-element.203, bf16[3,2560]{1,0:T(4,128)(2,1)S(1)} %collective-permute-done, ...), kind=kLoop, calls=%fused_computation.41 | loop fusion | flops 26211840 | bytes 9272320 | tf_op jit(solution)/shard_map/reduce_sum | solution.py:217
  149.3 3.2 copy.92
  157.9 2.9 fusion.47
  165.5 3.8 %fusion.48 = f32[256,128]{1,0:T(8,128)S(1)} fusion(bf16[256,40,64]{0,2,1:T(8,128)(2,1)} %copy-done.4, f32[256,40]{0,1:T(8,128)S(1)} %get-tuple-element.240), kind=kOutput, calls=%fused_computation.81 | convolution fusion | flops 504627200 | bytes 1482752 | tf_op jit(solution)/shard_map/while/body/eval_jaxpr/jhp,hpn->jn/dot_general | solution.py:151
  171.5 4.5 %fusion = f32[256,256]{0,1:T(8,128)S(1)} fusion(f32[40,256]{1,0:T(8,128)S(1)} %get-tuple-element.233, pred[256,256]{0,1:T(8,128)(4,1)S(1)} %copy-done.13, bf16[256,40,64]{0,2,1:T(8,128)(2,1)S(1)} %copy-done.5, bf16[256,40,64]{0,2,1:T(8,128)(2,1)S(1)} %bitcast.156), kind=kOutput, calls=%fused_computation.5 | convolution fusion | flops 351207424 | bytes 2990080 | tf_op jit(solution)/shard_map/while/body/eval_jaxpr/ihp,jhp->hij/dot_general | solution.py:145
  176.3 77.7 %all-gather.6.cloned.1.call-done = f32[160,64,128]{2,1,0:T(8,128)} async-done(((f32[40,64,128]{2,1,0:T(8,128)}), f32[160,64,128]{2,1,0:T(8,128)}) %all-gather.6.cloned.1.call-update) | async-done | bytes 5242896 | tf_op jit(solution)/shard_map/all_gather | solution.py:23
  260.1 6.5 %fusion.31 = f32[256,40,64]{0,2,1:T(8,128)} fusion(f32[256,40,64]{0,2,1:T(8,128)} %fusion.74, f32[256,40,64]{0,2,1:T(8,128)} %fusion.55, bf16[256,40,64]{0,2,1:T(8,128)(2,1)} %copy-done.4, f32[256,256]{0,1:T(8,128)} %copy-done.8, f32[40,256]{1,0:T(8,128)S(1)} %get-tuple-element.233, pred[256,256]{0,1:T(8,128)(4,1)} %copy-done.12, ...), kind=kOutput, calls=%fused_computation.57 | convolution fusion | flops 351928320 | bytes 9625600 | tf_op jit(solution)/shard_map/while/body/eval_jaxpr/hij,jhp->ihp/dot_general | solution.py:116
  266.6 3.4 %copy.100 = f32[256,2560]{1,0:T(8,128)} copy(f32[256,2560]{0,1:T(8,128)} %bitcast.162) | data formatting | bytes 5242880 | tf_op jit(solution)/shard_map/reshape | solution.py:181
  270.1 3.3 %fusion.37 = bf16[1,256,2560]{2,1,0:T(8,128)(2,1)} fusion(f32[256,2560]{1,0:T(8,128)} %copy.100, f32[256,2560]{1,0:T(8,128)S(1)} %copy-done, f32[2560]{0:T(1024)S(1)} %mul.481), kind=kLoop, calls=%fused_computation.69 | loop fusion | flops 1966080 | bytes 6563840 | tf_op jit(solution)/shard_map/broadcast_in_dim | solution.py:223
  273.4 3.7 %reduce-scatter.2.cloned.1.call-done = f32[128,256]{0,1:T(8,128)} async-done(((f32[256,256]{0,1:T(8,128)}), f32[128,256]{0,1:T(8,128)}) %reduce-scatter.2.cloned.1.call-update) | async-done | bytes 131088 | tf_op jit(solution)/shard_map/reduce_scatter | solution.py:201
  278.1 4.3 %all_gather.33 = f32[4,256]{1,0:T(4,128)S(1)} all-gather(f32[4,128]{1,0:T(4,128)S(1)} %pad_maximum_fusion.4), channel_id=1, replica_groups=mesh['groups'=2,'seq'=4,'head'=2,'dp'=2] {'head'}, dimensions={1}, use_global_device_ids=true | all-gather | bytes 6144 | tf_op jit(solution)/shard_map/all_gather | solution.py:216
  282.5 28.4 %all-reduce.1 = (f32[4,2560]{1,0:T(4,128)S(1)}, f32[4,256]{1,0:T(4,128)S(1)}, f32[40]{0:T(128)S(1)}) all-reduce(f32[4,2560]{1,0:T(4,128)S(1)} %copy-done.9, f32[4,256]{1,0:T(4,128)S(1)} %all_gather.33, f32[40]{0:T(128)S(1)} %reduce_sum.119), channel_id=1, replica_groups=mesh['groups'=2,'seq'=4,'head'=2,'dp'=2] {'seq','dp'}, use_global_device_ids=true, to_apply=%region_15.16 | all-reduce | flops 11304 | bytes 90432 | tf_op jit(solution)/shard_map/psum | solution.py:218
  313.9 3.7 %collective-permute-done.3 = f32[3,128]{1,0:T(4,128)S(1)} collective-permute-done((f32[3,128]{1,0:T(4,128)S(1)}, f32[3,128]{1,0:T(4,128)S(1)}, u32[]{:S(2)}, u32[]{:S(2)}) %collective-permute-start.3) | collective-permute-done | bytes 1568 | tf_op jit(solution)/shard_map/ppermute | solution.py:16
  317.7 5.0 %all_gather.32 = bf16[256,256]{1,0:T(8,128)(2,1)S(1)} all-gather(bf16[256,128]{1,0:T(8,128)(2,1)S(1)} %fusion.62), channel_id=1, replica_groups=mesh['groups'=2,'seq'=4,'head'=2,'dp'=2] {'head'}, dimensions={1}, use_global_device_ids=true | all-gather | bytes 196608 | tf_op jit(solution)/shard_map/all_gather | solution.py:215
  (135 shorter events, 46.0 us)
Async XLA Ops:
  7.2 10.5 %copy-start.7 = (bf16[1,256,256]{2,1,0:T(8,128)(2,1)S(1)}, bf16[1,256,256]{2,1,0:T(8,128)(2,1)}, u32[]{:S(2)}) copy-start(bf16[1,256,256]{2,1,0:T(8,128)(2,1)} %param.12) | copy-start | bytes 393220
  7.2 111.1 %all-gather.8.cloned.1.call-start = ((), (), s32[]{:S(2)}) async-start(), calls=%async_computation.3 | async-start | bytes 6553600 | tf_op jit(solution)/shard_map/all_gather | solution.py:23
  7.9 9.7 %collective-permute-start.1 = (bf16[3,256]{1,0:T(4,128)(2,1)S(1)}, bf16[3,256]{1,0:T(4,128)(2,1)S(1)}, u32[]{:S(2)}, u32[]{:S(2)}) collective-permute-start(bf16[3,256]{1,0:T(4,128)(2,1)S(1)} %slice_bitcast_fusion.1), channel_id=1, source_target_pairs={{0,4},{4,8},{8,12},{1,5},{5,9},{9,13},{2,6},{6,10},{10,14},{3,7},{... | collective-permute-start | bytes 4616 | tf_op jit(solution)/shard_map/ppermute | solution.py:16
  15.9 3.8 %copy-start.16 = (f32[40]{0:T(128)}, f32[40]{0:T(128)S(1)}, u32[]{:S(2)}) copy-start(f32[40]{0:T(128)S(1)} %exponential_multiply_fusion) | copy-start | bytes 484
  17.5 23.4 %copy-start.2 = (bf16[1,256,2560]{1,2,0:T(8,128)(2,1)}, bf16[1,256,2560]{1,2,0:T(8,128)(2,1)S(1)}, u32[]{:S(2)}) copy-start(bf16[1,256,2560]{1,2,0:T(8,128)(2,1)S(1)} %copy.101) | copy-start | bytes 3932164
  17.6 5.8 %copy-start.23 = (u32[32]{0:T(128)S(1)}, u32[32]{0:T(128)}, u32[]{:S(2)}) copy-start(u32[32]{0:T(128)} %constant.137) | copy-start | bytes 388
  17.6 18.8 %copy-start.22 = (f32[40]{0:T(128)S(1)}, f32[40]{0:T(128)}, u32[]{:S(2)}) copy-start(f32[40]{0:T(128)} %param.16) | copy-start | bytes 484
  17.6 19.3 %copy-start.14 = (f32[4,2560]{1,0:T(4,128)S(1)}, f32[4,2560]{1,0:T(4,128)}, u32[]{:S(2)}) copy-start(f32[4,2560]{1,0:T(4,128)} %param.14) | copy-start | bytes 122884
  19.8 234.3 %all-gather.6.cloned.1.call-start = ((), (), s32[]{:S(2)}) async-start(), calls=%async_computation.2 | async-start | bytes 6553600 | tf_op jit(solution)/shard_map/all_gather | solution.py:23
  19.8 113.8 %collective-permute-start = (bf16[3,2560]{1,0:T(4,128)(2,1)S(1)}, bf16[3,2560]{1,0:T(4,128)(2,1)S(1)}, u32[]{:S(2)}, u32[]{:S(2)}) collective-permute-start(bf16[3,2560]{1,0:T(4,128)(2,1)S(1)} %slice_bitcast_fusion), channel_id=1, source_target_pairs={{0,4},{4,8},{8,12},{1,5},{5,9},{9,13},{2,6},{6,10},{10,14},{3,7},{... | collective-permute-start | bytes 46088 | tf_op jit(solution)/shard_map/ppermute | solution.py:16
  36.9 4.1 %copy-start.12 = (pred[256,256]{0,1:T(8,128)(4,1)}, pred[256,256]{0,1:T(8,128)(4,1)S(1)}, u32[]{:S(2)}) copy-start(pred[256,256]{0,1:T(8,128)(4,1)S(1)} %iota_compare_fusion) | copy-start | bytes 196612
  133.7 11.0 %copy-start.6 = (bf16[1,256,2560]{2,1,0:T(8,128)(2,1)S(1)}, bf16[1,256,2560]{2,1,0:T(8,128)(2,1)}, u32[]{:S(2)}) copy-start(bf16[1,256,2560]{2,1,0:T(8,128)(2,1)} %param.17) | copy-start | bytes 3932164
  138.8 5.9 %collective-permute-start.2 = (f32[3,2560]{1,0:T(4,128)S(1)}, f32[3,2560]{1,0:T(4,128)S(1)}, u32[]{:S(2)}, u32[]{:S(2)}) collective-permute-start(f32[3,2560]{1,0:T(4,128)S(1)} %slice.196), channel_id=1, source_target_pairs={{4,0},{8,4},{12,8},{5,1},{9,5},{13,9},{6,2},{10,6},{14,10},{7,3},{... | collective-permute-start | bytes 92168 | tf_op jit(solution)/shard_map/ppermute | solution.py:16
  157.6 119.4 %reduce-scatter.2.cloned.1.call-start = ((), (), s32[]{:S(2)}) async-start(), calls=%async_computation.1 | async-start | bytes 393216 | tf_op jit(solution)/shard_map/reduce_scatter | solution.py:201
  165.5 3.8 %copy-start.5 = (bf16[256,40,64]{0,2,1:T(8,128)(2,1)S(1)}, bf16[256,40,64]{0,2,1:T(8,128)(2,1)}, u32[]{:S(2)}) copy-start(bf16[256,40,64]{0,2,1:T(8,128)(2,1)} %copy-done.4) | copy-start | bytes 3932164
  165.5 6.0 %copy-start.13 = (pred[256,256]{0,1:T(8,128)(4,1)S(1)}, pred[256,256]{0,1:T(8,128)(4,1)}, u32[]{:S(2)}) copy-start(pred[256,256]{0,1:T(8,128)(4,1)} %copy-done.12) | copy-start | bytes 196612
  254.4 4.6 %copy-start.11 = (f32[256,128]{1,0:T(8,128)S(1)}, f32[256,128]{1,0:T(8,128)}, u32[]{:S(2)}) copy-start(f32[256,128]{1,0:T(8,128)} %fusion.47) | copy-start | bytes 393220
  266.6 3.4 %copy-start = (f32[256,2560]{1,0:T(8,128)S(1)}, f32[256,2560]{1,0:T(8,128)}, u32[]{:S(2)}) copy-start(f32[256,2560]{1,0:T(8,128)} %get-tuple-element.229) | copy-start | bytes 7864324
  270.0 12.5 %copy-start.9 = (f32[4,2560]{1,0:T(4,128)S(1)}, f32[4,2560]{1,0:T(4,128)}, u32[]{:S(2)}) copy-start(f32[4,2560]{1,0:T(4,128)} %pad_maximum_fusion.3) | copy-start | bytes 122884
  270.0 47.6 %copy-start.18 = (f32[128]{0:T(128)S(1)}, f32[128]{0:T(128)}, u32[]{:S(2)}) copy-start(f32[128]{0:T(128)} %get-tuple-element.248) | copy-start | bytes 1540
  270.0 47.6 %copy-start.19 = (f32[128]{0:T(128)S(1)}, f32[128]{0:T(128)}, u32[]{:S(2)}) copy-start(f32[128]{0:T(128)} %get-tuple-element.249) | copy-start | bytes 1540
  270.0 47.6 %copy-start.20 = (f32[128]{0:T(128)S(1)}, f32[128]{0:T(128)}, u32[]{:S(2)}) copy-start(f32[128]{0:T(128)} %get-tuple-element.250) | copy-start | bytes 1540
  270.1 47.6 %copy-start.21 = (f32[128]{0:T(128)S(1)}, f32[128]{0:T(128)}, u32[]{:S(2)}) copy-start(f32[128]{0:T(128)} %get-tuple-element.251) | copy-start | bytes 1540
  312.1 5.5 %collective-permute-start.3 = (f32[3,128]{1,0:T(4,128)S(1)}, f32[3,128]{1,0:T(4,128)S(1)}, u32[]{:S(2)}, u32[]{:S(2)}) collective-permute-start(f32[3,128]{1,0:T(4,128)S(1)} %slice.201), channel_id=1, source_target_pairs={{4,0},{8,4},{12,8},{5,1},{9,5},{13,9},{6,2},{10,6},{14,10},{7,3},{... | collective-permute-start | bytes 4616 | tf_op jit(solution)/shard_map/ppermute | solution.py:16
  (7 other events, 15.7 us)
Sparse Core Ops, SparseCore 0:
  19.9 98.3 all-gather.7
  157.8 96.1 all-gather.5
  260.3 16.7 reduce-scatter.1
where the time goes:
time: 331 us; the launch traced here: 330 us
  waiting for transfers between devices  162 us (49%)
  blocking collectives  47.8 us (14%)
  matrix products  43.6 us (13%)
  other arithmetic  28.8 us (9%)
  local copies, waits for them, and re-layouts  20.7 us (6%)
  between operations  15 us (5%)
  starting transfers between devices  11.3 us (3%)
    all_gather x2, waiting for transfers between devices, carried_in(): gathered = jax.tree.map(lambda a: lax.all_gather(a, axis), part)  150 us
    psum x1, blocking collectives, local(): lax.psum((taps_x, taps_bc, skip_term), ('seq', 'dp'))  28.4 us
    ppermute x4, starting transfers between devices, shifted(): return lax.ppermute(block, axis, route)  11 us
    unnamed x1, blocking collectives  10.1 us
    ppermute x4, waiting for transfers between devices, shifted(): return lax.ppermute(block, axis, route)  8.27 us
  transfers between devices with their start and end apart: 7, of which 5 were waited for; matrix products, arithmetic and copies ran while one was open for 19% of the time, Pallas kernels for 0%

commit v1 on v0

v1 whole, which is shorter than its diff:
```python
import functools

import jax
import jax.numpy as jnp
from jax import lax
from jax.experimental import pallas as pl
from jax.experimental.pallas import tpu as pltpu
from jax.sharding import PartitionSpec as P

BLOCK_LEN = 256
LANES = 128
HALO = 8
NEG = -1e30
f32 = jnp.float32
bf16 = jnp.bfloat16
HIGHEST = lax.Precision.HIGHEST
VMEM_LIMIT = 48 * 1024 * 1024


def dot(a, b, precision=None):
    return jnp.dot(a, b, preferred_element_type=f32, precision=precision)


def dot_nt(a, b):
    return lax.dot_general(a, b, (((1,), (1,)), ((), ())), preferred_element_type=f32)


def sigmoid(v):
    return 0.5 * jnp.tanh(0.5 * v) + 0.5


def conv_rows(pad_ref, taps, lanes, rows, first):
    total = None
    for k in range(len(taps)):
        term = taps[k] * pad_ref[first + k : first + k + rows, lanes]
        total = term if total is None else total + term
    return total


def tap_rows(ref, lanes, count):
    block = ref[:, lanes]
    return [block[k : k + 1] for k in range(count)]


def spread(row_a, row_b):
    half, rows = LANES // 2, row_a.shape[1]
    both = jnp.concatenate(
        [jnp.broadcast_to(row_a, (half, rows)), jnp.broadcast_to(row_b, (half, rows))], axis=0
    )
    return both.T


def column(row):
    return jnp.broadcast_to(row, (LANES, row.shape[1])).T


def running_sum(dec):
    rows = dec.shape[1]
    before = lax.broadcasted_iota(jnp.int32, (rows, rows), 0)
    after = lax.broadcasted_iota(jnp.int32, (rows, rows), 1)
    upper = (before <= after).astype(f32)
    return dot(jnp.log(dec), upper, HIGHEST)


def gain_of(dec):
    return jnp.sqrt((1.0 - dec) * (1.0 + dec))


def tail_of(cum):
    return jnp.exp(cum[:, -1:] - cum)


def mapped_of(bc_ref, bch_ref, wbc_ref, bcpad, rows):
    bcpad[0:HALO, :] = bch_ref[...].astype(f32)
    bcpad[HALO : HALO + rows, :] = bc_ref[...].astype(f32)
    taps = wbc_ref.shape[0]
    weights = [wbc_ref[k : k + 1, :] for k in range(taps)]
    return conv_rows(bcpad, weights, slice(None), rows, HALO - taps + 1)


def state_kernel(first, heads_before, head_dim, scale, *refs):
    if first:
        dec_ref, x_ref, g_ref, xh_ref, wx_ref, bc_ref, bch_ref, wbc_ref = refs[:8]
        u_ref, v_ref, tot_ref, lw_ref, lg_ref, cum_ref, map_ref = refs[8:15]
        xpad, bt, ct, gt, sl, bcpad = refs[15:]
    else:
        dec_ref, x_ref, g_ref, xh_ref, wx_ref, cum_ref, map_ref = refs[:7]
        u_ref, v_ref, tot_ref, lw_ref, lg_ref = refs[7:12]
        xpad, bt, ct, gt, sl = refs[12:]
    rows, width = x_ref.shape
    taps = wx_ref.shape[0]
    state = bt.shape[0]

    @pl.when(pl.program_id(0) == 0)
    def _():
        dec = dec_ref[...]
        if first:
            cum = running_sum(dec)
            cum_ref[...] = cum
            pre = mapped_of(bc_ref, bch_ref, wbc_ref, bcpad, rows)
            mapped_f = pre * sigmoid(pre)
            map_ref[...] = mapped_f.astype(bf16)
        else:
            cum = cum_ref[...]
            mapped_f = map_ref[...].astype(f32)
        bt[...] = mapped_f[:, :state].T.astype(bf16)
        ct[...] = mapped_f[:, state:].T.astype(bf16)
        gt[...] = gain_of(dec) * tail_of(cum)
        sl[...] = scale * jnp.exp(cum)

    xpad[0:HALO, :] = xh_ref[...].astype(f32)
    xpad[HALO : HALO + rows, :] = x_ref[...].astype(f32)
    head0 = heads_before + pl.program_id(0) * (width // head_dim)
    for q in range(width // LANES):
        lanes = slice(q * LANES, (q + 1) * LANES)
        h = head0 + 2 * q
        pre = conv_rows(xpad, tap_rows(wx_ref, lanes, taps), lanes, rows, HALO - taps + 1)
        inner = (pre * sigmoid(pre)).astype(bf16).astype(f32)
        factor = spread(gt[pl.ds(h, 1), :], gt[pl.ds(h + 1, 1), :])
        lw_ref[:, lanes] = (inner * factor).astype(bf16)
        lead = spread(sl[pl.ds(h, 1), :], sl[pl.ds(h + 1, 1), :])
        lg_ref[:, lanes] = (g_ref[:, lanes].astype(f32) * lead).astype(bf16)
        tot_ref[:, lanes] = jnp.broadcast_to(lead[rows - 1 :, :] * (1.0 / scale), (8, LANES))
    u_ref[...] = dot(bt[...], lw_ref[...])
    v_ref[...] = dot(ct[...], lg_ref[...])


def intra_kernel(first, last, heads_before, head_dim, scale, *refs):
    x_ref, g_ref, xh_ref, wx_ref, dec_ref, cum_ref, map_ref, skip_ref = refs[:8]
    refs = refs[8:]
    if not first:
        dsim_in, gs_in = refs[:2]
        refs = refs[2:]
    y0_ref, dx_ref, q_ref, ls_ref, dsim_ref, gs_ref = refs[:6]
    refs = refs[6:]
    if last:
        dbc_ref = refs[0]
        refs = refs[1:]
    xpad, sim, gain, tail, sl = refs
    rows, width = x_ref.shape
    taps = wx_ref.shape[0]
    state = map_ref.shape[1] // 2
    half = rows // 2
    dec = dec_ref[...]
    gain[...] = gain_of(dec)
    tail[...] = tail_of(cum_ref[...])
    sl[...] = scale * jnp.exp(cum_ref[...])
    xpad[0:HALO, :] = xh_ref[...].astype(f32)
    xpad[HALO : HALO + rows, :] = x_ref[...].astype(f32)
    sim[...] = dot_nt(map_ref[:, state:], map_ref[:, :state])
    if first:
        dsim_ref[...] = jnp.zeros(dsim_ref.shape, f32)
        gs_ref[...] = jnp.zeros(gs_ref.shape, f32)
    else:
        dsim_ref[...] = dsim_in[...]
        gs_ref[...] = gs_in[...]
    lane = lax.broadcasted_iota(jnp.int32, (1, LANES), 1)
    low = lane < head_dim
    r_i = lax.broadcasted_iota(jnp.int32, (half, half), 0)
    c_i = lax.broadcasted_iota(jnp.int32, (half, half), 1)
    lower = r_i >= c_i

    def pair(q, carry):
        lanes = pl.ds(pl.multiple_of(q * LANES, LANES), LANES)
        h = heads_before + 2 * q
        pre = conv_rows(xpad, tap_rows(wx_ref, lanes, taps), lanes, rows, HALO - taps + 1)
        sg = sigmoid(pre)
        inner = (pre * sg).astype(bf16).astype(f32)
        sgrad = sg * (1.0 + pre * (1.0 - sg))
        gn = spread(gain[pl.ds(h, 1), :], gain[pl.ds(h + 1, 1), :])
        tl = spread(tail[pl.ds(h, 1), :], tail[pl.ds(h + 1, 1), :])
        ls = spread(sl[pl.ds(h, 1), :], sl[pl.ds(h + 1, 1), :])
        w = (inner * gn).astype(bf16)
        g = g_ref[:, lanes]
        gf = g.astype(f32)
        g_t = gf.T.astype(bf16)
        y = None
        dw_t = []
        for a in range(2):
            row = cum_ref[pl.ds(h + a, 1), :]
            col = column(row)
            keep = low if a == 0 else jnp.logical_not(low)
            d00 = jnp.exp(jnp.where(lower, col[:half] - row[:, :half], NEG))
            d10 = jnp.exp(col[half:] - row[:, :half])
            d11 = jnp.exp(jnp.where(lower, col[half:] - row[:, half:], NEG))
            m00 = (d00 * sim[0:half, 0:half]).astype(bf16)
            m10 = (d10 * sim[half:rows, 0:half]).astype(bf16)
            m11 = (d11 * sim[half:rows, half:rows]).astype(bf16)
            w_a = jnp.where(keep, w, jnp.zeros_like(w))
            top = dot(m00, w_a[:half])
            bot = dot(jnp.concatenate([m10, m11], axis=1), w_a)
            y_a = jnp.concatenate([top, bot], axis=0)
            y = y_a if y is None else y + y_a
            g_at = g_t[a * head_dim : (a + 1) * head_dim]
            left = dot(g_at, jnp.concatenate([m00, m10], axis=0))
            right = dot(g_at[:, half:], m11)
            dw_t.append(jnp.concatenate([left, right], axis=1))
            mix_top = dot_nt(g[:half], w_a[:half])
            mix_bot = dot_nt(g[half:], w_a)
            dsim_ref[0:half, 0:half] += d00 * mix_top
            dsim_ref[half:rows, 0:half] += d10 * mix_bot[:, :half]
            dsim_ref[half:rows, half:rows] += d11 * mix_bot[:, half:]
        dw = scale * jnp.concatenate(dw_t, axis=0).T
        skip = jnp.where(low, skip_ref[h], skip_ref[h + 1])
        y0_ref[:, lanes] = scale * y + skip * inner
        dx_ref[:, lanes] = (gn * dw + skip * gf) * sgrad
        q_ref[:, lanes] = (gn * tl * sgrad).astype(bf16)
        ls_ref[:, lanes] = ls.astype(bf16)
        gi = jnp.sum(gf * inner, axis=0, keepdims=True)
        sum_a = jnp.sum(jnp.where(low, gi, 0.0), axis=1, keepdims=True)
        sum_b = jnp.sum(jnp.where(low, 0.0, gi), axis=1, keepdims=True)
        gs_ref[...] += jnp.where(lane == h, sum_a, 0.0) + jnp.where(lane == h + 1, sum_b, 0.0)
        return carry

    lax.fori_loop(0, width // LANES, pair, 0)
    if last:
        ds = scale * dsim_ref[...]
        high = ds.astype(bf16)
        rest = (ds - high.astype(f32)).astype(bf16)
        ds_t = ds.T
        high_t = ds_t.astype(bf16)
        rest_t = (ds_t - high_t.astype(f32)).astype(bf16)
        b, c = map_ref[:, :state], map_ref[:, state:]
        dbc_ref[:, :state] = dot(high_t, c) + dot(rest_t, c)
        dbc_ref[:, state:] = dot(high, b) + dot(rest, b)


def pick(place, parts, wanted):
    total = jnp.zeros(parts[0].shape, bf16)
    for hop, ref in enumerate(parts):
        total = jnp.where(place == wanted(hop), ref[...], total)
    return total


def edge_kernel(count, hops, *refs):
    place_ref, dx_ref, q_ref, map_ref = refs[:4]
    parts, out_ref = refs[4 : 4 + hops], refs[4 + hops]
    state = map_ref.shape[1] // 2
    if hops:
        grad = pick(place_ref[0], parts, lambda hop: count - 2 - hop)
        extra = dot(map_ref[:, :state], grad)
        out_ref[...] = (dx_ref[...] + q_ref[...].astype(f32) * extra).astype(bf16)
    else:
        out_ref[...] = dx_ref[...].astype(bf16)


def finish_kernel(count, chunk, chunks, *refs):
    last = chunk == chunks - 1
    hops = count - 1
    place_ref, y0_ref, dx_ref, q_ref, ls_ref, x_ref, wx_ref = refs[:7]
    lw_ref, lg_ref, map_ref, edge_ref, dbc_in = refs[7:12]
    refs = refs[12:]
    parts, refs = refs[:hops], refs[hops:]
    if chunk:
        refs = refs[2:]
    if last:
        bc_ref, bch_ref, wbc_ref, gs_ref = refs[:4]
        before, refs = refs[4 : 4 + chunks - 1], refs[4 + chunks - 1 :]
        y_ref, gx_ref, sums_ref, head_ref, own_ref, dpad, dbc_ref, taps_ref, bcpad = refs
    else:
        y_ref, gx_ref, taps_ref, dbc_ref, dpad = refs
    rows, width = x_ref.shape
    taps = wx_ref.shape[0]
    state = map_ref.shape[1] // 2
    step = pl.program_id(0)

    @pl.when(step == 0)
    def _():
        dbc_ref[...] = dbc_in[...]

    place = place_ref[0]
    enter = pick(place, parts, lambda hop: hop + 1)
    grad = pick(place, parts, lambda hop: count - 2 - hop)
    b, c = map_ref[:, :state], map_ref[:, state:]
    y_ref[...] = (y0_ref[...] + ls_ref[...].astype(f32) * dot(c, enter)).astype(bf16)
    dpad[0:rows, :] = dx_ref[...] + q_ref[...].astype(f32) * dot(b, grad)
    dpad[rows : rows + HALO, :] = edge_ref[...].astype(f32)[0:HALO]
    dbc_ref[:, :state] += dot_nt(lw_ref[...], grad)
    dbc_ref[:, state:] += dot_nt(lg_ref[...], enter)
    for q in range(width // LANES):
        lanes = slice(q * LANES, (q + 1) * LANES)
        weights = tap_rows(wx_ref, lanes, taps)
        x = x_ref[:, lanes].astype(f32)
        total = None
        sums = []
        for k in range(taps):
            shifted = dpad[taps - 1 - k : taps - 1 - k + rows, lanes]
            term = weights[k] * shifted
            total = term if total is None else total + term
            sums.append(jnp.sum(shifted * x, axis=0, keepdims=True))
        gx_ref[:, lanes] = total.astype(bf16)
        sums = jnp.concatenate(sums + [jnp.zeros((8 - taps, LANES), f32)], axis=0)
        if last:
            at = pl.multiple_of(step * width + q * LANES, LANES)
            taps_ref[:, pl.ds(at, LANES)] = sums
        else:
            taps_ref[:, lanes] = sums

    if last:

        @pl.when(step == pl.num_programs(0) - 1)
        def _():
            pre = mapped_of(bc_ref, bch_ref, wbc_ref, bcpad, rows)
            sg = sigmoid(pre)
            dpre = dbc_ref[...] * (sg * (1.0 + pre * (1.0 - sg)))
            own_ref[...] = dpre
            at = 0
            for ref in before:
                sums_ref[:, at : at + ref.shape[1]] = ref[...]
                at += ref.shape[1]
            sums_ref[:, at : at + taps_ref.shape[1]] = taps_ref[...]
            at += taps_ref.shape[1]
            sums = []
            for k in range(taps):
                moved = bcpad[HALO - taps + 1 + k : HALO - taps + 1 + k + rows, :]
                sums.append(jnp.sum(dpre * moved, axis=0, keepdims=True))
            sums = jnp.concatenate(sums + [jnp.zeros((8 - taps, 2 * state), f32)], axis=0)
            sums_ref[:, at : at + 2 * state] = sums
            sums_ref[:, at + 2 * state :] = gs_ref[...]
            head_ref[0:rows, :] = dpre.astype(bf16)
            head_ref[rows:, :] = jnp.concatenate([sums, jnp.zeros_like(sums)], axis=0).astype(bf16)


def merge_kernel(heads, *refs):
    sums_ref, sums_dp, own_ref = refs[:3]
    others, crosses = refs[3 : 2 + heads], refs[2 + heads : 1 + 2 * heads]
    sums_out, full_ref, send_ref = refs[1 + 2 * heads :]
    rows, bc = own_ref.shape
    inner = sums_ref.shape[1] - bc - LANES
    full = own_ref[...]
    total = sums_ref[...] + sums_dp[...]
    taps_bc = total[:, inner : inner + bc]
    for ref in others:
        block = ref[...].astype(f32)
        full = full + block[:rows]
        taps_bc = taps_bc + block[rows : rows + 8]
    for ref in crosses:
        taps_bc = taps_bc + ref[...]
    full_ref[...] = full
    sums_out[:, 0:inner] = total[:, :inner]
    sums_out[:, inner : inner + bc] = taps_bc
    sums_out[:, inner + bc :] = total[:, inner + bc :]
    send_ref[0:8, :] = sums_out[...].astype(bf16)
    send_ref[8:16, :] = jnp.zeros((8, send_ref.shape[1]), bf16)
    send_ref[8:16, inner : inner + bc] = full[0:8].astype(bf16)


def last_kernel(count, norm_tokens, norm_skip, *refs):
    place_ref, sums_ref, full_ref, wbc_ref = refs[:4]
    parts = refs[4 : 3 + count]
    gbc_ref, tx_ref, tbc_ref, skip_ref, dpad = refs[3 + count :]
    taps, bc = wbc_ref.shape
    rows = full_ref.shape[0]
    inner = sums_ref.shape[1] - bc - LANES
    total = sums_ref[...]
    edge = jnp.zeros((8, bc), f32)
    for hop, ref in enumerate(parts):
        block = ref[...].astype(f32)
        total = total + block[0:8]
        if hop == count - 2:
            edge = jnp.where(place_ref[0] < count - 1, block[8:16, inner : inner + bc], 0.0)
    tx_ref[...] = total[0:taps, 0:inner] * norm_tokens
    tbc_ref[...] = total[0:taps, inner : inner + bc] * norm_tokens
    skip_ref[...] = total[0:1, inner + bc :] * norm_skip
    dpad[0:rows, :] = full_ref[...]
    dpad[rows : rows + 8, :] = edge
    out = None
    for k in range(taps):
        term = wbc_ref[k : k + 1, :] * dpad[taps - 1 - k : taps - 1 - k + rows, :]
        out = term if out is None else out + term
    gbc_ref[...] = out.astype(bf16)


def call(kernel, grid, ins, outs, scratch, name, flops=0, nbytes=0, kept=()):
    def spec(item):
        array, block, index = item
        if block == "smem":
            return pl.BlockSpec(memory_space=pltpu.SMEM)
        if block == "any":
            return pl.BlockSpec(memory_space=pl.ANY)
        if block is None:
            whole = array.shape
            return pl.BlockSpec(whole, lambda *_: (0,) * len(whole))
        return pl.BlockSpec(block, index)

    return pl.pallas_call(
        kernel,
        grid=grid,
        in_specs=[spec(i) for i in ins],
        out_specs=[spec(o) for o in outs],
        out_shape=[o[0] for o in outs],
        scratch_shapes=scratch,
        compiler_params=pltpu.CompilerParams(vmem_limit_bytes=VMEM_LIMIT),
        cost_estimate=pl.CostEstimate(flops=flops, bytes_accessed=nbytes, transcendentals=0),
        input_output_aliases=dict(kept),
        name=name,
    )(*[i[0] for i in ins])


def chain_routes(count, hop):
    return [(hop, hop + 1), (count - 1 - hop, count - 2 - hop)]


def local(x_input, bc_input, decays, conv_x, conv_bc, skip_gain, grad_out):
    x, bc, dec, g = x_input[0], bc_input[0], decays[0], grad_out[0]
    rows, inner = x.shape
    taps = conv_x.shape[0]
    heads = dec.shape[0]
    head_dim = inner // heads
    bcw = bc.shape[1]
    state = bcw // 2
    scale = state ** (-0.5)
    count = lax.axis_size("seq")
    head_count = lax.axis_size("head")
    dp_count = lax.axis_size("dp")
    assert rows == BLOCK_LEN and 2 * head_dim == LANES and count % 2 == 0 and dp_count == 2
    chunks = 2
    width = inner // chunks
    block = 640 if width % 640 == 0 else LANES
    per = width // block
    place = lax.axis_index("seq")
    place1 = place.astype(jnp.int32).reshape(1)
    chunk_heads = width // head_dim

    def shape(s, d=f32):
        return jax.ShapeDtypeStruct(s, d)

    tails = jnp.concatenate([x[rows - HALO :], bc[rows - HALO :]], axis=1)
    halo = lax.ppermute(tails, "seq", [(i, i + 1) for i in range(count - 1)])
    bc_halo = (halo, (HALO, bcw), lambda *_: (0, inner // bcw))

    states = []
    cum = mapped = None
    for c in range(chunks):
        first = c == 0

        def at(i, c=c):
            return (0, c * per + i)

        ins = [
            (dec, None, None),
            (x, (rows, block), at),
            (g, (rows, block), at),
            (halo, (HALO, block), at),
            (conv_x, (taps, block), at),
        ]
        outs = [
            (shape((state, width)), (state, block), lambda i: (0, i)),
            (shape((state, width)), (state, block), lambda i: (0, i)),
            (shape((8, width)), (8, block), lambda i: (0, i)),
            (shape((rows, width), bf16), (rows, block), lambda i: (0, i)),
            (shape((rows, width), bf16), (rows, block), lambda i: (0, i)),
        ]
        scratch = [
            pltpu.VMEM((rows + HALO, block), f32),
            pltpu.VMEM((state, rows), bf16),
            pltpu.VMEM((state, rows), bf16),
            pltpu.VMEM((heads, rows), f32),
            pltpu.VMEM((heads, rows), f32),
        ]
        if first:
            ins += [(bc, None, None), bc_halo, (conv_bc, None, None)]
            outs += [
                (shape((heads, rows)), None, None),
                (shape((rows, bcw), bf16), None, None),
            ]
            scratch += [pltpu.VMEM((rows + HALO, bcw), f32)]
        else:
            ins += [(cum, None, None), (mapped, None, None)]
        made = call(
            functools.partial(state_kernel, first, c * chunk_heads, head_dim, scale),
            (per,),
            ins,
            outs,
            scratch,
            "local_state",
        )
        if first:
            cum, mapped = made[5:]
        states.append(made[:5])

    received = [[] for _ in range(chunks)]

    def send(c, hop):
        u, v, tot = states[c][:3]
        own = jnp.where(place == hop, u, v)
        if hop:
            own = own + tot[0:1] * received[c][hop - 1].astype(f32)
        received[c].append(lax.ppermute(own.astype(bf16), "seq", chain_routes(count, hop)))

    intra = []
    dsim = gsum = None

    def inside(c):
        first, last = c == 0, c == chunks - 1

        def at(i):
            return (0, c)

        ins = [
            (x, (rows, width), at),
            (g, (rows, width), at),
            (halo, (HALO, width), at),
            (conv_x, (taps, width), at),
            (dec, None, None),
            (cum, None, None),
            (mapped, None, None),
            (skip_gain, "smem", None),
        ]
        if not first:
            ins += [(dsim, None, None), (gsum, None, None)]
        outs = [
            (shape((rows, width)), None, None),
            (shape((rows, width)), None, None),
            (shape((rows, width), bf16), None, None),
            (shape((rows, width), bf16), None, None),
            (shape((rows, rows)), None, None),
            (shape((8, LANES)), None, None),
        ]
        if last:
            outs += [(shape((rows, bcw)), None, None)]
        scratch = [
            pltpu.VMEM((rows + HALO, width), f32),
            pltpu.VMEM((rows, rows), f32),
            pltpu.VMEM((heads, rows), f32),
            pltpu.VMEM((heads, rows), f32),
            pltpu.VMEM((heads, rows), f32),
        ]
        return call(
            functools.partial(intra_kernel, first, last, c * chunk_heads, head_dim, scale),
            (1,),
            ins,
            outs,
            scratch,
            "inside_block",
        )

    edges = []

    def edge(c):
        y0, dx, q, ls = intra[c][:4]
        hops = count - 2
        made = call(
            functools.partial(edge_kernel, count, hops),
            (1,),
            [
                (place1, "smem", None),
                (dx, (16, width), lambda i: (0, 0)),
                (q, (16, width), lambda i: (0, 0)),
                (mapped, (16, bcw), lambda i: (0, 0)),
            ]
            + [(r, None, None) for r in received[c][:hops]],
            [(shape((16, width), bf16), None, None)],
            [],
            "first_rows",
        )[0]
        return lax.ppermute(made, "seq", [(i + 1, i) for i in range(count - 1)])

    for hop in range(count - 1):
        for c in range(chunks):
            send(c, hop)
    for c in range(chunks):
        made = inside(c)
        intra.append(made)
        dsim, gsum = made[4:6]
    dbc = intra[-1][6]
    for c in range(chunks):
        edges.append(edge(c))

    y = gx = None
    taps_parts = []
    for c in range(chunks):
        last = c == chunks - 1
        u, v, tot, lw, lg = states[c]
        y0, dx, q, ls = intra[c][:4]

        def mine(i):
            return (0, i)

        def at(i, c=c):
            return (0, c * per + i)

        ins = [
            (place1, "smem", None),
            (y0, (rows, block), mine),
            (dx, (rows, block), mine),
            (q, (rows, block), mine),
            (ls, (rows, block), mine),
            (x, (rows, block), at),
            (conv_x, (taps, block), at),
            (lw, (rows, block), mine),
            (lg, (rows, block), mine),
            (mapped, None, None),
            (edges[c], (16, block), mine),
            (dbc, None, None),
        ]
        ins += [(r, (state, block), mine) for r in received[c]]
        outs = [
            (shape((rows, inner), bf16), (rows, block), at),
            (shape((rows, inner), bf16), (rows, block), at),
        ]
        scratch = [pltpu.VMEM((rows + HALO, block), f32)]
        kept = ()
        if c:
            kept = ((len(ins), 0), (len(ins) + 1, 1))
            ins += [(y, "any", None), (gx, "any", None)]
        if last:
            ins += [(bc, None, None), bc_halo, (conv_bc, None, None), (gsum, None, None)]
            ins += [(t, None, None) for t in taps_parts]
            outs += [
                (shape((8, inner + bcw + LANES)), None, None),
                (shape((rows + 16, bcw), bf16), None, None),
                (shape((rows, bcw)), None, None),
            ]
            scratch += [
                pltpu.VMEM((rows, bcw), f32),
                pltpu.VMEM((8, width), f32),
                pltpu.VMEM((rows + HALO, bcw), f32),
            ]
        else:
            outs += [
                (shape((8, width)), (8, block), mine),
                (shape((rows, bcw)), None, None),
            ]
        made = call(
            functools.partial(finish_kernel, count, c, chunks),
            (per,),
            ins,
            outs,
            scratch,
            "finish",
            kept=kept,
        )
        y, gx = made[:2]
        if last:
            sums, to_heads, own = made[2:]
        else:
            taps_parts.append(made[2])
            dbc = made[3]

    cross = sums[:, inner : inner + bcw]
    swap = [(0, 1), (1, 0)]
    sums_dp = lax.ppermute(sums, "dp", swap)
    others, crosses = [], []
    for k in range(1, head_count):
        turn = [(i, (i + k) % head_count) for i in range(head_count)]
        others.append(lax.ppermute(to_heads, "head", turn))
        both = [(2 * i + j, 2 * t + 1 - j) for i, t in turn for j in range(2)]
        crosses.append(lax.ppermute(cross, ("head", "dp"), both))
    sums_all, full, to_seq = call(
        functools.partial(merge_kernel, head_count),
        (1,),
        [(a, None, None) for a in [sums, sums_dp, own] + others + crosses],
        [
            (shape(sums.shape), None, None),
            (shape((rows, bcw)), None, None),
            (shape((16, sums.shape[1]), bf16), None, None),
        ],
        [],
        "merge",
    )
    from_seq = [
        lax.ppermute(to_seq, "seq", [(i, (i + k) % count) for i in range(count)])
        for k in range(1, count)
    ]
    token_count = rows * count * dp_count
    norm_tokens = float(token_count) ** (-0.5)
    norm_skip = float(token_count * head_dim) ** (-0.5)
    gbc, tx, tbc, skip = call(
        functools.partial(last_kernel, count, norm_tokens, norm_skip),
        (1,),
        [(place1, "smem", None)] + [(a, None, None) for a in [sums_all, full, conv_bc] + from_seq],
        [
            (shape((rows, bcw), bf16), None, None),
            (shape((taps, inner)), None, None),
            (shape((taps, bcw)), None, None),
            (shape((1, LANES)), None, None),
        ],
        [pltpu.VMEM((rows + 8, bcw), f32)],
        "last",
    )
    return y[None], gx[None], gbc[None], tx, tbc, skip[0, :heads]


def solution(mesh):
    return jax.shard_map(
        local,
        mesh=mesh,
        in_specs=(
            P(("groups", "dp"), "seq", "head"),
            P(("groups", "dp"), "seq", None),
            P(("groups", "dp"), "head", "seq"),
            P(None, "head"),
            P(),
            P("head"),
            P(("groups", "dp"), "seq", "head"),
        ),
        out_specs=(
            P(("groups", "dp"), "seq", "head"),
            P(("groups", "dp"), "seq", "head"),
            P(("groups", "dp"), "seq", None),
            P("groups", "head"),
            P("groups", None),
            P(("groups", "head")),
        ),
        check_vma=False,
    )
```

time: 331 us -> 100 us (0.30)
  waiting for transfers between devices: 162 us -> 30.5 us
  blocking collectives: 47.8 us -> 0 us
  matrix products: 43.6 us -> 0 us
  Pallas kernels: 0 us -> 31.7 us
  other arithmetic: 28.8 us -> 0.55 us
  starting transfers between devices: 11.3 us -> 26.1 us
  between operations: 15 us -> 0.85 us
  local copies, waits for them, and re-layouts: 20.7 us -> 9.61 us
    all_gather x2 -> x0, waiting for transfers between devices: 150 us -> none  [carried_in(): gathered = jax.tree.map(lambda a: lax.all_gather(a, axis), part)]
    dot_general x16 -> x0, matrix products: 43.6 us -> none  [the longest x1 6.48 us: forward_block(): jnp.einsum('hij,jhp->ihp', mixing, w_b, preferred_element_type=jnp.float32)]
    pallas_call x0 -> x10, Pallas kernels: none -> 31.7 us  [call(): pl.pallas_call(kernel, grid=grid, in_specs=[spec(i) for i in ins], out_sp...]
    psum x1 -> x0, blocking collectives: 28.4 us -> none  [local(): lax.psum((taps_x, taps_bc, skip_term), ('seq', 'dp'))]
    ppermute x4 -> x15, waiting for transfers between devices: 8.27 us -> 30.5 us  [the longest x2 9.58 us: edge(): return lax.ppermute(made, 'seq', [(i + 1, i) for i in range(count - 1)])]
    ppermute x4 -> x15, starting transfers between devices: 11 us -> 26.1 us  [the longest x6 9.65 us: send(): lax.ppermute(own.astype(bf16), 'seq', chain_routes(count, hop))]
    reduce_sum x4 -> x0, other arithmetic: 10.9 us -> none  [the longest x2 6.15 us: conv_weight_grad(): jnp.sum(pregrad * padded[shift:shift + length].astype(jnp.float32), axis=0)]
    unnamed x1 -> x0, blocking collectives: 10.1 us -> none
  transfers between devices with their start and end apart: 7 -> 15, of which waited for: 5 -> 9; matrix products, arithmetic and copies ran while one was open for 19% -> 1% of each run, Pallas kernels for 0% -> 22%
where the time goes in v1:
time: 100 us; the launch traced here: 99.4 us
  Pallas kernels  31.7 us (32%)
  waiting for transfers between devices  30.5 us (30%)
  starting transfers between devices  26.1 us (26%)
  local copies, waits for them, and re-layouts  9.61 us (10%)
    pallas_call x10, Pallas kernels, call(): pl.pallas_call(kernel, grid=grid, in_specs=[spec(i) for i in ins], out_sp...  31.7 us
    ppermute x6, starting transfers between devices, send(): lax.ppermute(own.astype(bf16), 'seq', chain_routes(count, hop))  9.65 us
    ppermute x2, waiting for transfers between devices, edge(): return lax.ppermute(made, 'seq', [(i + 1, i) for i in range(count - 1)])  9.58 us
    ppermute x3, waiting for transfers between devices, local(): lax.ppermute(to_seq, 'seq', [(i, (i + k) % count) for i in range(count)])  8.32 us
    ppermute x6, waiting for transfers between devices, send(): lax.ppermute(own.astype(bf16), 'seq', chain_routes(count, hop))  7.93 us
    unnamed x22, local copies, waits for them, and re-layouts  7.58 us
    ppermute x3, starting transfers between devices, local(): lax.ppermute(to_seq, 'seq', [(i, (i + k) % count) for i in range(count)])  6.87 us
    ppermute x1, starting transfers between devices, local(): halo = lax.ppermute(tails, 'seq', [(i, i + 1) for i in range(count - 1)])  4.92 us
  transfers between devices with their start and end apart: 15, of which 9 were waited for; matrix products, arithmetic and copies ran while one was open for 1% of the time, Pallas kernels for 22%

profile of v1, /device:TPU:0, one launch (start us, length us, event | category | flops | bytes accessed | tf_op | source)
XLA Modules:
  0.0 99.4 jit_solution(2743070999420554727)
XLA Ops:
  2.1 4.9 %collective-permute-start = (bf16[8,2816]{1,0:T(8,128)(2,1)S(1)}, bf16[8,2816]{1,0:T(8,128)(2,1)S(1)}, u32[]{:S(2)}, u32[]{:S(2)}) collective-permute-start(bf16[8,2816]{1,0:T(8,128)(2,1)S(1)} %pad_maximum_fusion), channel_id=1, source_target_pairs={{0,4},{4,8},{8,12},{1,5},{5,9},{9,13},{2,6},{6,10},{10,14},{3,7},{... | collective-permute-start | bytes 135176 | tf_op jit(solution)/shard_map/ppermute | solution.py:429
  7.0 1.7 %collective-permute-done.refs_3_.refs_6_.refs_2_.refs_18_ = bf16[8,2816]{1,0:T(8,128)(2,1)S(1)} collective-permute-done((bf16[8,2816]{1,0:T(8,128)(2,1)S(1)}, bf16[8,2816]{1,0:T(8,128)(2,1)S(1)}, u32[]{:S(2)}, u32[]{:S(2)}) %collective-permute-start) | collective-permute-done | bytes 45088 | tf_op jit(solution)/shard_map/ppermute | solution.py:429
  8.7 1.3 %copy-done = bf16[1,256,2560]{2,1,0:T(8,128)(2,1)S(1)} copy-done((bf16[1,256,2560]{2,1,0:T(8,128)(2,1)S(1)}, bf16[1,256,2560]{2,1,0:T(8,128)(2,1)}, u32[]{:S(2)}) %copy-start) | copy-done | bytes 1310744
  10.0 1.3 %copy-done.1 = bf16[1,256,2560]{2,1,0:T(8,128)(2,1)S(1)} copy-done((bf16[1,256,2560]{2,1,0:T(8,128)(2,1)S(1)}, bf16[1,256,2560]{2,1,0:T(8,128)(2,1)}, u32[]{:S(2)}) %copy-start.1) | copy-done | bytes 1310744
  14.5 2.9 %local_state.2 = (f32[128,1280]{1,0:T(8,128)S(1)}, f32[128,1280]{1,0:T(8,128)S(1)}, f32[8,1280]{1,0:T(8,128)S(1)}, bf16[256,1280]{1,0:T(8,128)(2,1)S(1)}, bf16[2...) custom-call(f32[40,256]{1,0:T(8,128)S(1)} %bitcast.24, ...), custom_call_target="tpu_custom_call" | custom-call | tf_op jit(solution)/shard_map/local_state/pallas_call | solution.py:386
  17.5 4.3 %collective-permute-start.4 = (bf16[128,1280]{1,0:T(8,128)(2,1)S(1)}, bf16[128,1280]{1,0:T(8,128)(2,1)S(1)}, u32[]{:S(2)}, u32[]{:S(2)}) collective-permute-start(bf16[128,1280]{1,0:T(8,128)(2,1)S(1)} %select_convert_fusion), channel_id=1, source_target_pairs={{0,4},{12,8},{1,5},{13,9},{2,6},{14,10},{3,7},{15,11},{16,20},{28,... | collective-permute-start | bytes 983048 | tf_op jit(solution)/shard_map/ppermute | solution.py:489
  21.8 2.6 %local_state.3 = (f32[128,1280]{1,0:T(8,128)S(1)}, f32[128,1280]{1,0:T(8,128)S(1)}, f32[8,1280]{1,0:T(8,128)S(1)}, bf16[256,1280]{1,0:T(8,128)(2,1)S(1)}, bf16[256,1280]{1,0:T(8,128)(2,1)S(1)}) custom-call(f32[40,256]{1,0:T(8,128)S(1)} %bitcast.25, bf16[256,2560]{1,0:T(8,128)(2,1)S(1)} %bitcast.18, bf16[256,2560]{1,0:T(8,128)(2,1)S(1)} %bitcast.23, ...), custom_call_target="tpu_custom_call" | custom-call | tf_op jit(solution)/shard_map/local_state/pallas_call | solution.py:386
  24.5 1.3 %collective-permute-start.1 = (bf16[128,1280]{1,0:T(8,128)(2,1)S(1)}, bf16[128,1280]{1,0:T(8,128)(2,1)S(1)}, u32[]{:S(2)}, u32[]{:S(2)}) collective-permute-start(bf16[128,1280]{1,0:T(8,128)(2,1)S(1)} %select_convert_fusion.1), channel_id=1, source_target_pairs={{0,4},{12,8},{1,5},{13,9},{2,6},{14,10},{3,7},{15,11},{16,20},{28,... | collective-permute-start | bytes 983048 | tf_op jit(solution)/shard_map/ppermute | solution.py:489
  25.9 4.0 %collective-permute-done.4.refs_4_.refs_12_ = bf16[128,1280]{1,0:T(8,128)(2,1)S(1)} collective-permute-done((bf16[128,1280]{1,0:T(8,128)(2,1)S(1)}, bf16[128,1280]{1,0:T(8,128)(2,1)S(1)}, u32[]{:S(2)}, u32[]{:S(2)}) %collective-permute-start.4) | collective-permute-done | bytes 327712 | tf_op jit(solution)/shard_map/ppermute | solution.py:489
  30.7 3.9 %collective-permute-done.1.refs_4_.refs_12_ = bf16[128,1280]{1,0:T(8,128)(2,1)S(1)} collective-permute-done((bf16[128,1280]{1,0:T(8,128)(2,1)S(1)}, bf16[128,1280]{1,0:T(8,128)(2,1)S(1)}, u32[]{:S(2)}, u32[]{:S(2)}) %collective-permute-start.1) | collective-permute-done | bytes 327712 | tf_op jit(solution)/shard_map/ppermute | solution.py:489
  35.5 1.4 %collective-permute-start.7 = (bf16[128,1280]{1,0:T(8,128)(2,1)S(1)}, bf16[128,1280]{1,0:T(8,128)(2,1)S(1)}, u32[]{:S(2)}, u32[]{:S(2)}) collective-permute-start(bf16[128,1280]{1,0:T(8,128)(2,1)S(1)} %add_convert_fusion.1), channel_id=1, source_target_pairs={{8,12},{4,0},{9,13},{5,1},{10,14},{6,2},{11,15},{7,3},{24,28},{20,... | collective-permute-start | bytes 983048 | tf_op jit(solution)/shard_map/ppermute | solution.py:489
  37.1 1.3 %collective-permute-start.8 = (bf16[128,1280]{1,0:T(8,128)(2,1)S(1)}, bf16[128,1280]{1,0:T(8,128)(2,1)S(1)}, u32[]{:S(2)}, u32[]{:S(2)}) collective-permute-start(bf16[128,1280]{1,0:T(8,128)(2,1)S(1)} %add_convert_fusion), channel_id=1, source_target_pairs={{8,12},{4,0},{9,13},{5,1},{10,14},{6,2},{11,15},{7,3},{24,28},{20,... | collective-permute-start | bytes 983048 | tf_op jit(solution)/shard_map/ppermute | solution.py:489
  38.4 6.5 %inside_block.2 = (f32[256,1280]{1,0:T(8,128)S(1)}, f32[256,1280]{1,0:T(8,128)S(1)}, bf16[256,1280]{1,0:T(8,128)(2,1)S(1)}, bf16[256,1280]{1,0:T(8,128)(2,1)S(1)...) custom-call(bf16[256,2560]{1,0:T(8,128)(2,1)S(1)} %bitcast.19, bf16[256,2560]{1,0:T(8,128)(2,1)} %bitcast.20, ...), custom_call_target="tpu_custom_call" | custom-call | tf_op jit(solution)/shard_map/inside_block/pallas_call | solution.py:386
  46.0 1.3 %collective-permute-start.6 = (bf16[16,1280]{1,0:T(8,128)(2,1)S(1)}, bf16[16,1280]{1,0:T(8,128)(2,1)S(1)}, u32[]{:S(2)}, u32[]{:S(2)}) collective-permute-start(bf16[16,1280]{1,0:T(8,128)(2,1)S(1)} %first_rows.3), channel_id=1, source_target_pairs={{4,0},{8,4},{12,8},{5,1},{9,5},{13,9},{6,2},{10,6},{14,10},{7,3},{... | collective-permute-start | bytes 122888 | tf_op jit(solution)/shard_map/ppermute | solution.py:557
  47.2 7.4 %inside_block.3 = (f32[256,1280]{1,0:T(8,128)S(1)}, f32[256,1280]{1,0:T(8,128)S(1)}, bf16[256,1280]{1,0:T(8,128)(2,1)S(1)}, bf16[256,1280]{1,0:T(8,128)(2,1)S(1)...) custom-call(bf16[256,2560]{1,0:T(8,128)(2,1)} %bitcast.14, bf16[256,2560]{1,0:T(8,128)(2,1)} %bitcast.21, ...), custom_call_target="tpu_custom_call" | custom-call | tf_op jit(solution)/shard_map/inside_block/pallas_call | solution.py:386
  57.0 4.4 %collective-permute-done.6.refs_10_ = bf16[16,1280]{1,0:T(8,128)(2,1)S(1)} collective-permute-done((bf16[16,1280]{1,0:T(8,128)(2,1)S(1)}, bf16[16,1280]{1,0:T(8,128)(2,1)S(1)}, u32[]{:S(2)}, u32[]{:S(2)}) %collective-permute-start.6) | collective-permute-done | bytes 40992 | tf_op jit(solution)/shard_map/ppermute | solution.py:557
  61.4 5.2 %finish.2 = (bf16[256,2560]{1,0:T(8,128)(2,1)}, bf16[256,2560]{1,0:T(8,128)(2,1)}, f32[8,1280]{1,0:T(8,128)S(1)}, f32[256,256]{1,0:T(8,128)S(1)}) custom-call(s32[1]{0:T(128)} %bitcast.refs_0_, f32[256,1280]{1,0:T(8,128)S(1)} %get-tuple-element.59.refs_1_, f32[256,1280]{1,0:T(8,128)} %copy-done.2, bf16[256,1280]{1,0:T(8,128)(2,1)S(1)} %get-tuple-element.61.refs_2_.refs_3_, ...), custom_call_target="tpu_custom_call" | custom-call | tf_op jit(solution)/shard_map/finish/pallas_call | solution.py:386
  66.5 5.2 %collective-permute-done.3.refs_10_ = bf16[16,1280]{1,0:T(8,128)(2,1)S(1)} collective-permute-done((bf16[16,1280]{1,0:T(8,128)(2,1)S(1)}, bf16[16,1280]{1,0:T(8,128)(2,1)S(1)}, u32[]{:S(2)}, u32[]{:S(2)}) %collective-permute-start.3) | collective-permute-done | bytes 40992 | tf_op jit(solution)/shard_map/ppermute | solution.py:557
  71.7 5.8 %finish.3 = (bf16[256,2560]{1,0:T(8,128)(2,1)}, bf16[256,2560]{1,0:T(8,128)(2,1)}, f32[8,2944]{1,0:T(8,128)S(1)}, bf16[272,256]{1,0:T(8,128)(2,1)S(1)}, f32[256,256]{1,0:T(8,128)S(1)}) custom-call(s32[1]{0:T(128)} %bitcast.refs_0_, f32[256,1280]{1,0:T(8,128)S(1)} %get-tuple-element.50.refs_1_, ...), custom_call_target="tpu_custom_call", output_to_operand_aliasing={{0}: (15, {}), {1}: (16, {})} | custom-call | tf_op jit(solution)/shard_map/finish/pallas_call | solution.py:386
  77.6 1.5 %collective-permute-start.10 = (bf16[272,256]{1,0:T(8,128)(2,1)S(1)}, bf16[272,256]{1,0:T(8,128)(2,1)S(1)}, u32[]{:S(2)}, u32[]{:S(2)}) collective-permute-start(bf16[272,256]{1,0:T(8,128)(2,1)S(1)} %get-tuple-element.78), channel_id=1, source_target_pairs={{0,2},{2,0},{1,3},{3,1},{4,6},{6,4},{5,7},{7,5},{8,10},{10,8},{9,1... | collective-permute-start | bytes 417800 | tf_op jit(solution)/shard_map/ppermute | solution.py:647
  79.7 2.5 %collective-permute-done.11.refs_4_ = f32[8,256]{1,0:T(8,128)S(1)} collective-permute-done((f32[8,256]{1,0:T(8,128)S(1)}, f32[8,256]{1,0:T(8,128)S(1)}, u32[]{:S(2)}, u32[]{:S(2)}) %collective-permute-start.11) | collective-permute-done | bytes 8224 | tf_op jit(solution)/shard_map/ppermute | solution.py:649
  82.8 6.2 %collective-permute-start.14 = (bf16[16,2944]{1,0:T(8,128)(2,1)S(1)}, bf16[16,2944]{1,0:T(8,128)(2,1)S(1)}, u32[]{:S(2)}, u32[]{:S(2)}) collective-permute-start(bf16[16,2944]{1,0:T(8,128)(2,1)S(1)} %get-tuple-element.81), channel_id=1, source_target_pairs={{0,12},{4,0},{8,4},{12,8},{1,13},{5,1},{9,5},{13,9},{2,14},{6,2},{... | collective-permute-start | bytes 282632 | tf_op jit(solution)/shard_map/ppermute | solution.py:663
  89.6 2.5 %collective-permute-done.14.refs_6_ = bf16[16,2944]{1,0:T(8,128)(2,1)S(1)} collective-permute-done((bf16[16,2944]{1,0:T(8,128)(2,1)S(1)}, bf16[16,2944]{1,0:T(8,128)(2,1)S(1)}, u32[]{:S(2)}, u32[]{:S(2)}) %collective-permute-start.14) | collective-permute-done | bytes 94240 | tf_op jit(solution)/shard_map/ppermute | solution.py:663
  92.1 5.8 %collective-permute-done.13.refs_5_ = bf16[16,2944]{1,0:T(8,128)(2,1)S(1)} collective-permute-done((bf16[16,2944]{1,0:T(8,128)(2,1)S(1)}, bf16[16,2944]{1,0:T(8,128)(2,1)S(1)}, u32[]{:S(2)}, u32[]{:S(2)}) %collective-permute-start.13) | collective-permute-done | bytes 94240 | tf_op jit(solution)/shard_map/ppermute | solution.py:663
  (51 shorter events, 13.3 us)
Async XLA Ops:
  2.1 6.6 %collective-permute-start = (bf16[8,2816]{1,0:T(8,128)(2,1)S(1)}, bf16[8,2816]{1,0:T(8,128)(2,1)S(1)}, u32[]{:S(2)}, u32[]{:S(2)}) collective-permute-start(bf16[8,2816]{1,0:T(8,128)(2,1)S(1)} %pad_maximum_fusion), channel_id=1, source_target_pairs={{0,4},{4,8},{8,12},{1,5},{5,9},{9,13},{2,6},{6,10},{10,14},{3,7},{... | collective-permute-start | bytes 135176 | tf_op jit(solution)/shard_map/ppermute | solution.py:429
  8.7 1.3 %copy-start = (bf16[1,256,2560]{2,1,0:T(8,128)(2,1)S(1)}, bf16[1,256,2560]{2,1,0:T(8,128)(2,1)}, u32[]{:S(2)}) copy-start(bf16[1,256,2560]{2,1,0:T(8,128)(2,1)} %param.7) | copy-start | bytes 3932164
  10.0 1.3 %copy-start.1 = (bf16[1,256,2560]{2,1,0:T(8,128)(2,1)S(1)}, bf16[1,256,2560]{2,1,0:T(8,128)(2,1)}, u32[]{:S(2)}) copy-start(bf16[1,256,2560]{2,1,0:T(8,128)(2,1)} %param.13) | copy-start | bytes 3932164
  11.4 0.8 copy-start.4
  12.9 0.9 copy-start.7
  17.5 12.4 %collective-permute-start.4 = (bf16[128,1280]{1,0:T(8,128)(2,1)S(1)}, bf16[128,1280]{1,0:T(8,128)(2,1)S(1)}, u32[]{:S(2)}, u32[]{:S(2)}) collective-permute-start(bf16[128,1280]{1,0:T(8,128)(2,1)S(1)} %select_convert_fusion), channel_id=1, source_target_pairs={{0,4},{12,8},{1,5},{13,9},{2,6},{14,10},{3,7},{15,11},{16,20},{28,... | collective-permute-start | bytes 983048 | tf_op jit(solution)/shard_map/ppermute | solution.py:489
  24.5 10.1 %collective-permute-start.1 = (bf16[128,1280]{1,0:T(8,128)(2,1)S(1)}, bf16[128,1280]{1,0:T(8,128)(2,1)S(1)}, u32[]{:S(2)}, u32[]{:S(2)}) collective-permute-start(bf16[128,1280]{1,0:T(8,128)(2,1)S(1)} %select_convert_fusion.1), channel_id=1, source_target_pairs={{0,4},{12,8},{1,5},{13,9},{2,6},{14,10},{3,7},{15,11},{16,20},{28,... | collective-permute-start | bytes 983048 | tf_op jit(solution)/shard_map/ppermute | solution.py:489
  30.0 5.4 %collective-permute-start.5 = (bf16[128,1280]{1,0:T(8,128)(2,1)S(1)}, bf16[128,1280]{1,0:T(8,128)(2,1)S(1)}, u32[]{:S(2)}, u32[]{:S(2)}) collective-permute-start(bf16[128,1280]{1,0:T(8,128)(2,1)S(1)} %add_convert_fusion.2), channel_id=1, source_target_pairs={{4,8},{8,4},{5,9},{9,5},{6,10},{10,6},{7,11},{11,7},{20,24},{24,20... | collective-permute-start | bytes 983048 | tf_op jit(solution)/shard_map/ppermute | solution.py:489
  34.7 2.3 %collective-permute-start.2 = (bf16[128,1280]{1,0:T(8,128)(2,1)S(1)}, bf16[128,1280]{1,0:T(8,128)(2,1)S(1)}, u32[]{:S(2)}, u32[]{:S(2)}) collective-permute-start(bf16[128,1280]{1,0:T(8,128)(2,1)S(1)} %add_convert_fusion.3), channel_id=1, source_target_pairs={{4,8},{8,4},{5,9},{9,5},{6,10},{10,6},{7,11},{11,7},{20,24},{24,20... | collective-permute-start | bytes 983048 | tf_op jit(solution)/shard_map/ppermute | solution.py:489
  35.5 2.9 %copy-start.5 = (f32[4,2560]{1,0:T(4,128)S(1)}, f32[4,2560]{1,0:T(4,128)}, u32[]{:S(2)}) copy-start(f32[4,2560]{1,0:T(4,128)} %refs_6_.3) | copy-start | bytes 122884
  35.5 2.9 %copy-start.10 = (f32[40]{0:T(128)S(1)}, f32[40]{0:T(128)}, u32[]{:S(2)}) copy-start(f32[40]{0:T(128)} %refs_7_.5) | copy-start | bytes 484
  35.5 25.8 %collective-permute-start.7 = (bf16[128,1280]{1,0:T(8,128)(2,1)S(1)}, bf16[128,1280]{1,0:T(8,128)(2,1)S(1)}, u32[]{:S(2)}, u32[]{:S(2)}) collective-permute-start(bf16[128,1280]{1,0:T(8,128)(2,1)S(1)} %add_convert_fusion.1), channel_id=1, source_target_pairs={{8,12},{4,0},{9,13},{5,1},{10,14},{6,2},{11,15},{7,3},{24,28},{20,... | collective-permute-start | bytes 983048 | tf_op jit(solution)/shard_map/ppermute | solution.py:489
  37.1 34.6 %collective-permute-start.8 = (bf16[128,1280]{1,0:T(8,128)(2,1)S(1)}, bf16[128,1280]{1,0:T(8,128)(2,1)S(1)}, u32[]{:S(2)}, u32[]{:S(2)}) collective-permute-start(bf16[128,1280]{1,0:T(8,128)(2,1)S(1)} %add_convert_fusion), channel_id=1, source_target_pairs={{8,12},{4,0},{9,13},{5,1},{10,14},{6,2},{11,15},{7,3},{24,28},{20,... | collective-permute-start | bytes 983048 | tf_op jit(solution)/shard_map/ppermute | solution.py:489
  44.9 1.1 %copy-start.2 = (f32[256,1280]{1,0:T(8,128)}, f32[256,1280]{1,0:T(8,128)S(1)}, u32[]{:S(2)}) copy-start(f32[256,1280]{1,0:T(8,128)S(1)} %get-tuple-element.60.refs_1_.refs_2_) | copy-start | bytes 3932164
  46.0 15.4 %collective-permute-start.6 = (bf16[16,1280]{1,0:T(8,128)(2,1)S(1)}, bf16[16,1280]{1,0:T(8,128)(2,1)S(1)}, u32[]{:S(2)}, u32[]{:S(2)}) collective-permute-start(bf16[16,1280]{1,0:T(8,128)(2,1)S(1)} %first_rows.3), channel_id=1, source_target_pairs={{4,0},{8,4},{12,8},{5,1},{9,5},{13,9},{6,2},{10,6},{14,10},{7,3},{... | collective-permute-start | bytes 122888 | tf_op jit(solution)/shard_map/ppermute | solution.py:557
  54.6 1.1 %copy-start.3 = (f32[256,1280]{1,0:T(8,128)}, f32[256,1280]{1,0:T(8,128)S(1)}, u32[]{:S(2)}) copy-start(f32[256,1280]{1,0:T(8,128)S(1)} %get-tuple-element.51.refs_1_.refs_2_) | copy-start | bytes 3932164
  55.7 16.0 %collective-permute-start.3 = (bf16[16,1280]{1,0:T(8,128)(2,1)S(1)}, bf16[16,1280]{1,0:T(8,128)(2,1)S(1)}, u32[]{:S(2)}, u32[]{:S(2)}) collective-permute-start(bf16[16,1280]{1,0:T(8,128)(2,1)S(1)} %first_rows.2), channel_id=1, source_target_pairs={{4,0},{8,4},{12,8},{5,1},{9,5},{13,9},{6,2},{10,6},{14,10},{7,3},{... | collective-permute-start | bytes 122888 | tf_op jit(solution)/shard_map/ppermute | solution.py:557
  61.4 10.4 %copy-start.8 = (bf16[1,256,256]{2,1,0:T(8,128)(2,1)S(1)}, bf16[1,256,256]{2,1,0:T(8,128)(2,1)}, u32[]{:S(2)}) copy-start(bf16[1,256,256]{2,1,0:T(8,128)(2,1)} %param.8) | copy-start | bytes 393220
  77.6 5.1 %collective-permute-start.10 = (bf16[272,256]{1,0:T(8,128)(2,1)S(1)}, bf16[272,256]{1,0:T(8,128)(2,1)S(1)}, u32[]{:S(2)}, u32[]{:S(2)}) collective-permute-start(bf16[272,256]{1,0:T(8,128)(2,1)S(1)} %get-tuple-element.78), channel_id=1, source_target_pairs={{0,2},{2,0},{1,3},{3,1},{4,6},{6,4},{5,7},{7,5},{8,10},{10,8},{9,1... | collective-permute-start | bytes 417800 | tf_op jit(solution)/shard_map/ppermute | solution.py:647
  79.1 3.2 %collective-permute-start.9 = (f32[8,2944]{1,0:T(8,128)S(1)}, f32[8,2944]{1,0:T(8,128)S(1)}, u32[]{:S(2)}, u32[]{:S(2)}) collective-permute-start(f32[8,2944]{1,0:T(8,128)S(1)} %get-tuple-element.76.refs_0_), channel_id=1, source_target_pairs={{0,1},{1,0},{2,3},{3,2},{4,5},{5,4},{6,7},{7,6},{8,9},{9,8},{10,11... | collective-permute-start | bytes 282632 | tf_op jit(solution)/shard_map/ppermute | solution.py:643
  79.1 3.1 %collective-permute-start.11 = (f32[8,256]{1,0:T(8,128)S(1)}, f32[8,256]{1,0:T(8,128)S(1)}, u32[]{:S(2)}, u32[]{:S(2)}) collective-permute-start(f32[8,256]{1,0:T(8,128)S(1)} %slice.32), channel_id=1, source_target_pairs={{0,3},{1,2},{2,1},{3,0},{4,7},{5,6},{6,5},{7,4},{8,11},{9,10},{10,... | collective-permute-start | bytes 24584 | tf_op jit(solution)/shard_map/ppermute | solution.py:649
  82.8 9.3 %collective-permute-start.14 = (bf16[16,2944]{1,0:T(8,128)(2,1)S(1)}, bf16[16,2944]{1,0:T(8,128)(2,1)S(1)}, u32[]{:S(2)}, u32[]{:S(2)}) collective-permute-start(bf16[16,2944]{1,0:T(8,128)(2,1)S(1)} %get-tuple-element.81), channel_id=1, source_target_pairs={{0,12},{4,0},{8,4},{12,8},{1,13},{5,1},{9,5},{13,9},{2,14},{6,2},{... | collective-permute-start | bytes 282632 | tf_op jit(solution)/shard_map/ppermute | solution.py:663
  89.0 9.0 %collective-permute-start.13 = (bf16[16,2944]{1,0:T(8,128)(2,1)S(1)}, bf16[16,2944]{1,0:T(8,128)(2,1)S(1)}, u32[]{:S(2)}, u32[]{:S(2)}) collective-permute-start(bf16[16,2944]{1,0:T(8,128)(2,1)S(1)} %get-tuple-element.81), channel_id=1, source_target_pairs={{0,8},{4,12},{8,0},{12,4},{1,9},{5,13},{9,1},{13,5},{2,10},{6,14},... | collective-permute-start | bytes 282632 | tf_op jit(solution)/shard_map/ppermute | solution.py:663
  89.0 9.0 %collective-permute-start.12 = (bf16[16,2944]{1,0:T(8,128)(2,1)S(1)}, bf16[16,2944]{1,0:T(8,128)(2,1)S(1)}, u32[]{:S(2)}, u32[]{:S(2)}) collective-permute-start(bf16[16,2944]{1,0:T(8,128)(2,1)S(1)} %get-tuple-element.81), channel_id=1, source_target_pairs={{0,4},{4,8},{8,12},{12,0},{1,5},{5,9},{9,13},{13,1},{2,6},{6,10},{... | collective-permute-start | bytes 282632 | tf_op jit(solution)/shard_map/ppermute | solution.py:663
  (2 other events, 1.5 us)

commit v2 on v1

v2 whole, which is shorter than its diff:
```python
import functools

import jax
import jax.numpy as jnp
from jax import lax
from jax.experimental import pallas as pl
from jax.experimental.pallas import tpu as pltpu
from jax.sharding import PartitionSpec as P

BLOCK_LEN = 256
LANES = 128
HALO = 8
NEG = -1e30
f32 = jnp.float32
bf16 = jnp.bfloat16
HIGHEST = lax.Precision.HIGHEST
ROWS16 = 16
VMEM_LIMIT = 24 * 1024 * 1024


def dot(a, b, precision=None):
    return jnp.dot(a, b, preferred_element_type=f32, precision=precision)


def dot_nt(a, b):
    return lax.dot_general(a, b, (((1,), (1,)), ((), ())), preferred_element_type=f32)


def sigmoid(v):
    return 0.5 * jnp.tanh(0.5 * v) + 0.5


def conv_rows(pad_ref, taps, lanes, rows, first):
    total = None
    for k in range(len(taps)):
        term = taps[k] * pad_ref[first + k : first + k + rows, lanes]
        total = term if total is None else total + term
    return total


def tap_rows(ref, lanes, count):
    block = ref[:, lanes]
    return [block[k : k + 1] for k in range(count)]


def spread(row_a, row_b):
    half, rows = LANES // 2, row_a.shape[1]
    both = jnp.concatenate(
        [jnp.broadcast_to(row_a, (half, rows)), jnp.broadcast_to(row_b, (half, rows))], axis=0
    )
    return both.T


def column(row):
    return jnp.broadcast_to(row, (LANES, row.shape[1])).T


def running_sum(dec):
    rows = dec.shape[1]
    before = lax.broadcasted_iota(jnp.int32, (rows, rows), 0)
    after = lax.broadcasted_iota(jnp.int32, (rows, rows), 1)
    upper = (before <= after).astype(f32)
    return dot(jnp.log(dec), upper, HIGHEST)


def gain_of(dec):
    return jnp.sqrt((1.0 - dec) * (1.0 + dec))


def tail_of(cum):
    return jnp.exp(cum[:, -1:] - cum)


def mapped_of(bc_ref, bch_ref, wbc_ref, bcpad, rows):
    bcpad[0:HALO, :] = bch_ref[...].astype(f32)
    bcpad[HALO : HALO + rows, :] = bc_ref[...].astype(f32)
    taps = wbc_ref.shape[0]
    weights = [wbc_ref[k : k + 1, :] for k in range(taps)]
    return conv_rows(bcpad, weights, slice(None), rows, HALO - taps + 1)


def put_padded(pad_ref, halo, block):
    pad_ref[0:HALO, :] = halo
    pad_ref[HALO : HALO + block.shape[0], :] = block.astype(f32)


def tails_kernel(x_ref, bc_ref, out_ref):
    width = x_ref.shape[1]
    out_ref[:, :width] = x_ref[...].astype(f32)[ROWS16 - HALO :].astype(bf16)
    out_ref[:, width:] = bc_ref[...].astype(f32)[ROWS16 - HALO :].astype(bf16)


def head_rows(ref, h):
    return ref[pl.ds(h, 1), :], ref[pl.ds(h + 1, 1), :]


def first_state_kernel(head_dim, scale, *refs):
    dec_ref, x_ref, g_ref, wx_ref, bc_ref, wbc_ref, _ = refs[:7]
    u_ref, v_ref, tot_ref, gt16_ref, lg16_ref, x16_ref, cum_ref, map_ref, bc16_ref = refs[7:16]
    xpad, bt, ct, gt, sl, lw, lg, bcpad = refs[16:]
    rows, width = x_ref.shape
    taps = wx_ref.shape[0]
    state = bt.shape[0]

    @pl.when(pl.program_id(0) == 0)
    def _():
        dec = dec_ref[...]
        cum = running_sum(dec)
        cum_ref[...] = cum
        put_padded(bcpad, jnp.zeros((HALO, bcpad.shape[1]), f32), bc_ref[...])
        weights = [wbc_ref[k : k + 1, :] for k in range(taps)]
        pre = conv_rows(bcpad, weights, slice(None), rows, HALO - taps + 1)
        mapped_f = pre * sigmoid(pre)
        map_ref[...] = mapped_f.astype(bf16)
        bc16_ref[...] = bc_ref[0:ROWS16, :]
        late = lax.broadcasted_iota(jnp.int32, mapped_f.shape, 0) >= ROWS16
        mapped_f = jnp.where(late, mapped_f, 0.0)
        bt[...] = mapped_f[:, :state].T.astype(bf16)
        ct[...] = mapped_f[:, state:].T.astype(bf16)
        gt[...] = gain_of(dec) * tail_of(cum)
        sl[...] = scale * jnp.exp(cum)

    put_padded(xpad, jnp.zeros((HALO, width), f32), x_ref[...])
    x16_ref[...] = x_ref[0:ROWS16, :]
    head0 = pl.program_id(0) * (width // head_dim)
    for q in range(width // LANES):
        lanes = slice(q * LANES, (q + 1) * LANES)
        h = head0 + 2 * q
        pre = conv_rows(xpad, tap_rows(wx_ref, lanes, taps), lanes, rows, HALO - taps + 1)
        inner = (pre * sigmoid(pre)).astype(bf16).astype(f32)
        factor = spread(*head_rows(gt, h))
        gt16_ref[:, lanes] = factor[0:ROWS16]
        lw[:, lanes] = (inner * factor).astype(bf16)
        lead = spread(*head_rows(sl, h))
        lg[:, lanes] = (g_ref[:, lanes].astype(f32) * lead).astype(bf16)
        tot_ref[:, lanes] = jnp.broadcast_to(lead[rows - 1 :, :] * (1.0 / scale), (8, LANES))
    lg16_ref[...] = lg[0:ROWS16, :]
    u_ref[...] = dot(bt[...], lw[...])
    v_ref[...] = dot(ct[...], lg[...])


def fix_kernel(*refs):
    place_ref, u_ref, v_ref, gt16_ref, lg16_ref, x16_ref, wx_ref, halo_ref = refs[:8]
    map_ref, bc16_ref, wbc_ref = refs[8:11]
    pay_ref, u_out, v_out, map_out, xpad, bcpad = refs[11:]
    width = x16_ref.shape[1]
    inner_width = wx_ref.shape[1]
    taps = wx_ref.shape[0]
    state = map_ref.shape[1] // 2
    halo = halo_ref[...].astype(f32)
    put_padded(xpad, halo[:, :width], x16_ref[...])
    put_padded(bcpad, halo[:, inner_width:], bc16_ref[...])
    lanes = slice(0, width)
    pre = conv_rows(xpad, tap_rows(wx_ref, lanes, taps), lanes, ROWS16, HALO - taps + 1)
    inner = (pre * sigmoid(pre)).astype(bf16).astype(f32)
    lw = (inner * gt16_ref[...]).astype(bf16)
    weights = [wbc_ref[k : k + 1, :] for k in range(taps)]
    pre_bc = conv_rows(bcpad, weights, slice(None), ROWS16, HALO - taps + 1)
    mapped = (pre_bc * sigmoid(pre_bc)).astype(bf16)
    map_out[...] = map_ref[...]
    map_out[0:ROWS16, :] = mapped
    first = (((0,), (0,)), ((), ()))
    u = u_ref[...] + lax.dot_general(mapped[:, :state], lw, first, preferred_element_type=f32)
    v = v_ref[...] + lax.dot_general(
        mapped[:, state:], lg16_ref[...], first, preferred_element_type=f32
    )
    u_out[...] = u
    v_out[...] = v
    pay_ref[...] = jnp.where(place_ref[0] == 0, u, v).astype(bf16)


def state_kernel(start, width, head_dim, scale, *refs):
    dec_ref, x_ref, g_ref, halo_ref, wx_ref, cum_ref, map_ref, _ = refs[:8]
    u_ref, v_ref, tot_ref = refs[8:11]
    xpad, gt, sl, lw, lg = refs[11:]
    rows = x_ref.shape[0]
    taps = wx_ref.shape[0]
    state = map_ref.shape[1] // 2
    cum = cum_ref[...]
    gt[...] = gain_of(dec_ref[...]) * tail_of(cum)
    sl[...] = scale * jnp.exp(cum)
    chunk = slice(start, start + width)
    put_padded(xpad, halo_ref[:, chunk].astype(f32), x_ref[:, chunk])
    for q in range(width // LANES):
        lanes = slice(q * LANES, (q + 1) * LANES)
        full = slice(start + q * LANES, start + (q + 1) * LANES)
        h = start // head_dim + 2 * q
        pre = conv_rows(xpad, tap_rows(wx_ref, full, taps), lanes, rows, HALO - taps + 1)
        inner = (pre * sigmoid(pre)).astype(bf16).astype(f32)
        lw[:, lanes] = (inner * spread(*head_rows(gt, h))).astype(bf16)
        lead = spread(*head_rows(sl, h))
        lg[:, lanes] = (g_ref[:, full].astype(f32) * lead).astype(bf16)
        tot_ref[:, lanes] = jnp.broadcast_to(lead[rows - 1 :, :] * (1.0 / scale), (8, LANES))
    first = (((0,), (0,)), ((), ()))
    mapped = map_ref[...]
    u_ref[...] = lax.dot_general(mapped[:, :state], lw[...], first, preferred_element_type=f32)
    v_ref[...] = lax.dot_general(mapped[:, state:], lg[...], first, preferred_element_type=f32)


def message_kernel(hop, *refs):
    if hop:
        place_ref, u_ref, v_ref, tot_ref, came_ref, _, out_ref = refs
    else:
        place_ref, u_ref, v_ref, _, out_ref = refs
    own = jnp.where(place_ref[0] == hop, u_ref[...], v_ref[...])
    if hop:
        own = own + tot_ref[0:1, :] * came_ref[...].astype(f32)
    out_ref[...] = own.astype(bf16)


def intra_kernel(first, last, start, pairs, head_dim, scale, *refs):
    x_ref, g_ref, halo_ref, wx_ref, dec_ref, cum_ref, map_ref, skip_ref, _ = refs[:9]
    refs = refs[9:]
    if not first:
        dsim_in, gs_in = refs[:2]
        refs = refs[2:]
    y0_ref, dx_ref, q_ref, ls_ref, lw_ref, lg_ref, dsim_ref, gs_ref = refs[:8]
    refs = refs[8:]
    if last:
        dbc_ref = refs[0]
        refs = refs[1:]
    xpad, sim, gain, tail, sl = refs
    rows = x_ref.shape[0]
    width = pairs * LANES
    taps = wx_ref.shape[0]
    state = map_ref.shape[1] // 2
    half = rows // 2
    dec = dec_ref[...]
    gain[...] = gain_of(dec)
    tail[...] = tail_of(cum_ref[...])
    sl[...] = scale * jnp.exp(cum_ref[...])
    chunk = slice(start, start + width)
    put_padded(xpad, halo_ref[:, chunk].astype(f32), x_ref[:, chunk])
    sim[...] = dot_nt(map_ref[:, state:], map_ref[:, :state])
    if first:
        dsim_ref[...] = jnp.zeros(dsim_ref.shape, f32)
        gs_ref[...] = jnp.zeros(gs_ref.shape, f32)
    else:
        dsim_ref[...] = dsim_in[...]
        gs_ref[...] = gs_in[...]
    lane = lax.broadcasted_iota(jnp.int32, (1, LANES), 1)
    low = lane < head_dim
    r_i = lax.broadcasted_iota(jnp.int32, (half, half), 0)
    c_i = lax.broadcasted_iota(jnp.int32, (half, half), 1)
    lower = r_i >= c_i

    def pair(q, carry):
        lanes = pl.ds(pl.multiple_of(q * LANES, LANES), LANES)
        full = pl.ds(pl.multiple_of(start + q * LANES, LANES), LANES)
        h = start // head_dim + 2 * q
        pre = conv_rows(xpad, tap_rows(wx_ref, full, taps), lanes, rows, HALO - taps + 1)
        sg = sigmoid(pre)
        inner = (pre * sg).astype(bf16).astype(f32)
        sgrad = sg * (1.0 + pre * (1.0 - sg))
        gn = spread(*head_rows(gain, h))
        tl = spread(*head_rows(tail, h))
        ls = spread(*head_rows(sl, h))
        w = (inner * gn).astype(bf16)
        g = g_ref[:, full]
        gf = g.astype(f32)
        g_t = gf.T.astype(bf16)
        y = None
        dw_t = []
        for a in range(2):
            row = cum_ref[pl.ds(h + a, 1), :]
            col = column(row)
            keep = low if a == 0 else jnp.logical_not(low)
            d00 = jnp.exp(jnp.where(lower, col[:half] - row[:, :half], NEG))
            d10 = jnp.exp(col[half:] - row[:, :half])
            d11 = jnp.exp(jnp.where(lower, col[half:] - row[:, half:], NEG))
            m00 = (d00 * sim[0:half, 0:half]).astype(bf16)
            m10 = (d10 * sim[half:rows, 0:half]).astype(bf16)
            m11 = (d11 * sim[half:rows, half:rows]).astype(bf16)
            w_a = jnp.where(keep, w, jnp.zeros_like(w))
            top = dot(m00, w_a[:half])
            bot = dot(jnp.concatenate([m10, m11], axis=1), w_a)
            y_a = jnp.concatenate([top, bot], axis=0)
            y = y_a if y is None else y + y_a
            g_at = g_t[a * head_dim : (a + 1) * head_dim]
            left = dot(g_at, jnp.concatenate([m00, m10], axis=0))
            right = dot(g_at[:, half:], m11)
            dw_t.append(jnp.concatenate([left, right], axis=1))
            mix_top = dot_nt(g[:half], w_a[:half])
            mix_bot = dot_nt(g[half:], w_a)
            dsim_ref[0:half, 0:half] += d00 * mix_top
            dsim_ref[half:rows, 0:half] += d10 * mix_bot[:, :half]
            dsim_ref[half:rows, half:rows] += d11 * mix_bot[:, half:]
        dw = scale * jnp.concatenate(dw_t, axis=0).T
        skip = jnp.where(low, skip_ref[h], skip_ref[h + 1])
        y0_ref[:, lanes] = scale * y + skip * inner
        dx_ref[:, lanes] = (gn * dw + skip * gf) * sgrad
        q_ref[:, lanes] = (gn * tl * sgrad).astype(bf16)
        ls_ref[:, lanes] = ls.astype(bf16)
        lw_ref[:, lanes] = (inner * gn * tl).astype(bf16)
        lg_ref[:, lanes] = (gf * ls).astype(bf16)
        gi = jnp.sum(gf * inner, axis=0, keepdims=True)
        sum_a = jnp.sum(jnp.where(low, gi, 0.0), axis=1, keepdims=True)
        sum_b = jnp.sum(jnp.where(low, 0.0, gi), axis=1, keepdims=True)
        gs_ref[...] += jnp.where(lane == h, sum_a, 0.0) + jnp.where(lane == h + 1, sum_b, 0.0)
        return carry

    lax.fori_loop(0, pairs, pair, 0)
    if last:
        ds = scale * dsim_ref[...]
        high = ds.astype(bf16)
        rest = (ds - high.astype(f32)).astype(bf16)
        ds_t = ds.T
        high_t = ds_t.astype(bf16)
        rest_t = (ds_t - high_t.astype(f32)).astype(bf16)
        b, c = map_ref[:, :state], map_ref[:, state:]
        dbc_ref[:, :state] = dot(high_t, c) + dot(rest_t, c)
        dbc_ref[:, state:] = dot(high, b) + dot(rest, b)


def pick(place, parts, wanted):
    total = jnp.zeros(parts[0].shape, bf16)
    for hop, ref in enumerate(parts):
        total = jnp.where(place == wanted(hop), ref[...], total)
    return total


def edge_kernel(count, hops, parts, *refs):
    place_ref, map_ref = refs[:2]
    blocks, refs = refs[2 : 2 + 2 * parts], refs[2 + 2 * parts :]
    came, out_ref = refs[:hops], refs[hops]
    state = map_ref.shape[1] // 2
    grad = pick(place_ref[0], came, lambda hop: count - 2 - hop)
    extra = dot(map_ref[0:ROWS16, :state], grad)
    at = 0
    for p in range(parts):
        dx_ref, q_ref = blocks[2 * p : 2 * p + 2]
        lanes = slice(at, at + dx_ref.shape[1])
        rows = dx_ref[0:ROWS16, :] + q_ref[0:ROWS16, :].astype(f32) * extra[:, lanes]
        out_ref[:, lanes] = rows.astype(bf16)
        at += dx_ref.shape[1]


def finish_kernel(count, start, parts, last, pairs_a_step, *refs):
    hops = count - 1
    place_ref, x_ref, wx_ref, map_ref, edge_ref, dbc_in, _ = refs[:7]
    blocks, refs = refs[7 : 7 + 6 * parts], refs[7 + 6 * parts :]
    came, refs = refs[:hops], refs[hops:]
    if start:
        refs = refs[2:]
    if last:
        bc_ref, halo_ref, wbc_ref, gs_ref, before_ref = refs[:5]
        y_ref, gx_ref, own_ref, head_ref, sums_ref, sums_bc_ref = refs[5:11]
        dbc_ref, taps_ref, enter, grad, dpad, bcpad = refs[11:]
    else:
        y_ref, gx_ref, taps_ref, dbc_ref, enter, grad, dpad = refs
    rows = x_ref.shape[0]
    taps = wx_ref.shape[0]
    state = map_ref.shape[1] // 2
    step = pl.program_id(0)
    place = place_ref[0]
    b, c = map_ref[:, :state], map_ref[:, state:]

    def work(lo, part, at, out):
        y0_ref, dx_ref, q_ref, ls_ref, lw_ref, lg_ref = blocks[6 * part : 6 * part + 6]
        lanes, mine, here = (slice(v, v + LANES) for v in (lo, at, out))
        full = slice(start + lo, start + lo + LANES)
        inter = dot(c, enter[:, lanes])
        y_ref[:, here] = (y0_ref[:, mine] + ls_ref[:, mine].astype(f32) * inter).astype(bf16)
        inter = dot(b, grad[:, lanes])
        dpad[0:rows, here] = dx_ref[:, mine] + q_ref[:, mine].astype(f32) * inter
        dpad[rows : rows + HALO, here] = edge_ref[:, lanes].astype(f32)[0:HALO]
        weights = tap_rows(wx_ref, full, taps)
        x = x_ref[:, full].astype(f32)
        total = None
        sums = []
        for k in range(taps):
            shifted = dpad[taps - 1 - k : taps - 1 - k + rows, here]
            term = weights[k] * shifted
            total = term if total is None else total + term
            sums.append(jnp.sum(shifted * x, axis=0, keepdims=True))
        gx_ref[:, here] = total.astype(bf16)
        sums = jnp.concatenate(sums + [jnp.zeros((8 - taps, LANES), f32)], axis=0)
        taps_ref[:, lanes] = sums

    spans = []
    lo = 0
    for part in range(parts):
        for at in range(0, blocks[6 * part].shape[1], LANES):
            spans.append((lo, part, at))
            lo += LANES
    for number in range(len(spans) // pairs_a_step):

        @pl.when(step == number)
        def _(number=number):
            if number == 0:
                enter[...] = pick(place, came, lambda hop: hop + 1)
                grad[...] = pick(place, came, lambda hop: count - 2 - hop)
            for i in range(pairs_a_step):
                lo, part, at = spans[number * pairs_a_step + i]
                work(lo, part, at, i * LANES)

    @pl.when(step == pl.num_programs(0) - 1)
    def _():
        d_b, d_c = dbc_in[:, :state], dbc_in[:, state:]
        lo = 0
        for part in range(parts):
            lw_ref, lg_ref = blocks[6 * part + 4 : 6 * part + 6]
            lanes = slice(lo, lo + lw_ref.shape[1])
            d_b = d_b + dot_nt(lw_ref[...], grad[:, lanes])
            d_c = d_c + dot_nt(lg_ref[...], enter[:, lanes])
            lo += lw_ref.shape[1]
        dbc_ref[:, :state] = d_b
        dbc_ref[:, state:] = d_c
        if last:
            put_padded(bcpad, halo_ref[:, x_ref.shape[1] :].astype(f32), bc_ref[...])
            weights = [wbc_ref[k : k + 1, :] for k in range(taps)]
            pre = conv_rows(bcpad, weights, slice(None), rows, HALO - taps + 1)
            sg = sigmoid(pre)
            dpre = dbc_ref[...] * (sg * (1.0 + pre * (1.0 - sg)))
            own_ref[...] = dpre
            sums_ref[:, 0 : before_ref.shape[1]] = before_ref[...]
            sums_ref[:, before_ref.shape[1] :] = taps_ref[...]
            sums = []
            for k in range(taps):
                moved = bcpad[HALO - taps + 1 + k : HALO - taps + 1 + k + rows, :]
                sums.append(jnp.sum(dpre * moved, axis=0, keepdims=True))
            sums = jnp.concatenate(sums + [jnp.zeros((8 - taps, 2 * state), f32)], axis=0)
            sums_bc_ref[:, : 2 * state] = sums
            sums_bc_ref[:, 2 * state :] = gs_ref[...]
            head_ref[0:rows, :] = dpre.astype(bf16)
            head_ref[rows:, :] = jnp.concatenate([sums, jnp.zeros_like(sums)], axis=0).astype(bf16)


def merge_kernel(heads, *refs):
    sums_ref, sums_dp, small_ref, small_dp, own_ref = refs[:5]
    others, crosses = refs[5 : 4 + heads], refs[4 + heads : 3 + 2 * heads]
    full_ref, out_ref, send_ref = refs[3 + 2 * heads :]
    rows, bc = own_ref.shape
    half = sums_ref.shape[1] // 2
    full = own_ref[...]
    total = sums_ref[...] + sums_dp[...]
    small = small_ref[...] + small_dp[...]
    taps_bc = small[:, :bc]
    for ref in others:
        block = ref[...].astype(f32)
        full = full + block[:rows]
        taps_bc = taps_bc + block[rows : rows + 8]
    for ref in crosses:
        taps_bc = taps_bc + ref[:, :bc]
    full_ref[...] = full
    send_ref[0:4, 0:half] = total[0:4, :half]
    send_ref[4:8, 0:half] = total[0:4, half:]
    send_ref[0:4, half : half + bc] = taps_bc[0:4]
    send_ref[4:8, half : half + bc] = full[0:4]
    send_ref[:, half + bc :] = small[:, bc:]
    out_ref[...] = send_ref[...].astype(bf16)


def last_kernel(count, norm_tokens, norm_skip, *refs):
    place_ref, sums_ref, full_ref, wbc_ref = refs[:4]
    parts = refs[4 : 3 + count]
    gbc_ref, tx_ref, tbc_ref, skip_ref, dpad = refs[3 + count :]
    taps, bc = wbc_ref.shape
    rows = full_ref.shape[0]
    half = tx_ref.shape[1] // 2
    total = sums_ref[...].astype(f32)
    edge = jnp.zeros((4, bc), f32)
    for hop, ref in enumerate(parts):
        block = ref[...].astype(f32)
        total = total + block
        if hop == count - 2:
            edge = jnp.where(place_ref[0] < count - 1, block[4:8, half : half + bc], 0.0)
    tx_ref[:, :half] = total[0:taps, 0:half] * norm_tokens
    tx_ref[:, half:] = total[4 : 4 + taps, 0:half] * norm_tokens
    tbc_ref[...] = total[0:taps, half : half + bc] * norm_tokens
    skip_ref[...] = total[0:1, half + bc : half + bc + skip_ref.shape[1]] * norm_skip
    dpad[0:rows, :] = full_ref[...]
    dpad[rows : rows + 4, :] = edge
    out = None
    for k in range(taps):
        term = wbc_ref[k : k + 1, :] * dpad[taps - 1 - k : taps - 1 - k + rows, :]
        out = term if out is None else out + term
    gbc_ref[...] = out.astype(bf16)


def call(kernel, name, ins, outs, scratch=(), grid=(1,), kept=(), flops=0, nbytes=0):
    def spec(item):
        if not isinstance(item, tuple):
            whole = item.shape
            return pl.BlockSpec(whole, lambda *_: (0,) * len(whole))
        if item[1] == "smem":
            return pl.BlockSpec(memory_space=pltpu.SMEM)
        if item[1] == "any":
            return pl.BlockSpec(memory_space=pl.ANY)
        return pl.BlockSpec(item[1], item[2])

    def array(item):
        return item[0] if isinstance(item, tuple) else item

    return pl.pallas_call(
        kernel,
        grid=grid,
        in_specs=[spec(i) for i in ins],
        out_specs=[spec(o) for o in outs],
        out_shape=[array(o) for o in outs],
        scratch_shapes=list(scratch),
        compiler_params=pltpu.CompilerParams(vmem_limit_bytes=VMEM_LIMIT),
        cost_estimate=pl.CostEstimate(flops=flops, bytes_accessed=nbytes, transcendentals=0),
        input_output_aliases=dict(kept),
        name=name,
    )(*[array(i) for i in ins])


def chain_routes(count, hop):
    return [(hop, hop + 1), (count - 1 - hop, count - 2 - hop)]


def shape(s, d=f32):
    return jax.ShapeDtypeStruct(s, d)


def local(x_input, bc_input, decays, conv_x, conv_bc, skip_gain, grad_out):
    x, bc, dec, g = x_input[0], bc_input[0], decays[0], grad_out[0]
    rows, inner = x.shape
    taps = conv_x.shape[0]
    heads = dec.shape[0]
    head_dim = inner // heads
    bcw = bc.shape[1]
    state = bcw // 2
    scale = state ** (-0.5)
    count = lax.axis_size("seq")
    head_count = lax.axis_size("head")
    dp_count = lax.axis_size("dp")
    assert rows == BLOCK_LEN and 2 * head_dim == LANES and taps == 4
    assert count % 2 == 0 and count > 2 and dp_count == 2
    width = inner // 2
    chunks = (0, 1)
    block = 640 if width % 640 == 0 else LANES
    per = width // block
    pairs = width // LANES
    split = (pairs - pairs // 2, pairs // 2)
    place = lax.axis_index("seq").astype(jnp.int32).reshape(1)
    where_am_i = (place, "smem")

    def vmem(s, d=f32):
        return pltpu.VMEM(s, d)

    last16 = rows // ROWS16 - 1
    tails = call(
        tails_kernel,
        "tails",
        [
            (x, (ROWS16, inner), lambda i: (last16, 0)),
            (bc, (ROWS16, bcw), lambda i: (last16, 0)),
        ],
        [shape((HALO, inner + bcw), bf16)],
    )[0]
    halo = lax.ppermute(tails, "seq", [(i, i + 1) for i in range(count - 1)])

    def at(i):
        return (0, i)

    made = call(
        functools.partial(first_state_kernel, head_dim, scale),
        "first_state",
        [
            dec,
            (x, (rows, block), at),
            (g, (rows, block), at),
            (conv_x, (taps, block), at),
            bc,
            conv_bc,
            (tails, "any"),
        ],
        [
            (shape((state, width)), (state, block), at),
            (shape((state, width)), (state, block), at),
            (shape((8, width)), (8, block), at),
            (shape((ROWS16, width)), (ROWS16, block), at),
            (shape((ROWS16, width), bf16), (ROWS16, block), at),
            (shape((ROWS16, width), bf16), (ROWS16, block), at),
            shape((heads, rows)),
            shape((rows, bcw), bf16),
            shape((ROWS16, bcw), bf16),
        ],
        [
            vmem((rows + HALO, block)),
            vmem((state, rows), bf16),
            vmem((state, rows), bf16),
            vmem((heads, rows)),
            vmem((heads, rows)),
            vmem((rows, block), bf16),
            vmem((rows, block), bf16),
            vmem((rows + HALO, bcw)),
        ],
        grid=(per,),
    )
    u, v, tot, gt16, lg16, x16, cum, mapped, bc16 = made
    pay, u, v, mapped = call(
        fix_kernel,
        "fix_first_rows",
        [where_am_i, u, v, gt16, lg16, x16, conv_x, halo, mapped, bc16, conv_bc],
        [
            shape((state, width), bf16),
            shape((state, width)),
            shape((state, width)),
            shape((rows, bcw), bf16),
        ],
        [vmem((ROWS16 + HALO, width)), vmem((ROWS16 + HALO, bcw))],
    )
    states = [(u, v, tot)]
    received = [[], []]

    def hop_on(c, message):
        routes = chain_routes(count, len(received[c]))
        received[c].append(lax.ppermute(message, "seq", routes))

    def message(c, after):
        u, v, tot = states[c]
        hop = len(received[c])
        ins = [where_am_i, u, v]
        if hop:
            ins += [tot, received[c][-1]]
        return call(
            functools.partial(message_kernel, hop),
            "message",
            ins + [(after, "any")],
            [shape((state, width), bf16)],
        )[0]

    parts = [[], []]
    carried = []

    def inside(number, after):
        c, p = divmod(number, 2)
        first, last = number == 0, number == 3
        start = c * width + sum(split[:p]) * LANES
        span = split[p] * LANES
        ins = [x, g, halo, conv_x, dec, cum, mapped, (skip_gain, "smem"), (after, "any")]
        if not first:
            ins += carried
        outs = [
            shape((rows, span)),
            shape((rows, span)),
            shape((rows, span), bf16),
            shape((rows, span), bf16),
            shape((rows, span), bf16),
            shape((rows, span), bf16),
            shape((rows, rows)),
            shape((8, LANES)),
        ]
        if last:
            outs += [shape((rows, bcw))]
        made = call(
            functools.partial(intra_kernel, first, last, start, split[p], head_dim, scale),
            "inside_block",
            ins,
            outs,
            [
                vmem((rows + HALO, span)),
                vmem((rows, rows)),
                vmem((heads, rows)),
                vmem((heads, rows)),
                vmem((heads, rows)),
            ],
        )
        parts[c].append(made[:6])
        carried[:] = made[6:8]
        return made[-1]

    def edge(c):
        hops = count - 2
        ins = [where_am_i, mapped]
        for made in parts[c]:
            ins += made[1:3]
        made = call(
            functools.partial(edge_kernel, count, hops, len(parts[c])),
            "first_rows",
            ins + received[c][:hops],
            [shape((ROWS16, width), bf16)],
        )[0]
        return lax.ppermute(made, "seq", [(i + 1, i) for i in range(count - 1)])

    hop_on(0, pay)
    u, v, tot = call(
        functools.partial(state_kernel, width, width, head_dim, scale),
        "state",
        [dec, x, g, halo, conv_x, cum, mapped, (pay, "any")],
        [shape((state, width)), shape((state, width)), shape((8, width))],
        [
            vmem((rows + HALO, width)),
            vmem((heads, rows)),
            vmem((heads, rows)),
            vmem((rows, width), bf16),
            vmem((rows, width), bf16),
        ],
    )
    states.append((u, v, tot))
    done = inside(0, v)
    number = 1
    turn = 1
    sent = None
    for _ in range(2 * count - 3):
        sent = message(turn, done)
        hop_on(turn, sent)
        if number < 4:
            done = inside(number, sent)
            number += 1
        turn = 1 - turn
        if len(received[0]) == count - 1 and turn == 0:
            break
    edges = [edge(0), edge(1)]
    dbc = done

    y = gx = None
    before = None
    for c in chunks:
        last = c == 1
        a_step = 2 if pairs % 2 == 0 else 1
        steps = pairs // a_step
        step_lanes = a_step * LANES

        def out_at(i, c=c, steps=steps):
            return (0, c * steps + i)

        ins = [where_am_i, x, conv_x, mapped, edges[c], dbc, (sent, "any")]
        for made in parts[c]:
            ins += made
        ins += received[c]
        outs = [
            (shape((rows, inner), bf16), (rows, step_lanes), out_at),
            (shape((rows, inner), bf16), (rows, step_lanes), out_at),
        ]
        inner_scratch = [
            vmem((state, width), bf16),
            vmem((state, width), bf16),
            vmem((rows + HALO, step_lanes)),
        ]
        kept = ()
        if c:
            kept = ((len(ins), 0), (len(ins) + 1, 1))
            ins += [(y, "any"), (gx, "any")]
        if last:
            ins += [bc, halo, conv_bc, carried[1], before]
            outs += [
                shape((rows, bcw)),
                shape((rows + 16, bcw), bf16),
                shape((8, inner)),
                shape((8, bcw + LANES)),
            ]
            scratch = [vmem((rows, bcw)), vmem((8, width))] + inner_scratch
            scratch += [vmem((rows + HALO, bcw))]
        else:
            outs += [shape((8, width)), shape((rows, bcw))]
            scratch = inner_scratch
        made = call(
            functools.partial(finish_kernel, count, c * width, len(parts[c]), last, a_step),
            "finish",
            ins,
            outs,
            scratch,
            grid=(steps,),
            kept=kept,
        )
        y, gx = made[:2]
        if last:
            own, to_heads, sums, small = made[2:]
        else:
            before, dbc = made[2:]

    swap = [(0, 1), (1, 0)]
    sums_dp = lax.ppermute(sums, "dp", swap)
    small_dp = lax.ppermute(small, "dp", swap)
    others, crosses = [], []
    for k in range(1, head_count):
        turn = [(i, (i + k) % head_count) for i in range(head_count)]
        others.append(lax.ppermute(to_heads, "head", turn))
        both = [(2 * i + j, 2 * t + 1 - j) for i, t in turn for j in range(2)]
        crosses.append(lax.ppermute(small, ("head", "dp"), both))
    send_width = inner // 2 + bcw + LANES
    full, to_seq = call(
        functools.partial(merge_kernel, head_count),
        "merge",
        [sums, sums_dp, small, small_dp, own] + others + crosses,
        [shape((rows, bcw)), shape((8, send_width), bf16)],
        [vmem((8, send_width))],
    )
    from_seq = [
        lax.ppermute(to_seq, "seq", [(i, (i + k) % count) for i in range(count)])
        for k in range(1, count)
    ]
    token_count = rows * count * dp_count
    norm_tokens = float(token_count) ** (-0.5)
    norm_skip = float(token_count * head_dim) ** (-0.5)
    gbc, tx, tbc, skip = call(
        functools.partial(last_kernel, count, norm_tokens, norm_skip),
        "last",
        [where_am_i, to_seq, full, conv_bc] + from_seq,
        [
            shape((rows, bcw), bf16),
            shape((taps, inner)),
            shape((taps, bcw)),
            shape((1, heads)),
        ],
        [vmem((rows + 4, bcw))],
    )
    return y[None], gx[None], gbc[None], tx, tbc, skip.reshape(heads)


def solution(mesh):
    return jax.shard_map(
        local,
        mesh=mesh,
        in_specs=(
            P(("groups", "dp"), "seq", "head"),
            P(("groups", "dp"), "seq", None),
            P(("groups", "dp"), "head", "seq"),
            P(None, "head"),
            P(),
            P("head"),
            P(("groups", "dp"), "seq", "head"),
        ),
        out_specs=(
            P(("groups", "dp"), "seq", "head"),
            P(("groups", "dp"), "seq", "head"),
            P(("groups", "dp"), "seq", None),
            P("groups", "head"),
            P("groups", None),
            P(("groups", "head")),
        ),
        check_vma=False,
    )
```

time: 100 us -> 79.6 us (0.80)
  waiting for transfers between devices: 30.5 us -> 19.9 us
  local copies, waits for them, and re-layouts: 9.61 us -> 4.46 us
  starting transfers between devices: 26.1 us -> 22.6 us
    ppermute x7 -> x8, waiting for transfers between devices: 10.4 us -> 3.07 us  [the longest x1 2.36 us: local(): crosses.append(lax.ppermute(small, ('head', 'dp'), both))]
    ppermute x3, waiting for transfers between devices: 8.32 us -> 2.39 us  [local(): lax.ppermute(to_seq, 'seq', [(i, (i + k) % count) for i in range(count)])]
    ppermute x2, waiting for transfers between devices: 9.58 us -> 14.4 us  [edge(): return lax.ppermute(made, 'seq', [(i + 1, i) for i in range(count - 1)])]
    unnamed x22, local copies, waits for them, and re-layouts: 7.58 us -> 4.46 us
    ppermute x3, starting transfers between devices: 6.87 us -> 3.86 us  [local(): lax.ppermute(to_seq, 'seq', [(i, (i + k) % count) for i in range(count)])]
    ppermute x1, waiting for transfers between devices: 1.68 us -> 0.01 us  [local(): halo = lax.ppermute(tails, 'seq', [(i, i + 1) for i in range(count - 1)])]
    slice x5 -> x0, local copies, waits for them, and re-layouts: 1.52 us -> none  [the longest x2 1.47 us: local(): tails = jnp.concatenate([x[rows - HALO:], bc[rows - HALO:]], axis=1)]
    ppermute x7 -> x8, starting transfers between devices: 10.3 us -> 9.41 us  [the longest x6 8.76 us: hop_on(): received[c].append(lax.ppermute(message, 'seq', routes))]
  transfers between devices with their start and end apart: 15 -> 16, of which waited for: 9 -> 5; matrix products, arithmetic and copies ran while one was open for 1% -> 0% of each run, Pallas kernels for 22% -> 32%
where the time goes in v2:
time: 79.6 us; the launch traced here: 79.2 us
  Pallas kernels  31.3 us (39%)
  starting transfers between devices  22.6 us (28%)
  waiting for transfers between devices  19.9 us (25%)
  local copies, waits for them, and re-layouts  4.46 us (6%)
  between operations  0.92 us (1%)
    pallas_call x19, Pallas kernels, call(): pl.pallas_call(kernel, grid=grid, in_specs=[spec(i) for i in ins], out_sp...  31.3 us
    ppermute x2, waiting for transfers between devices, edge(): return lax.ppermute(made, 'seq', [(i + 1, i) for i in range(count - 1)])  14.4 us
    ppermute x6, starting transfers between devices, hop_on(): received[c].append(lax.ppermute(message, 'seq', routes))  8.76 us
    ppermute x1, starting transfers between devices, local(): halo = lax.ppermute(tails, 'seq', [(i, i + 1) for i in range(count - 1)])  5.06 us
    unnamed x22, local copies, waits for them, and re-layouts  4.46 us
    ppermute x3, starting transfers between devices, local(): lax.ppermute(to_seq, 'seq', [(i, (i + k) % count) for i in range(count)])  3.86 us
    ppermute x2, starting transfers between devices, edge(): return lax.ppermute(made, 'seq', [(i + 1, i) for i in range(count - 1)])  2.76 us
    ppermute x3, waiting for transfers between devices, local(): lax.ppermute(to_seq, 'seq', [(i, (i + k) % count) for i in range(count)])  2.39 us
  transfers between devices with their start and end apart: 16, of which 5 were waited for; matrix products, arithmetic and copies ran while one was open for 0% of the time, Pallas kernels for 32%

profile of v2, /device:TPU:0, one launch (start us, length us, event | category | flops | bytes accessed | tf_op | source)
XLA Modules:
  0.0 79.2 jit_solution(131864355222868594)
XLA Ops:
  0.6 1.3 %copy-done = bf16[1,256,2560]{2,1,0:T(8,128)(2,1)S(1)} copy-done((bf16[1,256,2560]{2,1,0:T(8,128)(2,1)S(1)}, bf16[1,256,2560]{2,1,0:T(8,128)(2,1)}, u32[]{:S(2)}) %copy-start) | copy-done | bytes 1310744
  2.0 0.9 %copy-done.6 = bf16[1,256,256]{2,1,0:T(8,128)(2,1)S(1)} copy-done((bf16[1,256,256]{2,1,0:T(8,128)(2,1)S(1)}, bf16[1,256,256]{2,1,0:T(8,128)(2,1)}, u32[]{:S(2)}) %copy-start.6) | copy-done | bytes 131096
  2.9 5.1 %collective-permute-start = (bf16[8,2816]{1,0:T(8,128)(2,1)S(1)}, bf16[8,2816]{1,0:T(8,128)(2,1)S(1)}, u32[]{:S(2)}, u32[]{:S(2)}) collective-permute-start(bf16[8,2816]{1,0:T(8,128)(2,1)S(1)} %tails.1.refs_6_), channel_id=1, source_target_pairs={{0,4},{4,8},{8,12},{1,5},{5,9},{9,13},{2,6},{6,10},{10,14},{3,7},{... | collective-permute-start | bytes 135176 | tf_op jit(solution)/shard_map/ppermute | solution.py:553
  8.0 1.3 %copy-done.2 = bf16[1,256,2560]{2,1,0:T(8,128)(2,1)S(1)} copy-done((bf16[1,256,2560]{2,1,0:T(8,128)(2,1)S(1)}, bf16[1,256,2560]{2,1,0:T(8,128)(2,1)}, u32[]{:S(2)}) %copy-start.2) | copy-done | bytes 1310744
  9.3 0.9 %copy-done.7 = bf16[1,256,256]{2,1,0:T(8,128)(2,1)S(1)} copy-done((bf16[1,256,256]{2,1,0:T(8,128)(2,1)S(1)}, bf16[1,256,256]{2,1,0:T(8,128)(2,1)}, u32[]{:S(2)}) %copy-start.7) | copy-done | bytes 131096
  10.2 2.8 %first_state.1 = (f32[128,1280]{1,0:T(8,128)S(1)}, f32[128,1280]{1,0:T(8,128)S(1)}, f32[8,1280]{1,0:T(8,128)S(1)}, f32[16,1280]{1,0:T(8,128)S(1)}, bf16[16,1280]...) custom-call(f32[40,256]{1,0:T(8,128)S(1)} %bitcast.24, ...), custom_call_target="tpu_custom_call" | custom-call | tf_op jit(solution)/shard_map/first_state/pallas_call | solution.py:495
  13.5 3.5 %collective-permute-start.1 = (bf16[128,1280]{1,0:T(8,128)(2,1)S(1)}, bf16[128,1280]{1,0:T(8,128)(2,1)S(1)}, u32[]{:S(2)}, u32[]{:S(2)}) collective-permute-start(bf16[128,1280]{1,0:T(8,128)(2,1)S(1)} %get-tuple-element.82.refs_7_), channel_id=1, source_target_pairs={{0,4},{12,8},{1,5},{13,9},{2,6},{14,10},{3,7},{15,11},{16,20},{28,... | collective-permute-start | bytes 983048 | tf_op jit(solution)/shard_map/ppermute | solution.py:611
  17.0 2.0 %state.1 = (f32[128,1280]{1,0:T(8,128)S(1)}, f32[128,1280]{1,0:T(8,128)S(1)}, f32[8,1280]{1,0:T(8,128)S(1)}) custom-call(f32[40,256]{1,0:T(8,128)S(1)} %bitcast.25, bf16[256,2560]{1,0:T(8,128)(2,1)S(1)} %bitcast.11, bf16[256,2560]{1,0:T(8,128)(2,1)S(1)} %bitcast.19, bf16[8,2816]{1,0:T(8,128)(2,1)S(1)} %collective-permute-done.refs_7_.refs_3_.refs_2_.refs_25_, ...), custom_call_target="tpu_custom_call" | custom-call | tf_op jit(solution)/shard_map/state/pallas_call | solution.py:495
  19.1 3.5 %inside_block.4 = (f32[256,640]{1,0:T(8,128)S(1)}, f32[256,640]{1,0:T(8,128)S(1)}, bf16[256,640]{1,0:T(8,128)(2,1)S(1)}, bf16[256,640]{1,0:T(8,128)(2,1)S(1)}, b...) custom-call(bf16[256,2560]{1,0:T(8,128)(2,1)S(1)} %bitcast.12, ...), custom_call_target="tpu_custom_call" | custom-call | tf_op jit(solution)/shard_map/inside_block/pallas_call | solution.py:495
  22.7 1.3 %collective-permute-start.2 = (bf16[128,1280]{1,0:T(8,128)(2,1)S(1)}, bf16[128,1280]{1,0:T(8,128)(2,1)S(1)}, u32[]{:S(2)}, u32[]{:S(2)}) collective-permute-start(bf16[128,1280]{1,0:T(8,128)(2,1)S(1)} %message.5.refs_8_), channel_id=1, source_target_pairs={{0,4},{12,8},{1,5},{13,9},{2,6},{14,10},{3,7},{15,11},{16,20},{28,... | collective-permute-start | bytes 983048 | tf_op jit(solution)/shard_map/ppermute | solution.py:611
  24.0 3.5 %inside_block.5 = (f32[256,640]{1,0:T(8,128)S(1)}, f32[256,640]{1,0:T(8,128)S(1)}, bf16[256,640]{1,0:T(8,128)(2,1)S(1)}, bf16[256,640]{1,0:T(8,128)(2,1)S(1)}, b...) custom-call(bf16[256,2560]{1,0:T(8,128)(2,1)S(1)} %bitcast.13, ...), custom_call_target="tpu_custom_call" | custom-call | tf_op jit(solution)/shard_map/inside_block/pallas_call | solution.py:495
  28.4 3.5 %inside_block.6 = (f32[256,640]{1,0:T(8,128)S(1)}, f32[256,640]{1,0:T(8,128)S(1)}, bf16[256,640]{1,0:T(8,128)(2,1)S(1)}, bf16[256,640]{1,0:T(8,128)(2,1)S(1)}, b...) custom-call(bf16[256,2560]{1,0:T(8,128)(2,1)S(1)} %bitcast.14, ...), custom_call_target="tpu_custom_call" | custom-call | tf_op jit(solution)/shard_map/inside_block/pallas_call | solution.py:495
  32.7 4.2 %inside_block.7 = (f32[256,640]{1,0:T(8,128)S(1)}, f32[256,640]{1,0:T(8,128)S(1)}, bf16[256,640]{1,0:T(8,128)(2,1)S(1)}, bf16[256,640]{1,0:T(8,128)(2,1)S(1)}, b...) custom-call(bf16[256,2560]{1,0:T(8,128)(2,1)S(1)} %bitcast.15, ...), custom_call_target="tpu_custom_call" | custom-call | tf_op jit(solution)/shard_map/inside_block/pallas_call | solution.py:495
  37.0 1.3 %collective-permute-start.7 = (bf16[128,1280]{1,0:T(8,128)(2,1)S(1)}, bf16[128,1280]{1,0:T(8,128)(2,1)S(1)}, u32[]{:S(2)}, u32[]{:S(2)}) collective-permute-start(bf16[128,1280]{1,0:T(8,128)(2,1)S(1)} %message.9), channel_id=1, source_target_pairs={{8,12},{4,0},{9,13},{5,1},{10,14},{6,2},{11,15},{7,3},{24,28},{20,... | collective-permute-start | bytes 983048 | tf_op jit(solution)/shard_map/ppermute | solution.py:611
  38.4 1.3 %collective-permute-start.8 = (bf16[128,1280]{1,0:T(8,128)(2,1)S(1)}, bf16[128,1280]{1,0:T(8,128)(2,1)S(1)}, u32[]{:S(2)}, u32[]{:S(2)}) collective-permute-start(bf16[128,1280]{1,0:T(8,128)(2,1)S(1)} %message.8.refs_6_), channel_id=1, source_target_pairs={{8,12},{4,0},{9,13},{5,1},{10,14},{6,2},{11,15},{7,3},{24,28},{20,... | collective-permute-start | bytes 983048 | tf_op jit(solution)/shard_map/ppermute | solution.py:611
  39.9 1.3 %collective-permute-start.6 = (bf16[16,1280]{1,0:T(8,128)(2,1)S(1)}, bf16[16,1280]{1,0:T(8,128)(2,1)S(1)}, u32[]{:S(2)}, u32[]{:S(2)}) collective-permute-start(bf16[16,1280]{1,0:T(8,128)(2,1)S(1)} %first_rows.3), channel_id=1, source_target_pairs={{4,0},{8,4},{12,8},{5,1},{9,5},{13,9},{6,2},{10,6},{14,10},{7,3},{... | collective-permute-start | bytes 122888 | tf_op jit(solution)/shard_map/ppermute | solution.py:677
  41.4 1.5 %collective-permute-start.4 = (bf16[16,1280]{1,0:T(8,128)(2,1)S(1)}, bf16[16,1280]{1,0:T(8,128)(2,1)S(1)}, u32[]{:S(2)}, u32[]{:S(2)}) collective-permute-start(bf16[16,1280]{1,0:T(8,128)(2,1)S(1)} %first_rows.2), channel_id=1, source_target_pairs={{4,0},{8,4},{12,8},{5,1},{9,5},{13,9},{6,2},{10,6},{14,10},{7,3},{... | collective-permute-start | bytes 122888 | tf_op jit(solution)/shard_map/ppermute | solution.py:677
  42.9 14.4 %collective-permute-done.6.refs_4_ = bf16[16,1280]{1,0:T(8,128)(2,1)S(1)} collective-permute-done((bf16[16,1280]{1,0:T(8,128)(2,1)S(1)}, bf16[16,1280]{1,0:T(8,128)(2,1)S(1)}, u32[]{:S(2)}, u32[]{:S(2)}) %collective-permute-start.6) | collective-permute-done | bytes 40992 | tf_op jit(solution)/shard_map/ppermute | solution.py:677
  57.3 4.6 %finish.2 = (bf16[256,2560]{1,0:T(8,128)(2,1)}, bf16[256,2560]{1,0:T(8,128)(2,1)}, f32[8,1280]{1,0:T(8,128)S(1)}, f32[256,256]{1,0:T(8,128)S(1)}) custom-call(s32[1]{0:T(128)} %bitcast.refs_0_, bf16[256,2560]{1,0:T(8,128)(2,1)S(1)} %bitcast.16, f32[4,2560]{1,0:T(4,128)S(1)} %copy-done.4, bf16[256,256]{1,0:T(8,128)(2,1)S(1)} %get-tuple-element.77.refs_6_.refs_1_.refs_3_, ...), custom_call_target="tpu_custom_call" | custom-call | tf_op jit(solution)/shard_map/finish/pallas_call | solution.py:495
  61.9 4.9 %finish.3 = (bf16[256,2560]{1,0:T(8,128)(2,1)}, bf16[256,2560]{1,0:T(8,128)(2,1)}, f32[256,256]{1,0:T(8,128)S(1)}, bf16[272,256]{1,0:T(8,128)(2,1)S(1)}, f32[8,2560]{1,0:T(8,128)S(1)}, /*index=5*/f32[8,384]{1,0:T(8,128)S(1)}) custom-call(s32[1]{0:T(128)} %bitcast.refs_0_, ...), custom_call_target="tpu_custom_call", output_to_operand_aliasing={{0}: (22, {}), {1}: (23, {})} | custom-call | tf_op jit(solution)/shard_map/finish/pallas_call | solution.py:495
  66.8 1.5 %collective-permute-start.11 = (bf16[272,256]{1,0:T(8,128)(2,1)S(1)}, bf16[272,256]{1,0:T(8,128)(2,1)S(1)}, u32[]{:S(2)}, u32[]{:S(2)}) collective-permute-start(bf16[272,256]{1,0:T(8,128)(2,1)S(1)} %get-tuple-element.127), channel_id=1, source_target_pairs={{0,2},{2,0},{1,3},{3,1},{4,6},{6,4},{5,7},{7,5},{8,10},{10,8},{9,1... | collective-permute-start | bytes 417800 | tf_op jit(solution)/shard_map/ppermute | solution.py:772
  69.6 2.4 %collective-permute-done.12.refs_6_ = f32[8,384]{1,0:T(8,128)S(1)} collective-permute-done((f32[8,384]{1,0:T(8,128)S(1)}, f32[8,384]{1,0:T(8,128)S(1)}, u32[]{:S(2)}, u32[]{:S(2)}) %collective-permute-start.12) | collective-permute-done | bytes 12320 | tf_op jit(solution)/shard_map/ppermute | solution.py:774
  72.2 3.7 %collective-permute-start.15 = (bf16[8,1664]{1,0:T(8,128)(2,1)S(1)}, bf16[8,1664]{1,0:T(8,128)(2,1)S(1)}, u32[]{:S(2)}, u32[]{:S(2)}) collective-permute-start(bf16[8,1664]{1,0:T(8,128)(2,1)S(1)} %get-tuple-element.128.refs_1_), channel_id=1, source_target_pairs={{0,12},{4,0},{8,4},{12,8},{1,13},{5,1},{9,5},{13,9},{2,14},{6,2},{... | collective-permute-start | bytes 79880 | tf_op jit(solution)/shard_map/ppermute | solution.py:784
  75.9 1.8 %collective-permute-done.13.refs_4_ = bf16[8,1664]{1,0:T(8,128)(2,1)S(1)} collective-permute-done((bf16[8,1664]{1,0:T(8,128)(2,1)S(1)}, bf16[8,1664]{1,0:T(8,128)(2,1)S(1)}, u32[]{:S(2)}, u32[]{:S(2)}) %collective-permute-start.13) | collective-permute-done | bytes 26656 | tf_op jit(solution)/shard_map/ppermute | solution.py:784
  (49 shorter events, 5.8 us)
Async XLA Ops:
  2.9 5.1 %copy-start.1 = (bf16[1,256,2560]{2,1,0:T(8,128)(2,1)S(1)}, bf16[1,256,2560]{2,1,0:T(8,128)(2,1)}, u32[]{:S(2)}) copy-start(bf16[1,256,2560]{2,1,0:T(8,128)(2,1)} %param.7) | copy-start | bytes 3932164
  2.9 5.1 %copy-start.4 = (f32[4,2560]{1,0:T(4,128)S(1)}, f32[4,2560]{1,0:T(4,128)}, u32[]{:S(2)}) copy-start(f32[4,2560]{1,0:T(4,128)} %refs_2_.3) | copy-start | bytes 122884
  2.9 5.1 %copy-start.5 = (f32[1,40,256]{2,1,0:T(8,128)S(1)}, f32[1,40,256]{2,1,0:T(8,128)}, u32[]{:S(2)}) copy-start(f32[1,40,256]{2,1,0:T(8,128)} %param.9) | copy-start | bytes 122884
  2.9 5.1 %copy-start.9 = (f32[4,256]{1,0:T(4,128)S(1)}, f32[4,256]{1,0:T(4,128)}, u32[]{:S(2)}) copy-start(f32[4,256]{1,0:T(4,128)} %refs_3_.11) | copy-start | bytes 12292
  2.9 10.2 %collective-permute-start = (bf16[8,2816]{1,0:T(8,128)(2,1)S(1)}, bf16[8,2816]{1,0:T(8,128)(2,1)S(1)}, u32[]{:S(2)}, u32[]{:S(2)}) collective-permute-start(bf16[8,2816]{1,0:T(8,128)(2,1)S(1)} %tails.1.refs_6_), channel_id=1, source_target_pairs={{0,4},{4,8},{8,12},{1,5},{5,9},{9,13},{2,6},{6,10},{10,14},{3,7},{... | collective-permute-start | bytes 135176 | tf_op jit(solution)/shard_map/ppermute | solution.py:553
  8.0 1.3 %copy-start.2 = (bf16[1,256,2560]{2,1,0:T(8,128)(2,1)S(1)}, bf16[1,256,2560]{2,1,0:T(8,128)(2,1)}, u32[]{:S(2)}) copy-start(bf16[1,256,2560]{2,1,0:T(8,128)(2,1)} %param.13) | copy-start | bytes 3932164
  13.1 4.0 %copy-start.3 = (bf16[1,256,2560]{2,1,0:T(8,128)(2,1)S(1)}, bf16[1,256,2560]{2,1,0:T(8,128)(2,1)}, u32[]{:S(2)}) copy-start(bf16[1,256,2560]{2,1,0:T(8,128)(2,1)} %param.13) | copy-start | bytes 3932164
  13.5 14.0 %collective-permute-start.1 = (bf16[128,1280]{1,0:T(8,128)(2,1)S(1)}, bf16[128,1280]{1,0:T(8,128)(2,1)S(1)}, u32[]{:S(2)}, u32[]{:S(2)}) collective-permute-start(bf16[128,1280]{1,0:T(8,128)(2,1)S(1)} %get-tuple-element.82.refs_7_), channel_id=1, source_target_pairs={{0,4},{12,8},{1,5},{13,9},{2,6},{14,10},{3,7},{15,11},{16,20},{28,... | collective-permute-start | bytes 983048 | tf_op jit(solution)/shard_map/ppermute | solution.py:611
  17.0 2.0 %copy-start.10 = (f32[40]{0:T(128)S(1)}, f32[40]{0:T(128)}, u32[]{:S(2)}) copy-start(f32[40]{0:T(128)} %refs_7_.7) | copy-start | bytes 484
  22.7 9.2 %collective-permute-start.2 = (bf16[128,1280]{1,0:T(8,128)(2,1)S(1)}, bf16[128,1280]{1,0:T(8,128)(2,1)S(1)}, u32[]{:S(2)}, u32[]{:S(2)}) collective-permute-start(bf16[128,1280]{1,0:T(8,128)(2,1)S(1)} %message.5.refs_8_), channel_id=1, source_target_pairs={{0,4},{12,8},{1,5},{13,9},{2,6},{14,10},{3,7},{15,11},{16,20},{28,... | collective-permute-start | bytes 983048 | tf_op jit(solution)/shard_map/ppermute | solution.py:611
  27.7 9.2 %collective-permute-start.5 = (bf16[128,1280]{1,0:T(8,128)(2,1)S(1)}, bf16[128,1280]{1,0:T(8,128)(2,1)S(1)}, u32[]{:S(2)}, u32[]{:S(2)}) collective-permute-start(bf16[128,1280]{1,0:T(8,128)(2,1)S(1)} %message.6.refs_8_), channel_id=1, source_target_pairs={{4,8},{8,4},{5,9},{9,5},{6,10},{10,6},{7,11},{11,7},{20,24},{24,20... | collective-permute-start | bytes 983048 | tf_op jit(solution)/shard_map/ppermute | solution.py:611
  32.0 6.3 %collective-permute-start.3 = (bf16[128,1280]{1,0:T(8,128)(2,1)S(1)}, bf16[128,1280]{1,0:T(8,128)(2,1)S(1)}, u32[]{:S(2)}, u32[]{:S(2)}) collective-permute-start(bf16[128,1280]{1,0:T(8,128)(2,1)S(1)} %message.7.refs_8_), channel_id=1, source_target_pairs={{4,8},{8,4},{5,9},{9,5},{6,10},{10,6},{7,11},{11,7},{20,24},{24,20... | collective-permute-start | bytes 983048 | tf_op jit(solution)/shard_map/ppermute | solution.py:611
  37.0 20.3 %collective-permute-start.7 = (bf16[128,1280]{1,0:T(8,128)(2,1)S(1)}, bf16[128,1280]{1,0:T(8,128)(2,1)S(1)}, u32[]{:S(2)}, u32[]{:S(2)}) collective-permute-start(bf16[128,1280]{1,0:T(8,128)(2,1)S(1)} %message.9), channel_id=1, source_target_pairs={{8,12},{4,0},{9,13},{5,1},{10,14},{6,2},{11,15},{7,3},{24,28},{20,... | collective-permute-start | bytes 983048 | tf_op jit(solution)/shard_map/ppermute | solution.py:611
  38.4 23.5 %collective-permute-start.8 = (bf16[128,1280]{1,0:T(8,128)(2,1)S(1)}, bf16[128,1280]{1,0:T(8,128)(2,1)S(1)}, u32[]{:S(2)}, u32[]{:S(2)}) collective-permute-start(bf16[128,1280]{1,0:T(8,128)(2,1)S(1)} %message.8.refs_6_), channel_id=1, source_target_pairs={{8,12},{4,0},{9,13},{5,1},{10,14},{6,2},{11,15},{7,3},{24,28},{20,... | collective-permute-start | bytes 983048 | tf_op jit(solution)/shard_map/ppermute | solution.py:611
  39.9 17.4 %collective-permute-start.6 = (bf16[16,1280]{1,0:T(8,128)(2,1)S(1)}, bf16[16,1280]{1,0:T(8,128)(2,1)S(1)}, u32[]{:S(2)}, u32[]{:S(2)}) collective-permute-start(bf16[16,1280]{1,0:T(8,128)(2,1)S(1)} %first_rows.3), channel_id=1, source_target_pairs={{4,0},{8,4},{12,8},{5,1},{9,5},{13,9},{6,2},{10,6},{14,10},{7,3},{... | collective-permute-start | bytes 122888 | tf_op jit(solution)/shard_map/ppermute | solution.py:677
  41.4 20.5 %collective-permute-start.4 = (bf16[16,1280]{1,0:T(8,128)(2,1)S(1)}, bf16[16,1280]{1,0:T(8,128)(2,1)S(1)}, u32[]{:S(2)}, u32[]{:S(2)}) collective-permute-start(bf16[16,1280]{1,0:T(8,128)(2,1)S(1)} %first_rows.2), channel_id=1, source_target_pairs={{4,0},{8,4},{12,8},{5,1},{9,5},{13,9},{6,2},{10,6},{14,10},{7,3},{... | collective-permute-start | bytes 122888 | tf_op jit(solution)/shard_map/ppermute | solution.py:677
  57.3 4.6 %copy-start.8 = (bf16[1,256,256]{2,1,0:T(8,128)(2,1)S(1)}, bf16[1,256,256]{2,1,0:T(8,128)(2,1)}, u32[]{:S(2)}) copy-start(bf16[1,256,256]{2,1,0:T(8,128)(2,1)} %param.8) | copy-start | bytes 393220
  66.8 5.2 %collective-permute-start.11 = (bf16[272,256]{1,0:T(8,128)(2,1)S(1)}, bf16[272,256]{1,0:T(8,128)(2,1)S(1)}, u32[]{:S(2)}, u32[]{:S(2)}) collective-permute-start(bf16[272,256]{1,0:T(8,128)(2,1)S(1)} %get-tuple-element.127), channel_id=1, source_target_pairs={{0,2},{2,0},{1,3},{3,1},{4,6},{6,4},{5,7},{7,5},{8,10},{10,8},{9,1... | collective-permute-start | bytes 417800 | tf_op jit(solution)/shard_map/ppermute | solution.py:772
  68.3 3.7 %collective-permute-start.9 = (f32[8,2560]{1,0:T(8,128)S(1)}, f32[8,2560]{1,0:T(8,128)S(1)}, u32[]{:S(2)}, u32[]{:S(2)}) collective-permute-start(f32[8,2560]{1,0:T(8,128)S(1)} %get-tuple-element.124.refs_0_), channel_id=1, source_target_pairs={{0,1},{1,0},{2,3},{3,2},{4,5},{5,4},{6,7},{7,6},{8,9},{9,8},{10,11... | collective-permute-start | bytes 245768 | tf_op jit(solution)/shard_map/ppermute | solution.py:767
  68.3 1.3 %collective-permute-start.10 = (f32[8,384]{1,0:T(8,128)S(1)}, f32[8,384]{1,0:T(8,128)S(1)}, u32[]{:S(2)}, u32[]{:S(2)}) collective-permute-start(f32[8,384]{1,0:T(8,128)S(1)} %get-tuple-element.125.refs_2_), channel_id=1, source_target_pairs={{0,1},{1,0},{2,3},{3,2},{4,5},{5,4},{6,7},{7,6},{8,9},{9,8},{10,11... | collective-permute-start | bytes 36872 | tf_op jit(solution)/shard_map/ppermute | solution.py:768
  68.8 3.2 %collective-permute-start.12 = (f32[8,384]{1,0:T(8,128)S(1)}, f32[8,384]{1,0:T(8,128)S(1)}, u32[]{:S(2)}, u32[]{:S(2)}) collective-permute-start(f32[8,384]{1,0:T(8,128)S(1)} %get-tuple-element.125.refs_2_), channel_id=1, source_target_pairs={{0,3},{1,2},{2,1},{3,0},{4,7},{5,6},{6,5},{7,4},{8,11},{9,10},{10,... | collective-permute-start | bytes 36872 | tf_op jit(solution)/shard_map/ppermute | solution.py:774
  72.0 5.7 %collective-permute-start.13 = (bf16[8,1664]{1,0:T(8,128)(2,1)S(1)}, bf16[8,1664]{1,0:T(8,128)(2,1)S(1)}, u32[]{:S(2)}, u32[]{:S(2)}) collective-permute-start(bf16[8,1664]{1,0:T(8,128)(2,1)S(1)} %get-tuple-element.128.refs_1_), channel_id=1, source_target_pairs={{0,4},{4,8},{8,12},{12,0},{1,5},{5,9},{9,13},{13,1},{2,6},{6,10},{... | collective-permute-start | bytes 79880 | tf_op jit(solution)/shard_map/ppermute | solution.py:784
  72.1 5.6 %collective-permute-start.14 = (bf16[8,1664]{1,0:T(8,128)(2,1)S(1)}, bf16[8,1664]{1,0:T(8,128)(2,1)S(1)}, u32[]{:S(2)}, u32[]{:S(2)}) collective-permute-start(bf16[8,1664]{1,0:T(8,128)(2,1)S(1)} %get-tuple-element.128.refs_1_), channel_id=1, source_target_pairs={{0,8},{4,12},{8,0},{12,4},{1,9},{5,13},{9,1},{13,5},{2,10},{6,14},... | collective-permute-start | bytes 79880 | tf_op jit(solution)/shard_map/ppermute | solution.py:784
  72.2 6.1 %collective-permute-start.15 = (bf16[8,1664]{1,0:T(8,128)(2,1)S(1)}, bf16[8,1664]{1,0:T(8,128)(2,1)S(1)}, u32[]{:S(2)}, u32[]{:S(2)}) collective-permute-start(bf16[8,1664]{1,0:T(8,128)(2,1)S(1)} %get-tuple-element.128.refs_1_), channel_id=1, source_target_pairs={{0,12},{4,0},{8,4},{12,8},{1,13},{5,1},{9,5},{13,9},{2,14},{6,2},{... | collective-permute-start | bytes 79880 | tf_op jit(solution)/shard_map/ppermute | solution.py:784
  (3 other events, 3.1 us)

commit v3 on v2

v3 whole, which is shorter than its diff:
```python
import functools

import jax
import jax.numpy as jnp
from jax import lax
from jax.experimental import pallas as pl
from jax.experimental.pallas import tpu as pltpu
from jax.sharding import PartitionSpec as P

BLOCK_LEN = 256
LANES = 128
HALO = 8
NEG = -1e30
f32 = jnp.float32
bf16 = jnp.bfloat16
HIGHEST = lax.Precision.HIGHEST
ROWS16 = 16
VMEM_LIMIT = 24 * 1024 * 1024


def dot(a, b, precision=None):
    return jnp.dot(a, b, preferred_element_type=f32, precision=precision)


def dot_nt(a, b):
    return lax.dot_general(a, b, (((1,), (1,)), ((), ())), preferred_element_type=f32)


def sigmoid(v):
    return 0.5 * jnp.tanh(0.5 * v) + 0.5


def conv_rows(pad_ref, weights, rows):
    first = HALO - len(weights) + 1
    total = None
    for k, weight in enumerate(weights):
        term = weight * pad_ref[first + k : first + k + rows, :]
        total = term if total is None else total + term
    return total


def tap_rows(ref, lanes):
    block = ref[:, lanes]
    return [block[k : k + 1] for k in range(block.shape[0])]


def silu_grad(pre):
    sg = sigmoid(pre)
    return sg * (1.0 + pre * (1.0 - sg))


def spread(row_a, row_b):
    half, rows = LANES // 2, row_a.shape[1]
    both = jnp.concatenate(
        [jnp.broadcast_to(row_a, (half, rows)), jnp.broadcast_to(row_b, (half, rows))], axis=0
    )
    return both.T


def column(row):
    return jnp.broadcast_to(row, (LANES, row.shape[1])).T


def running_sum(dec):
    rows = dec.shape[1]
    before = lax.broadcasted_iota(jnp.int32, (rows, rows), 0)
    after = lax.broadcasted_iota(jnp.int32, (rows, rows), 1)
    upper = (before <= after).astype(f32)
    return dot(jnp.log(dec), upper, HIGHEST)


def gain_of(dec):
    return jnp.sqrt((1.0 - dec) * (1.0 + dec))


def tail_of(cum):
    return jnp.exp(cum[:, -1:] - cum)


def put_padded(pad_ref, halo, block):
    pad_ref[0:HALO, :] = halo
    pad_ref[HALO : HALO + block.shape[0], :] = block.astype(f32)


def lane_blocks(width):
    return [slice(at, at + LANES) for at in range(0, width, LANES)]


def tails_kernel(x_hbm, bc_hbm, out_ref, x16, bc16, sems):
    rows, width = x_hbm.shape
    last = pl.ds(rows - ROWS16, ROWS16)
    run_copies(
        [
            pltpu.make_async_copy(x_hbm.at[last, :], x16, sems.at[0]),
            pltpu.make_async_copy(bc_hbm.at[last, :], bc16, sems.at[1]),
        ]
    )
    out_ref[:, :width] = x16[...].astype(f32)[ROWS16 - HALO :].astype(bf16)
    out_ref[:, width:] = bc16[...].astype(f32)[ROWS16 - HALO :].astype(bf16)


def run_copies(copies):
    for copy in copies:
        copy.start()
    for copy in copies:
        copy.wait()


def early_load_kernel(count, *refs):
    place_ref, x_hbm, g_hbm = refs[:3]
    small = (len(refs) - 7) // 2
    sources, kept, sems = refs[3 : 3 + small], refs[-1 - small : -1], refs[-1]
    xa, ga = refs[4 + small : 6 + small]
    place = place_ref[0]
    chunk = pl.ds(0, xa.shape[1])
    copies = [pltpu.make_async_copy(sources[i], kept[i], sems.at[i]) for i in range(small)]
    for copy in copies:
        copy.start()

    @pl.when(place == 0)
    def _():
        run_copies([pltpu.make_async_copy(x_hbm.at[:, chunk], xa, sems.at[small])])

    @pl.when(place == count - 1)
    def _():
        run_copies([pltpu.make_async_copy(g_hbm.at[:, chunk], ga, sems.at[small + 1])])

    for copy in copies:
        copy.wait()


def load_kernel(x_hbm, g_hbm, _, x_ref, g_ref, sems):
    run_copies(
        [
            pltpu.make_async_copy(x_hbm, x_ref, sems.at[0]),
            pltpu.make_async_copy(g_hbm, g_ref, sems.at[1]),
        ]
    )


def head_rows(ref, h):
    return ref[pl.ds(h, 1), :], ref[pl.ds(h + 1, 1), :]


def state_of(bc_rows, factors):
    over = (((0,), (0,)), ((), ()))
    return lax.dot_general(bc_rows, factors, over, preferred_element_type=f32)


def weighted_tails(start, heads_at, x_ref, wx_ref, halo, gt, pad, lw):
    rows, width = lw.shape
    for q, lanes in enumerate(lane_blocks(width)):
        full = slice(start + q * LANES, start + (q + 1) * LANES)
        one = pad.at[q]
        put_padded(one, halo(full), x_ref[:, full])
        pre = conv_rows(one, tap_rows(wx_ref, full), rows)
        inner = (pre * sigmoid(pre)).astype(bf16).astype(f32)
        factor = spread(*head_rows(gt, heads_at + 2 * q))
        lw[:, lanes] = (inner * factor).astype(bf16)


def led_gradients(start, heads_at, g_ref, sl, lg):
    for q, lanes in enumerate(lane_blocks(lg.shape[1])):
        full = slice(start + q * LANES, start + (q + 1) * LANES)
        lead = spread(*head_rows(sl, heads_at + 2 * q))
        lg[:, lanes] = (g_ref[:, full].astype(f32) * lead).astype(bf16)


def first_state_kernel(count, width, scale, *refs):
    place_ref, dec_ref, x_ref, g_ref, wx_ref, bc_ref, wbc_ref = refs[:7]
    uv_ref, lg16_ref, cum_ref, map_ref = refs[7:11]
    pad, gt, sl, lw, lg, bcpad = refs[11:]
    rows = x_ref.shape[0]
    state = map_ref.shape[1] // 2
    dec = dec_ref[...]
    cum = running_sum(dec)
    cum_ref[...] = cum
    for half in range(2):
        lanes = slice(half * state, (half + 1) * state)
        one = bcpad.at[half]
        put_padded(one, jnp.zeros((HALO, state), f32), bc_ref[:, lanes])
        pre = conv_rows(one, tap_rows(wbc_ref, lanes), rows)
        map_ref[:, lanes] = (pre * sigmoid(pre)).astype(bf16)
    place = place_ref[0]

    @pl.when(place == 0)
    def _():
        gt[...] = gain_of(dec) * tail_of(cum)
        none = jnp.zeros((HALO, LANES), f32)
        weighted_tails(0, 0, x_ref, wx_ref, lambda _: none, gt, pad, lw)
        uv_ref[...] = state_of(map_ref[:, :state], lw[...])

    @pl.when(place == count - 1)
    def _():
        sl[...] = scale * jnp.exp(cum)
        led_gradients(0, 0, g_ref, sl, lg)
        lg16_ref[...] = lg[0:ROWS16, :]
        c = map_ref[:, state:]
        late = lax.broadcasted_iota(jnp.int32, c.shape, 0) >= ROWS16
        uv_ref[...] = state_of(jnp.where(late, c, jnp.zeros_like(c)), lg[...])


def fix_kernel(count, *refs):
    place_ref, uv_ref, lg16_ref, halo_ref, map_ref, bc_ref, wbc_ref = refs[:7]
    pay_ref, map_out, bcpad = refs[7:]
    rows, bcw = map_ref.shape
    state = bcw // 2
    inner = halo_ref.shape[1] - bcw
    map_out[...] = map_ref[...]
    for half in range(2):
        lanes = slice(half * state, (half + 1) * state)
        one = bcpad.at[half]
        edge = halo_ref[:, inner + half * state : inner + (half + 1) * state].astype(f32)
        put_padded(one, edge, bc_ref[0:ROWS16, lanes])
        pre = conv_rows(one, tap_rows(wbc_ref, lanes), ROWS16)
        map_out[0:ROWS16, lanes] = (pre * sigmoid(pre)).astype(bf16)

    @pl.when(place_ref[0] == 0)
    def _():
        pay_ref[...] = uv_ref[...].astype(bf16)

    @pl.when(place_ref[0] == count - 1)
    def _():
        extra = state_of(map_out[0:ROWS16, state:], lg16_ref[...])
        pay_ref[...] = (uv_ref[...] + extra).astype(bf16)


def middle_state_kernel(count, start, heads_at, scale, *refs):
    place_ref, dec_ref, x_ref, g_ref, halo_ref, wx_ref, cum_ref, map_ref, _ = refs[:9]
    u_ref, v_ref, tot_ref = refs[9:12]
    pad, gt, sl, lw, lg = refs[12:]
    rows = x_ref.shape[0]
    state = map_ref.shape[1] // 2
    place = place_ref[0]

    @pl.when(jnp.logical_and(place > 0, place < count - 1))
    def _():
        cum = cum_ref[...]
        gt[...] = gain_of(dec_ref[...]) * tail_of(cum)
        lead = jnp.exp(cum)
        sl[...] = scale * lead

        def halo(full):
            return halo_ref[:, full].astype(f32)

        weighted_tails(start, heads_at, x_ref, wx_ref, halo, gt, pad, lw)
        led_gradients(start, heads_at, g_ref, sl, lg)
        for q, lanes in enumerate(lane_blocks(lw.shape[1])):
            low = lax.broadcasted_iota(jnp.int32, (8, LANES), 1) < LANES // 2
            a, b = (lead[heads_at + 2 * q + i :, rows - 1 :][:1] for i in range(2))
            tot_ref[:, lanes] = jnp.where(low, a, b)
        u_ref[...] = state_of(map_ref[:, :state], lw[...])
        v_ref[...] = state_of(map_ref[:, state:], lg[...])


def end_state_kernel(count, start, heads_at, scale, *refs):
    place_ref, dec_ref, x_ref, g_ref, halo_ref, wx_ref, cum_ref, map_ref, _ = refs[:9]
    pay_ref, pad, gt, sl, lw, lg = refs[9:]
    state = map_ref.shape[1] // 2
    place = place_ref[0]

    @pl.when(place == 0)
    def _():
        gt[...] = gain_of(dec_ref[...]) * tail_of(cum_ref[...])

        def halo(full):
            return halo_ref[:, full].astype(f32)

        weighted_tails(start, heads_at, x_ref, wx_ref, halo, gt, pad, lw)
        pay_ref[...] = state_of(map_ref[:, :state], lw[...]).astype(bf16)

    @pl.when(place == count - 1)
    def _():
        sl[...] = scale * jnp.exp(cum_ref[...])
        led_gradients(start, heads_at, g_ref, sl, lg)
        pay_ref[...] = state_of(map_ref[:, state:], lg[...]).astype(bf16)


def message_kernel(hop, place_ref, u_ref, v_ref, tot_ref, came_ref, _, out_ref):
    own = jnp.where(place_ref[0] == hop, u_ref[...], v_ref[...])
    out_ref[...] = (own + tot_ref[0:1, :] * came_ref[...].astype(f32)).astype(bf16)


def last_message_kernel(count, parts, *refs):
    hops = count - 2
    place_ref, u_ref, v_ref, tot_ref, map_ref = refs[:5]
    blocks, refs = refs[7 : 7 + 2 * parts], refs[7 + 2 * parts :]
    came, (out_ref, edge_ref) = refs[:hops], refs[hops:]
    state = u_ref.shape[0]
    place = place_ref[0]
    own = jnp.where(place == hops, u_ref[...], v_ref[...])
    own = own + tot_ref[0:1, :] * came[-1][...].astype(f32)
    out_ref[0:state, :] = own.astype(bf16)
    grad = pick(place, came, lambda hop: count - 2 - hop)
    extra = dot(map_ref[0:ROWS16, :state], grad)
    at = 0
    for p in range(parts):
        dx_ref, q_ref = blocks[2 * p : 2 * p + 2]
        lanes = slice(at, at + dx_ref.shape[1])
        rows = dx_ref[0:ROWS16, :] + q_ref[0:ROWS16, :].astype(f32) * extra[:, lanes]
        edge_ref[:, lanes] = rows.astype(bf16)
        at += dx_ref.shape[1]
    out_ref[state:, :] = edge_ref[...]


def intra_kernel(first, last, start, pairs, head_dim, scale, *refs):
    x_ref, g_ref, halo_ref, wx_ref, dec_ref, cum_ref, map_ref, skip_ref, _ = refs[:9]
    refs = refs[9:]
    if not first:
        dsim_in, gs_in = refs[:2]
        refs = refs[2:]
    y0_ref, dx_ref, q_ref, ls_ref, lw_ref, lg_ref, dsim_ref, gs_ref = refs[:8]
    refs = refs[8:]
    if last:
        dbc_ref = refs[0]
        refs = refs[1:]
    pad, sim, gain = refs
    rows = x_ref.shape[0]
    state = map_ref.shape[1] // 2
    half = rows // 2
    gain[...] = gain_of(dec_ref[...])
    sim[...] = dot_nt(map_ref[:, state:], map_ref[:, :state])
    if first:
        dsim_ref[...] = jnp.zeros(dsim_ref.shape, f32)
        gs_ref[...] = jnp.zeros(gs_ref.shape, f32)
    else:
        dsim_ref[...] = dsim_in[...]
        gs_ref[...] = gs_in[...]
    lane = lax.broadcasted_iota(jnp.int32, (1, LANES), 1)
    low = lane < head_dim
    r_i = lax.broadcasted_iota(jnp.int32, (half, half), 0)
    c_i = lax.broadcasted_iota(jnp.int32, (half, half), 1)
    lower = r_i >= c_i

    def pair(q):
        lanes = slice(q * LANES, (q + 1) * LANES)
        full = slice(start + q * LANES, start + (q + 1) * LANES)
        h = start // head_dim + 2 * q
        one = pad.at[q]
        put_padded(one, halo_ref[:, full].astype(f32), x_ref[:, full])
        pre = conv_rows(one, tap_rows(wx_ref, full), rows)
        sg = sigmoid(pre)
        inner = (pre * sg).astype(bf16).astype(f32)
        sgrad = sg * (1.0 + pre * (1.0 - sg))
        gn = spread(*head_rows(gain, h))
        cums = head_rows(cum_ref, h)
        cols = [column(row) for row in cums]
        both = jnp.where(low, cols[0], cols[1])
        tl = jnp.exp(both[rows - 1 :] - both)
        ls = scale * jnp.exp(both)
        w = (inner * gn).astype(bf16)
        g = g_ref[:, full]
        gf = g.astype(f32)
        g_t = gf.T.astype(bf16)
        y = None
        dw_t = []
        for a in range(2):
            row, col = cums[a], cols[a]
            keep = low if a == 0 else jnp.logical_not(low)
            d00 = jnp.exp(jnp.where(lower, col[:half] - row[:, :half], NEG))
            d10 = jnp.exp(col[half:] - row[:, :half])
            d11 = jnp.exp(jnp.where(lower, col[half:] - row[:, half:], NEG))
            m00 = (d00 * sim[0:half, 0:half]).astype(bf16)
            m10 = (d10 * sim[half:rows, 0:half]).astype(bf16)
            m11 = (d11 * sim[half:rows, half:rows]).astype(bf16)
            w_a = jnp.where(keep, w, jnp.zeros_like(w))
            top = dot(m00, w_a[:half])
            bot = dot(jnp.concatenate([m10, m11], axis=1), w_a)
            y_a = jnp.concatenate([top, bot], axis=0)
            y = y_a if y is None else y + y_a
            g_at = g_t[a * head_dim : (a + 1) * head_dim]
            left = dot(g_at, jnp.concatenate([m00, m10], axis=0))
            right = dot(g_at[:, half:], m11)
            dw_t.append(jnp.concatenate([left, right], axis=1))
            mix_top = dot_nt(g[:half], w_a[:half])
            mix_bot = dot_nt(g[half:], w_a)
            dsim_ref[0:half, 0:half] += d00 * mix_top
            dsim_ref[half:rows, 0:half] += d10 * mix_bot[:, :half]
            dsim_ref[half:rows, half:rows] += d11 * mix_bot[:, half:]
        dw = scale * jnp.concatenate(dw_t, axis=0).T
        skip = jnp.where(low, skip_ref[h], skip_ref[h + 1])
        y0_ref[:, lanes] = scale * y + skip * inner
        dx_ref[:, lanes] = (gn * dw + skip * gf) * sgrad
        q_ref[:, lanes] = (gn * tl * sgrad).astype(bf16)
        ls_ref[:, lanes] = ls.astype(bf16)
        lw_ref[:, lanes] = (inner * gn * tl).astype(bf16)
        lg_ref[:, lanes] = (gf * ls).astype(bf16)
        gi = jnp.sum(gf * inner, axis=0, keepdims=True)
        sum_a = jnp.sum(jnp.where(low, gi, 0.0), axis=1, keepdims=True)
        sum_b = jnp.sum(jnp.where(low, 0.0, gi), axis=1, keepdims=True)
        gs_ref[...] += jnp.where(lane == h, sum_a, 0.0) + jnp.where(lane == h + 1, sum_b, 0.0)

    for q in range(pairs):
        pair(q)
    if last:
        ds = scale * dsim_ref[...]
        high = ds.astype(bf16)
        rest = (ds - high.astype(f32)).astype(bf16)
        ds_t = ds.T
        high_t = ds_t.astype(bf16)
        rest_t = (ds_t - high_t.astype(f32)).astype(bf16)
        b, c = map_ref[:, :state], map_ref[:, state:]
        dbc_ref[:, :state] = dot(high_t, c) + dot(rest_t, c)
        dbc_ref[:, state:] = dot(high, b) + dot(rest, b)


def pick(place, parts, wanted, rows=None):
    total = jnp.zeros(parts[0].shape, bf16)
    for hop, ref in enumerate(parts):
        total = jnp.where(place == wanted(hop), ref[0:rows, :], total)
    return total


def finish_bc_kernel(count, last, parts, *refs):
    hops = count - 1
    place_ref, map_ref, dbc_in = refs[:3]
    blocks, refs = refs[5 : 5 + 2 * parts], refs[5 + 2 * parts :]
    came, refs = refs[:hops], refs[hops:]
    if last:
        bc_ref, halo_ref, wbc_ref, gs_ref, own_ref, small_ref, bcpad = refs
    else:
        (dbc_ref,) = refs
    rows, bcw = map_ref.shape
    state = bcw // 2
    place = place_ref[0]
    enter = pick(place, came, lambda hop: hop + 1, state)
    grad = pick(place, came, lambda hop: count - 2 - hop, state)
    d_b, d_c = dbc_in[:, :state], dbc_in[:, state:]
    lo = 0
    for part in range(parts):
        lw_ref, lg_ref = blocks[2 * part : 2 * part + 2]
        lanes = slice(lo, lo + lw_ref.shape[1])
        d_b = d_b + dot_nt(lw_ref[...], grad[:, lanes])
        d_c = d_c + dot_nt(lg_ref[...], enter[:, lanes])
        lo += lw_ref.shape[1]
    if not last:
        dbc_ref[:, :state] = d_b
        dbc_ref[:, state:] = d_c
        return
    taps = wbc_ref.shape[0]
    inner = halo_ref.shape[1] - bcw
    for half in range(2):
        lanes = slice(half * state, (half + 1) * state)
        one = bcpad.at[half]
        edge = halo_ref[:, inner + half * state : inner + (half + 1) * state].astype(f32)
        put_padded(one, edge, bc_ref[:, lanes])
        dpre = (d_b, d_c)[half] * silu_grad(conv_rows(one, tap_rows(wbc_ref, lanes), rows))
        own_ref[:, lanes] = dpre
        sums = []
        for k in range(taps):
            moved = one[HALO - taps + 1 + k : HALO - taps + 1 + k + rows, :]
            sums.append(jnp.sum(dpre * moved, axis=0, keepdims=True))
        sums = jnp.concatenate(sums + [jnp.zeros((8 - taps, state), f32)], axis=0)
        small_ref[:, lanes] = sums
    small_ref[:, bcw:] = gs_ref[...]


def finish_kernel(count, start, parts, pieces, *refs):
    hops = count - 1
    place_ref, x_ref, wx_ref, map_ref, edge_ref, _ = refs[:6]
    blocks, refs = refs[6 : 6 + 4 * parts], refs[6 + 4 * parts :]
    came, refs = refs[:hops], refs[hops:]
    if start:
        before_ref = refs[0]
        refs = refs[3:]
    y_hbm, gx_hbm, taps_ref, enter, grad, edge, pad, y_ref, gx_ref, sems = refs
    rows = x_ref.shape[0]
    taps = wx_ref.shape[0]
    state, width = enter.shape
    place = place_ref[0]
    b, c = map_ref[:, :state], map_ref[:, state:]
    enter[...] = pick(place, came, lambda hop: hop + 1, state)
    grad[...] = pick(place, came, lambda hop: count - 2 - hop, state)
    edge[...] = jnp.where(place == 0, came[-1][state:, :], edge_ref[...])
    if start:
        taps_ref[:, 0:start] = before_ref[...]
    spans = []
    for part in range(parts):
        for at in range(0, blocks[4 * part].shape[1], LANES):
            spans.append((part, slice(at, at + LANES)))
    copies = []
    first = 0
    for number, size in enumerate(pieces):
        for q in range(first, first + size):
            part, mine = spans[q]
            y0_ref, dx_ref, q_ref, ls_ref = blocks[4 * part : 4 * part + 4]
            lanes = slice(q * LANES, (q + 1) * LANES)
            full = slice(start + q * LANES, start + (q + 1) * LANES)
            inter = dot(c, enter[:, lanes])
            y_ref[:, lanes] = (y0_ref[:, mine] + ls_ref[:, mine].astype(f32) * inter).astype(bf16)
            one = pad.at[q]
            one[0:rows, :] = dx_ref[:, mine] + q_ref[:, mine].astype(f32) * dot(b, grad[:, lanes])
            one[rows : rows + HALO, :] = edge[:, lanes].astype(f32)[0:HALO]
            x = x_ref[:, full].astype(f32)
            total = None
            sums = []
            for k, weight in enumerate(tap_rows(wx_ref, full)):
                shifted = one[taps - 1 - k : taps - 1 - k + rows, :]
                term = weight * shifted
                total = term if total is None else total + term
                sums.append(jnp.sum(shifted * x, axis=0, keepdims=True))
            gx_ref[:, lanes] = total.astype(bf16)
            sums = jnp.concatenate(sums + [jnp.zeros((8 - taps, LANES), f32)], axis=0)
            taps_ref[:, full] = sums
        lanes = slice(first * LANES, (first + size) * LANES)
        full = slice(start + first * LANES, start + (first + size) * LANES)
        for i, (made, out) in enumerate(((y_ref, y_hbm), (gx_ref, gx_hbm))):
            copy = pltpu.make_async_copy(made.at[:, lanes], out.at[:, full], sems.at[number, i])
            copy.start()
            copies.append(copy)
        first += size
    for copy in copies:
        copy.wait()


def pack_kernel(own_ref, small_ref, small_dp, small_out, head_ref):
    rows, bcw = own_ref.shape
    small = small_ref[...] + small_dp[...]
    small_out[...] = small
    head_ref[0:rows, :] = own_ref[...].astype(bf16)
    sums = small[:, :bcw]
    head_ref[rows:, :] = jnp.concatenate([sums, jnp.zeros_like(sums)], axis=0).astype(bf16)


def merge_kernel(heads, *refs):
    sums_ref, sums_dp, small_ref, own_ref = refs[:4]
    others, (full_ref, out_ref, send_ref) = refs[4 : 3 + heads], refs[3 + heads :]
    rows, bc = own_ref.shape
    half = sums_ref.shape[1] // 2
    full = own_ref[...]
    total = sums_ref[...] + sums_dp[...]
    taps_bc = small_ref[:, :bc]
    for ref in others:
        block = ref[...].astype(f32)
        full = full + block[:rows]
        taps_bc = taps_bc + block[rows : rows + 8]
    full_ref[...] = full
    send_ref[0:4, 0:half] = total[0:4, :half]
    send_ref[4:8, 0:half] = total[0:4, half:]
    send_ref[0:4, half : half + bc] = taps_bc[0:4]
    send_ref[4:8, half : half + bc] = full[0:4]
    send_ref[:, half + bc :] = small_ref[:, bc:]
    out_ref[...] = send_ref[...].astype(bf16)


def conv_bc_kernel(full_ref, wbc_ref, _, out_ref, pad):
    taps = wbc_ref.shape[0]
    rows, bcw = full_ref.shape
    for half in range(2):
        lanes = slice(half * bcw // 2, (half + 1) * bcw // 2)
        one = pad.at[half]
        one[0:rows, :] = full_ref[:, lanes]
        one[rows:, :] = jnp.zeros((HALO, bcw // 2), f32)
        out = None
        for k, weight in enumerate(tap_rows(wbc_ref, lanes)):
            term = weight * one[taps - 1 - k : taps - 1 - k + rows, :]
            out = term if out is None else out + term
        out_ref[:, lanes] = out


def last_kernel(count, norm_tokens, norm_skip, *refs):
    place_ref, sums_ref, conv_ref, wbc_ref = refs[:4]
    parts = refs[4 : 3 + count]
    gbc_ref, tx_ref, tbc_ref, skip_ref = refs[3 + count :]
    taps, bc = wbc_ref.shape
    rows = conv_ref.shape[0]
    half = tx_ref.shape[1] // 2
    total = sums_ref[...].astype(f32)
    edge = jnp.zeros((4, bc), f32)
    for hop, ref in enumerate(parts):
        block = ref[...].astype(f32)
        total = total + block
        if hop == count - 2:
            edge = jnp.where(place_ref[0] < count - 1, block[4:8, half : half + bc], 0.0)
    tx_ref[:, :half] = total[0:taps, 0:half] * norm_tokens
    tx_ref[:, half:] = total[4 : 4 + taps, 0:half] * norm_tokens
    tbc_ref[...] = total[0:taps, half : half + bc] * norm_tokens
    skip_ref[...] = total[0:1, half + bc : half + bc + skip_ref.shape[1]] * norm_skip
    gbc_ref[0 : rows - ROWS16, :] = conv_ref[0 : rows - ROWS16, :].astype(bf16)
    row = lax.broadcasted_iota(jnp.int32, (ROWS16, bc), 0)
    end = conv_ref[rows - ROWS16 :, :]
    for k in range(taps - 1):
        for j in range(taps - 1 - k):
            at = ROWS16 - (taps - 1 - k) + j
            end = end + jnp.where(row == at, wbc_ref[k : k + 1, :] * edge[j : j + 1], 0.0)
    gbc_ref[rows - ROWS16 :, :] = end.astype(bf16)


COST_US = {
    "tails": 0.9,
    "early_load": 1.0,
    "load": 1.6,
    "first_state": 1.4,
    "middle_state": 1.5,
    "end_state": 1.1,
    "inside_block": 2.7,
    "finish": 2.4,
    "finish_bc": 0.6,
}
BYTES_PER_US = 3_500_000


def call(kernel, name, ins, outs, scratch=(), grid=(1,), kept=()):
    def spec(item):
        if not isinstance(item, tuple):
            whole = item.shape
            return pl.BlockSpec(whole, lambda *_: (0,) * len(whole))
        if item[1] == "smem":
            return pl.BlockSpec(memory_space=pltpu.SMEM)
        if item[1] == "any":
            return pl.BlockSpec(memory_space=pl.ANY)
        if item[1] == "hbm":
            return pl.BlockSpec(memory_space=pltpu.HBM)
        return pl.BlockSpec(item[1], item[2])

    def array(item):
        return item[0] if isinstance(item, tuple) else item

    return pl.pallas_call(
        kernel,
        grid=grid,
        in_specs=[spec(i) for i in ins],
        out_specs=[spec(o) for o in outs],
        out_shape=[array(o) for o in outs],
        scratch_shapes=list(scratch),
        compiler_params=pltpu.CompilerParams(vmem_limit_bytes=VMEM_LIMIT),
        cost_estimate=pl.CostEstimate(
            flops=0, bytes_accessed=int(COST_US.get(name, 0.1) * BYTES_PER_US), transcendentals=0
        ),
        input_output_aliases=dict(kept),
        name=name,
    )(*[array(i) for i in ins])


def chain_routes(count, hop):
    return [(hop, hop + 1), (count - 1 - hop, count - 2 - hop)]


def shape(s, d=f32):
    return jax.ShapeDtypeStruct(s, d)


def local(x_input, bc_input, decays, conv_x, conv_bc, skip_gain, grad_out):
    x, bc, dec, g = x_input[0], bc_input[0], decays[0], grad_out[0]
    rows, inner = x.shape
    taps = conv_x.shape[0]
    heads = dec.shape[0]
    head_dim = inner // heads
    bcw = bc.shape[1]
    state = bcw // 2
    scale = state ** (-0.5)
    count = lax.axis_size("seq")
    head_count = lax.axis_size("head")
    dp_count = lax.axis_size("dp")
    assert rows == BLOCK_LEN and 2 * head_dim == LANES and taps == 4
    assert count % 2 == 0 and count > 2 and dp_count == 2
    width = inner // 2
    chunks = (0, 1)
    block = 640 if width % 640 == 0 else LANES
    per = width // block
    pairs = width // LANES
    split = (pairs - pairs // 2, pairs // 2)
    place = lax.axis_index("seq").astype(jnp.int32).reshape(1)
    where_am_i = (place, "smem")

    def vmem(s, d=f32):
        return pltpu.VMEM(s, d)

    def in_hbm(a):
        return (pltpu.with_memory_space_constraint(a, pltpu.HBM), "hbm")

    tails = call(
        tails_kernel,
        "tails",
        [in_hbm(x), in_hbm(bc)],
        [shape((HALO, inner + bcw), bf16)],
        [vmem((ROWS16, inner), bf16), vmem((ROWS16, bcw), bf16), pltpu.SemaphoreType.DMA((2,))],
    )[0]
    halo = lax.ppermute(tails, "seq", [(i, i + 1) for i in range(count - 1)])
    x_in, g_in = x, g
    sources = [bc, dec, conv_x, conv_bc]
    xa, ga, bc, dec, conv_x, conv_bc = call(
        functools.partial(early_load_kernel, count),
        "early_load",
        [where_am_i, in_hbm(x), in_hbm(g)] + [in_hbm(a) for a in sources] + [(tails, "any")],
        [shape((rows, width), bf16), shape((rows, width), bf16)]
        + [shape(a.shape, a.dtype) for a in sources],
        [pltpu.SemaphoreType.DMA((len(sources) + 2,))],
    )

    def padded(blocks, length=rows):
        return vmem((blocks, length + HALO, LANES))

    state_scratch = [
        padded(pairs),
        vmem((heads, rows)),
        vmem((heads, rows)),
        vmem((rows, width), bf16),
        vmem((rows, width), bf16),
    ]
    uv, lg16, cum, mapped = call(
        functools.partial(first_state_kernel, count, width, scale),
        "first_state",
        [where_am_i, dec, xa, ga, conv_x, bc, conv_bc],
        [
            shape((state, width)),
            shape((ROWS16, width), bf16),
            shape((heads, rows)),
            shape((rows, bcw), bf16),
        ],
        state_scratch + [padded(2)],
    )
    pay, mapped = call(
        functools.partial(fix_kernel, count),
        "fix_first_rows",
        [where_am_i, uv, lg16, halo, mapped, bc, conv_bc],
        [shape((state, width), bf16), shape((rows, bcw), bf16)],
        [padded(2, ROWS16)],
    )

    def state_call(kernel, name, c, after, outs):
        start = c * width
        return call(
            functools.partial(kernel, count, start, start // head_dim, scale),
            name,
            [where_am_i, dec, x, g, halo, conv_x, cum, mapped, (after, "any")],
            outs,
            state_scratch,
        )

    def middle_state(c, after):
        outs = [shape((state, width)), shape((state, width)), shape((8, width))]
        states[c] = state_call(middle_state_kernel, "middle_state", c, after, outs)
        return states[c][0]

    def end_state(c, after):
        outs = [shape((state, width), bf16)]
        return state_call(end_state_kernel, "end_state", c, after, outs)[0]

    states = [None, None]
    received = [[], []]

    def hop_on(c, message):
        routes = chain_routes(count, len(received[c]))
        received[c].append(lax.ppermute(message, "seq", routes))

    def message(c, after):
        hop = len(received[c])
        return call(
            functools.partial(message_kernel, hop),
            "message",
            [where_am_i, *states[c], received[c][-1], (after, "any")],
            [shape((state, width), bf16)],
        )[0]

    parts = [[], []]
    carried = []
    edges = []
    inside_last = []

    def inside(number, after):
        c, p = divmod(number, 2)
        first, last = number == 0, number == 3
        start = c * width + sum(split[:p]) * LANES
        span = split[p] * LANES
        ins = [x, g, halo, conv_x, dec, cum, mapped, (skip_gain, "smem"), (after, "any")]
        if not first:
            ins += carried
        outs = [
            shape((rows, span)),
            shape((rows, span)),
            shape((rows, span), bf16),
            shape((rows, span), bf16),
            shape((rows, span), bf16),
            shape((rows, span), bf16),
            shape((rows, rows)),
            shape((8, LANES)),
        ]
        if last:
            outs += [shape((rows, bcw))]
        made = call(
            functools.partial(intra_kernel, first, last, start, split[p], head_dim, scale),
            "inside_block",
            ins,
            outs,
            [padded(split[p]), vmem((rows, rows)), vmem((heads, rows))],
        )
        parts[c].append(made[:6])
        carried[:] = made[6:8]
        if last:
            inside_last[:] = [made[8], made[7]]
        return made[0]

    def last_message(c, after):
        u, v, tot = states[c]
        seen = edges[0] if edges else after
        ins = [where_am_i, u, v, tot, mapped, (after, "any"), (seen, "any")]
        for made in parts[c]:
            ins += made[1:3]
        return call(
            functools.partial(last_message_kernel, count, len(parts[c])),
            "last_message",
            ins + received[c],
            [shape((state + ROWS16, width), bf16), shape((ROWS16, width), bf16)],
        )

    def edge_on(block):
        return lax.ppermute(block, "seq", [(i + 1, i) for i in range(1, count - 1)])

    hop_on(0, pay)
    x, g = call(
        load_kernel,
        "load",
        [in_hbm(x_in), in_hbm(g_in), (pay, "any")],
        [shape(x_in.shape, bf16), shape(g_in.shape, bf16)],
        [pltpu.SemaphoreType.DMA((2,))],
    )
    after = middle_state(0, pay)
    after = inside(0, after)
    after = end_state(1, after)
    hop_on(1, after)
    after = middle_state(1, after)
    for hop in range(1, count - 1):
        for c in chunks:
            if hop < count - 2:
                after = message(c, after)
                hop_on(c, after)
            else:
                after, block = last_message(c, after)
                hop_on(c, after)
                edges.append(edge_on(block))
            if hop == 1 and c == 0:
                after = inside(1, after)
            if hop == count - 2 and c == 0:
                after = inside(2, after)
                after = inside(3, after)
    dbc, gsum = inside_last

    def finish_bc(c, after):
        last = c == 1
        ins = [where_am_i, mapped, dbc, (after, "any"), (edges[c], "any")]
        for made in parts[c]:
            ins += made[4:6]
        ins += received[c]
        outs = [shape((rows, bcw))]
        scratch = []
        if last:
            ins += [bc, halo, conv_bc, gsum]
            outs += [shape((8, bcw + LANES))]
            scratch = [padded(2)]
        kernel = functools.partial(finish_bc_kernel, count, last, len(parts[c]))
        return call(kernel, "finish_bc", ins, outs, scratch)

    def finish(c, after, kept_y, before):
        start = c * width
        pieces = (4, 4, 2) if pairs == 10 else (pairs - 1, 1)
        ins = [where_am_i, x, conv_x, mapped, edges[c], (after, "any")]
        for made in parts[c]:
            ins += made[:4]
        ins += received[c]
        kept = ()
        if c:
            kept = ((len(ins) + 1, 0), (len(ins) + 2, 1))
            ins += [before, (kept_y[0], "hbm"), (kept_y[1], "hbm")]
        return call(
            functools.partial(finish_kernel, count, start, len(parts[c]), pieces),
            "finish",
            ins,
            [
                (shape((rows, inner), bf16), "hbm"),
                (shape((rows, inner), bf16), "hbm"),
                shape((8, start + width)),
            ],
            [
                vmem((state, width), bf16),
                vmem((state, width), bf16),
                vmem((ROWS16, width), bf16),
                padded(pairs),
                vmem((rows, width), bf16),
                vmem((rows, width), bf16),
                pltpu.SemaphoreType.DMA((len(pieces), 2)),
            ],
            kept=kept,
        )

    y, gx, before = finish(0, after, None, None)
    dbc = finish_bc(0, before)[0]
    own, small = finish_bc(1, dbc)

    swap = [(0, 1), (1, 0)]
    small, to_heads = call(
        pack_kernel,
        "pack",
        [own, small, lax.ppermute(small, "dp", swap)],
        [shape(small.shape), shape((rows + ROWS16, bcw), bf16)],
    )
    others = []
    for k in range(1, head_count):
        turn = [(i, (i + k) % head_count) for i in range(head_count)]
        others.append(lax.ppermute(to_heads, "head", turn))
    y, gx, sums = finish(1, to_heads, (y, gx), before)
    sums_dp = lax.ppermute(sums, "dp", swap)
    send_width = inner // 2 + bcw + LANES
    full, to_seq = call(
        functools.partial(merge_kernel, head_count),
        "merge",
        [sums, sums_dp, small, own] + others,
        [shape((rows, bcw)), shape((8, send_width), bf16)],
        [vmem((8, send_width))],
    )
    from_seq = [
        lax.ppermute(to_seq, "seq", [(i, (i + k) % count) for i in range(count)])
        for k in range(1, count)
    ]
    token_count = rows * count * dp_count
    norm_tokens = float(token_count) ** (-0.5)
    norm_skip = float(token_count * head_dim) ** (-0.5)
    conv = call(
        conv_bc_kernel,
        "conv_bc",
        [full, conv_bc, (to_seq, "any")],
        [shape((rows, bcw))],
        [padded(2)],
    )[0]
    gbc, tx, tbc, skip = call(
        functools.partial(last_kernel, count, norm_tokens, norm_skip),
        "last",
        [where_am_i, to_seq, conv, conv_bc] + from_seq,
        [
            shape((rows, bcw), bf16),
            shape((taps, inner)),
            shape((taps, bcw)),
            shape((1, heads)),
        ],
    )
    return y[None], gx[None], gbc[None], tx, tbc, skip.reshape(heads)


def solution(mesh):
    return jax.shard_map(
        local,
        mesh=mesh,
        in_specs=(
            P(("groups", "dp"), "seq", "head"),
            P(("groups", "dp"), "seq", None),
            P(("groups", "dp"), "head", "seq"),
            P(None, "head"),
            P(),
            P("head"),
            P(("groups", "dp"), "seq", "head"),
        ),
        out_specs=(
            P(("groups", "dp"), "seq", "head"),
            P(("groups", "dp"), "seq", "head"),
            P(("groups", "dp"), "seq", None),
            P("groups", "head"),
            P("groups", None),
            P(("groups", "head")),
        ),
        check_vma=False,
    )
```

time: 79.6 us -> 68.3 us (0.86)
  Pallas kernels: 31.3 us -> 25.7 us
  local copies, waits for them, and re-layouts: 4.46 us -> 0.63 us
  waiting for transfers between devices: 19.9 us -> 18.4 us
    ppermute x4 -> x3, waiting for transfers between devices: 17.5 us -> 1.17 us  [the longest x1 1.16 us: local(): lax.ppermute(small, 'dp', swap)]
    ppermute x6, waiting for transfers between devices: 0.02 us -> 10.7 us  [hop_on(): received[c].append(lax.ppermute(message, 'seq', routes))]
    pallas_call x19 -> x24, Pallas kernels: 31.3 us -> 25.7 us  [call(): pl.pallas_call(kernel, grid=grid, in_specs=[spec(i) for i in ins], out_sp...]
    unnamed x22 -> x2, local copies, waits for them, and re-layouts: 4.46 us -> 0.63 us
    ppermute x3, waiting for transfers between devices: 2.39 us -> 4.69 us  [local(): lax.ppermute(to_seq, 'seq', [(i, (i + k) % count) for i in range(count)])]
    ppermute x4 -> x3, starting transfers between devices: 3.42 us -> 1.4 us  [the longest x2 1.33 us: edge_on(): return lax.ppermute(block, 'seq', [(i + 1, i) for i in range(1, count - 1)])]
    ppermute x3, starting transfers between devices: 3.86 us -> 5.86 us  [local(): lax.ppermute(to_seq, 'seq', [(i, (i + k) % count) for i in range(count)])]
    ppermute x1, waiting for transfers between devices: 0.01 us -> 1.26 us  [local(): sums_dp = lax.ppermute(sums, 'dp', swap)]
  transfers between devices with their start and end apart: 16 -> 15, of which waited for: 5 -> 9; matrix products, arithmetic and copies ran while one was open for 0% -> 0% of each run, Pallas kernels for 32% -> 34%
where the time goes in v3:
time: 68.3 us; the launch traced here: 68 us
  Pallas kernels  25.7 us (38%)
  starting transfers between devices  22.4 us (33%)
  waiting for transfers between devices  18.4 us (27%)
  between operations  0.9 us (1%)
    pallas_call x24, Pallas kernels, call(): pl.pallas_call(kernel, grid=grid, in_specs=[spec(i) for i in ins], out_sp...  25.7 us
    ppermute x6, waiting for transfers between devices, hop_on(): received[c].append(lax.ppermute(message, 'seq', routes))  10.7 us
    ppermute x6, starting transfers between devices, hop_on(): received[c].append(lax.ppermute(message, 'seq', routes))  8.6 us
    ppermute x3, starting transfers between devices, local(): lax.ppermute(to_seq, 'seq', [(i, (i + k) % count) for i in range(count)])  5.86 us
    ppermute x1, starting transfers between devices, local(): halo = lax.ppermute(tails, 'seq', [(i, i + 1) for i in range(count - 1)])  4.93 us
    ppermute x3, waiting for transfers between devices, local(): lax.ppermute(to_seq, 'seq', [(i, (i + k) % count) for i in range(count)])  4.69 us
    ppermute x1, starting transfers between devices, local(): others.append(lax.ppermute(to_heads, 'head', turn))  1.55 us
  transfers between devices with their start and end apart: 15, of which 9 were waited for; matrix products, arithmetic and copies ran while one was open for 0% of the time, Pallas kernels for 34%

profile of v3, /device:TPU:0, one launch (start us, length us, event | category | flops | bytes accessed | tf_op | source)
XLA Modules:
  0.0 68.0 jit_solution(377893077064644233)
XLA Ops:
  0.6 0.9 %tails.1.refs_7_ = bf16[8,2816]{1,0:T(8,128)(2,1)S(1)} custom-call(bf16[256,2560]{1,0:T(8,128)(2,1)} %bitcast.9, bf16[256,256]{1,0:T(8,128)(2,1)} %bitcast.16), custom_call_target="tpu_custom_call" | custom-call | bytes 3150000 | tf_op jit(solution)/shard_map/tails/pallas_call | solution.py:619
  1.6 4.9 %collective-permute-start = (bf16[8,2816]{1,0:T(8,128)(2,1)S(1)}, bf16[8,2816]{1,0:T(8,128)(2,1)S(1)}, u32[]{:S(2)}, u32[]{:S(2)}) collective-permute-start(bf16[8,2816]{1,0:T(8,128)(2,1)S(1)} %tails.1.refs_7_), channel_id=1, source_target_pairs={{0,4},{4,8},{8,12},{1,5},{5,9},{9,13},{2,6},{6,10},{10,14},{3,7},{... | collective-permute-start | bytes 135176 | tf_op jit(solution)/shard_map/ppermute | solution.py:679
  6.5 1.3 %early_load.1 = (bf16[256,1280]{1,0:T(8,128)(2,1)S(1)}, bf16[256,1280]{1,0:T(8,128)(2,1)S(1)}, bf16[256,256]{1,0:T(8,128)(2,1)S(1)}, f32[40,256]{1,0:T(8,128)S(1...) custom-call(s32[1]{0:T(128)} %bitcast.refs_0_.place_ref, bf16[256,2560]{1,0:T(8,128)(2,1)} %bitcast.10, ...), custom_call_target="tpu_custom_call" | custom-call | bytes 3500000 | tf_op jit(solution)/shard_map/early_load/pallas_call | solution.py:619
  7.8 1.4 %first_state.1 = (f32[128,1280]{1,0:T(8,128)S(1)}, bf16[16,1280]{1,0:T(8,128)(2,1)S(1)}, f32[40,256]{1,0:T(8,128)S(1)}, bf16[256,256]{1,0:T(8,128)(2,1)S(1)}) custom-call(s32[1]{0:T(128)} %bitcast.refs_0_.place_ref, f32[40,256]{1,0:T(8,128)S(1)} %get-tuple-element.78.refs_1_.refs_4_, bf16[256,1280]{1,0:T(8,128)(2,1)S(1)} %get-tuple-element.79.refs_2_, ...), custom_call_target="tpu_custom_call" | custom-call | bytes 4900000 | tf_op jit(solution)/shard_map/first_state/pallas_call | solution.py:619
  9.3 3.2 %collective-permute-start.2 = (bf16[128,1280]{1,0:T(8,128)(2,1)S(1)}, bf16[128,1280]{1,0:T(8,128)(2,1)S(1)}, u32[]{:S(2)}, u32[]{:S(2)}) collective-permute-start(bf16[128,1280]{1,0:T(8,128)(2,1)S(1)} %get-tuple-element.87._.refs_8_), channel_id=1, source_target_pairs={{0,4},{12,8},{1,5},{13,9},{2,6},{14,10},{3,7},{15,11},{16,20},{28,... | collective-permute-start | bytes 983048 | tf_op jit(solution)/shard_map/ppermute | solution.py:745
  12.5 1.7 %load.1 = (bf16[256,2560]{1,0:T(8,128)(2,1)S(1)}, bf16[256,2560]{1,0:T(8,128)(2,1)S(1)}) custom-call(bf16[256,2560]{1,0:T(8,128)(2,1)} %bitcast.11, bf16[256,2560]{1,0:T(8,128)(2,1)} %bitcast.13, bf16[128,1280]{1,0:T(8,128)(2,1)S(1)} %get-tuple-element.87._.refs_8_), custom_call_target="tpu_custom_call" | custom-call | bytes 5600000 | tf_op jit(solution)/shard_map/load/pallas_call | solution.py:619
  14.9 2.7 %inside_block.4 = (f32[256,640]{1,0:T(8,128)S(1)}, f32[256,640]{1,0:T(8,128)S(1)}, bf16[256,640]{1,0:T(8,128)(2,1)S(1)}, bf16[256,640]{1,0:T(8,128)(2,1)S(1)}, b...) custom-call(bf16[256,2560]{1,0:T(8,128)(2,1)S(1)} %get-tuple-element., ...), custom_call_target="tpu_custom_call" | custom-call | bytes 9450000 | tf_op jit(solution)/shard_map/inside_block/pallas_call | solution.py:619
  17.6 1.1 %end_state.1.refs_8_ = bf16[128,1280]{1,0:T(8,128)(2,1)S(1)} custom-call(s32[1]{0:T(128)} %bitcast.refs_0_.place_ref, f32[40,256]{1,0:T(8,128)S(1)} %get-tuple-element.78.refs_1_.refs_4_, bf16[256,2560]{1,0:T(8,128)(2,1)S(1)} %get-tuple-element.88.refs_2_.refs_0_.refs_1_, bf16[256,2560]{1,0:T(8,128)(2,1)S(1)} %get-tuple-element.90.refs_3_.refs_1_, ...), custom_call_target="tpu_custom_call" | custom-call | bytes 3850000 | tf_op jit(solution)/shard_map/end_state/pallas_call | solution.py:619
  18.8 1.3 %collective-permute-start.1 = (bf16[128,1280]{1,0:T(8,128)(2,1)S(1)}, bf16[128,1280]{1,0:T(8,128)(2,1)S(1)}, u32[]{:S(2)}, u32[]{:S(2)}) collective-permute-start(bf16[128,1280]{1,0:T(8,128)(2,1)S(1)} %end_state.1.refs_8_), channel_id=1, source_target_pairs={{0,4},{12,8},{1,5},{13,9},{2,6},{14,10},{3,7},{15,11},{16,20},{28,... | collective-permute-start | bytes 983048 | tf_op jit(solution)/shard_map/ppermute | solution.py:745
  20.9 2.8 %inside_block.5 = (f32[256,640]{1,0:T(8,128)S(1)}, f32[256,640]{1,0:T(8,128)S(1)}, bf16[256,640]{1,0:T(8,128)(2,1)S(1)}, bf16[256,640]{1,0:T(8,128)(2,1)S(1)}, b...) custom-call(bf16[256,2560]{1,0:T(8,128)(2,1)S(1)} %get-tuple-element., ...), custom_call_target="tpu_custom_call" | custom-call | bytes 9450000 | tf_op jit(solution)/shard_map/inside_block/pallas_call | solution.py:619
  23.7 2.2 %collective-permute-done.1.came_ref.refs_11_.refs_9_.refs_14_ = bf16[128,1280]{1,0:T(8,128)(2,1)S(1)} collective-permute-done((bf16[128,1280]{1,0:T(8,128)(2,1)S(1)}, bf16[128,1280]{1,0:T(8,128)(2,1)S(1)}, u32[]{:S(2)}, u32[]{:S(2)}) %collective-permute-start.1) | collective-permute-done | bytes 327712 | tf_op jit(solution)/shard_map/ppermute | solution.py:745
  27.7 1.5 %collective-permute-start.7 = (bf16[144,1280]{1,0:T(8,128)(2,1)S(1)}, bf16[144,1280]{1,0:T(8,128)(2,1)S(1)}, u32[]{:S(2)}, u32[]{:S(2)}) collective-permute-start(bf16[144,1280]{1,0:T(8,128)(2,1)S(1)} %get-tuple-element.106.refs_8_), channel_id=1, source_target_pairs={{8,12},{4,0},{9,13},{5,1},{10,14},{6,2},{11,15},{7,3},{24,28},{20,... | collective-permute-start | bytes 1105928 | tf_op jit(solution)/shard_map/ppermute | solution.py:745
  29.2 2.7 %inside_block.6 = (f32[256,640]{1,0:T(8,128)S(1)}, f32[256,640]{1,0:T(8,128)S(1)}, bf16[256,640]{1,0:T(8,128)(2,1)S(1)}, bf16[256,640]{1,0:T(8,128)(2,1)S(1)}, b...) custom-call(bf16[256,2560]{1,0:T(8,128)(2,1)S(1)} %get-tuple-element., ...), custom_call_target="tpu_custom_call" | custom-call | bytes 9450000 | tf_op jit(solution)/shard_map/inside_block/pallas_call | solution.py:619
  31.9 3.2 %inside_block.7 = (f32[256,640]{1,0:T(8,128)S(1)}, f32[256,640]{1,0:T(8,128)S(1)}, bf16[256,640]{1,0:T(8,128)(2,1)S(1)}, bf16[256,640]{1,0:T(8,128)(2,1)S(1)}, b...) custom-call(bf16[256,2560]{1,0:T(8,128)(2,1)S(1)} %get-tuple-element, ...), custom_call_target="tpu_custom_call" | custom-call | bytes 9450000 | tf_op jit(solution)/shard_map/inside_block/pallas_call | solution.py:619
  35.4 1.3 %collective-permute-start.8 = (bf16[144,1280]{1,0:T(8,128)(2,1)S(1)}, bf16[144,1280]{1,0:T(8,128)(2,1)S(1)}, u32[]{:S(2)}, u32[]{:S(2)}) collective-permute-start(bf16[144,1280]{1,0:T(8,128)(2,1)S(1)} %get-tuple-element.120.refs_5_), channel_id=1, source_target_pairs={{8,12},{4,0},{9,13},{5,1},{10,14},{6,2},{11,15},{7,3},{24,28},{20,... | collective-permute-start | bytes 1105928 | tf_op jit(solution)/shard_map/ppermute | solution.py:745
  37.4 3.6 %collective-permute-done.7.refs_16_.refs_11_ = bf16[144,1280]{1,0:T(8,128)(2,1)S(1)} collective-permute-done((bf16[144,1280]{1,0:T(8,128)(2,1)S(1)}, bf16[144,1280]{1,0:T(8,128)(2,1)S(1)}, u32[]{:S(2)}, u32[]{:S(2)}) %collective-permute-start.7) | collective-permute-done | bytes 368672 | tf_op jit(solution)/shard_map/ppermute | solution.py:745
  41.0 2.4 %finish.2 = (bf16[256,2560]{1,0:T(8,128)(2,1)}, bf16[256,2560]{1,0:T(8,128)(2,1)}, f32[8,1280]{1,0:T(8,128)S(1)}) custom-call(s32[1]{0:T(128)} %bitcast.refs_0_.place_ref, bf16[256,2560]{1,0:T(8,128)(2,1)S(1)} %get-tuple-element.88.refs_2_.refs_0_.refs_1_, f32[4,2560]{1,0:T(4,128)S(1)} %get-tuple-element.81.refs_4_.refs_5_.refs_3_.refs_2_, ...), custom_call_target="tpu_custom_call" | custom-call | bytes 8400000 | tf_op jit(solution)/shard_map/finish/pallas_call | solution.py:619
  43.9 4.9 %collective-permute-done.8.refs_11_.refs_16_ = bf16[144,1280]{1,0:T(8,128)(2,1)S(1)} collective-permute-done((bf16[144,1280]{1,0:T(8,128)(2,1)S(1)}, bf16[144,1280]{1,0:T(8,128)(2,1)S(1)}, u32[]{:S(2)}, u32[]{:S(2)}) %collective-permute-start.8) | collective-permute-done | bytes 368672 | tf_op jit(solution)/shard_map/ppermute | solution.py:745
  49.6 1.2 %collective-permute-done.9.small_dp = f32[8,384]{1,0:T(8,128)S(1)} collective-permute-done((f32[8,384]{1,0:T(8,128)S(1)}, f32[8,384]{1,0:T(8,128)S(1)}, u32[]{:S(2)}, u32[]{:S(2)}) %collective-permute-start.9) | collective-permute-done | bytes 12320 | tf_op jit(solution)/shard_map/ppermute | solution.py:894
  50.8 1.5 %collective-permute-start.11 = (bf16[272,256]{1,0:T(8,128)(2,1)S(1)}, bf16[272,256]{1,0:T(8,128)(2,1)S(1)}, u32[]{:S(2)}, u32[]{:S(2)}) collective-permute-start(bf16[272,256]{1,0:T(8,128)(2,1)S(1)} %get-tuple-element.135.refs_5_), channel_id=1, source_target_pairs={{0,2},{2,0},{1,3},{3,1},{4,6},{6,4},{5,7},{7,5},{8,10},{10,8},{9,1... | collective-permute-start | bytes 417800 | tf_op jit(solution)/shard_map/ppermute | solution.py:900
  52.3 2.4 %finish.3 = (bf16[256,2560]{1,0:T(8,128)(2,1)}, bf16[256,2560]{1,0:T(8,128)(2,1)}, f32[8,2560]{1,0:T(8,128)S(1)}) custom-call(s32[1]{0:T(128)} %bitcast.refs_0_.place_ref, bf16[256,2560]{1,0:T(8,128)(2,1)S(1)} %get-tuple-element.88.refs_2_.refs_0_.refs_1_, ...), custom_call_target="tpu_custom_call", output_to_operand_aliasing={{0}: (18, {}), {1}: (19, {})} | custom-call | bytes 8400000 | tf_op jit(solution)/shard_map/finish/pallas_call | solution.py:619
  54.7 1.3 %collective-permute-done.10.refs_1_ = f32[8,2560]{1,0:T(8,128)S(1)} collective-permute-done((f32[8,2560]{1,0:T(8,128)S(1)}, f32[8,2560]{1,0:T(8,128)S(1)}, u32[]{:S(2)}, u32[]{:S(2)}) %collective-permute-start.10) | collective-permute-done | bytes 81952 | tf_op jit(solution)/shard_map/ppermute | solution.py:902
  56.6 5.0 %collective-permute-start.14 = (bf16[8,1664]{1,0:T(8,128)(2,1)S(1)}, bf16[8,1664]{1,0:T(8,128)(2,1)S(1)}, u32[]{:S(2)}, u32[]{:S(2)}) collective-permute-start(bf16[8,1664]{1,0:T(8,128)(2,1)S(1)} %get-tuple-element.144._.refs_1_), channel_id=1, source_target_pairs={{0,12},{4,0},{8,4},{12,8},{1,13},{5,1},{9,5},{13,9},{2,14},{6,2},{... | collective-permute-start | bytes 79880 | tf_op jit(solution)/shard_map/ppermute | solution.py:912
  63.2 3.2 %collective-permute-done.13.refs_5_ = bf16[8,1664]{1,0:T(8,128)(2,1)S(1)} collective-permute-done((bf16[8,1664]{1,0:T(8,128)(2,1)S(1)}, bf16[8,1664]{1,0:T(8,128)(2,1)S(1)}, u32[]{:S(2)}, u32[]{:S(2)}) %collective-permute-start.13) | collective-permute-done | bytes 26656 | tf_op jit(solution)/shard_map/ppermute | solution.py:912
  (32 shorter events, 9.5 us)
Async XLA Ops:
  1.6 7.7 %collective-permute-start = (bf16[8,2816]{1,0:T(8,128)(2,1)S(1)}, bf16[8,2816]{1,0:T(8,128)(2,1)S(1)}, u32[]{:S(2)}, u32[]{:S(2)}) collective-permute-start(bf16[8,2816]{1,0:T(8,128)(2,1)S(1)} %tails.1.refs_7_), channel_id=1, source_target_pairs={{0,4},{4,8},{8,12},{1,5},{5,9},{9,13},{2,6},{6,10},{10,14},{3,7},{... | collective-permute-start | bytes 135176 | tf_op jit(solution)/shard_map/ppermute | solution.py:679
  9.3 10.8 %collective-permute-start.2 = (bf16[128,1280]{1,0:T(8,128)(2,1)S(1)}, bf16[128,1280]{1,0:T(8,128)(2,1)S(1)}, u32[]{:S(2)}, u32[]{:S(2)}) collective-permute-start(bf16[128,1280]{1,0:T(8,128)(2,1)S(1)} %get-tuple-element.87._.refs_8_), channel_id=1, source_target_pairs={{0,4},{12,8},{1,5},{13,9},{2,6},{14,10},{3,7},{15,11},{16,20},{28,... | collective-permute-start | bytes 983048 | tf_op jit(solution)/shard_map/ppermute | solution.py:745
  14.2 0.7 copy-start
  18.8 7.1 %collective-permute-start.1 = (bf16[128,1280]{1,0:T(8,128)(2,1)S(1)}, bf16[128,1280]{1,0:T(8,128)(2,1)S(1)}, u32[]{:S(2)}, u32[]{:S(2)}) collective-permute-start(bf16[128,1280]{1,0:T(8,128)(2,1)S(1)} %end_state.1.refs_8_), channel_id=1, source_target_pairs={{0,4},{12,8},{1,5},{13,9},{2,6},{14,10},{3,7},{15,11},{16,20},{28,... | collective-permute-start | bytes 983048 | tf_op jit(solution)/shard_map/ppermute | solution.py:745
  20.3 6.4 %collective-permute-start.3 = (bf16[128,1280]{1,0:T(8,128)(2,1)S(1)}, bf16[128,1280]{1,0:T(8,128)(2,1)S(1)}, u32[]{:S(2)}, u32[]{:S(2)}) collective-permute-start(bf16[128,1280]{1,0:T(8,128)(2,1)S(1)} %message.2.refs_8_), channel_id=1, source_target_pairs={{4,8},{8,4},{5,9},{9,5},{6,10},{10,6},{7,11},{11,7},{20,24},{24,20... | collective-permute-start | bytes 983048 | tf_op jit(solution)/shard_map/ppermute | solution.py:745
  26.0 9.1 %collective-permute-start.5 = (bf16[128,1280]{1,0:T(8,128)(2,1)S(1)}, bf16[128,1280]{1,0:T(8,128)(2,1)S(1)}, u32[]{:S(2)}, u32[]{:S(2)}) collective-permute-start(bf16[128,1280]{1,0:T(8,128)(2,1)S(1)} %message.3.refs_5_.refs_6_), channel_id=1, source_target_pairs={{4,8},{8,4},{5,9},{9,5},{6,10},{10,6},{7,11},{11,7},{20,24},{24,20... | collective-permute-start | bytes 983048 | tf_op jit(solution)/shard_map/ppermute | solution.py:745
  27.0 8.0 %collective-permute-start.4 = (bf16[16,1280]{1,0:T(8,128)(2,1)S(1)}, bf16[16,1280]{1,0:T(8,128)(2,1)S(1)}, u32[]{:S(2)}, u32[]{:S(2)}) collective-permute-start(bf16[16,1280]{1,0:T(8,128)(2,1)S(1)} %get-tuple-element.113), channel_id=1, source_target_pairs={{8,4},{12,8},{9,5},{13,9},{10,6},{14,10},{11,7},{15,11},{24,20},{2... | collective-permute-start | bytes 122888 | tf_op jit(solution)/shard_map/ppermute | solution.py:808
  27.7 13.3 %collective-permute-start.7 = (bf16[144,1280]{1,0:T(8,128)(2,1)S(1)}, bf16[144,1280]{1,0:T(8,128)(2,1)S(1)}, u32[]{:S(2)}, u32[]{:S(2)}) collective-permute-start(bf16[144,1280]{1,0:T(8,128)(2,1)S(1)} %get-tuple-element.106.refs_8_), channel_id=1, source_target_pairs={{8,12},{4,0},{9,13},{5,1},{10,14},{6,2},{11,15},{7,3},{24,28},{20,... | collective-permute-start | bytes 1105928 | tf_op jit(solution)/shard_map/ppermute | solution.py:745
  35.4 13.4 %collective-permute-start.8 = (bf16[144,1280]{1,0:T(8,128)(2,1)S(1)}, bf16[144,1280]{1,0:T(8,128)(2,1)S(1)}, u32[]{:S(2)}, u32[]{:S(2)}) collective-permute-start(bf16[144,1280]{1,0:T(8,128)(2,1)S(1)} %get-tuple-element.120.refs_5_), channel_id=1, source_target_pairs={{8,12},{4,0},{9,13},{5,1},{10,14},{6,2},{11,15},{7,3},{24,28},{20,... | collective-permute-start | bytes 1105928 | tf_op jit(solution)/shard_map/ppermute | solution.py:745
  36.7 7.2 %collective-permute-start.6 = (bf16[16,1280]{1,0:T(8,128)(2,1)S(1)}, bf16[16,1280]{1,0:T(8,128)(2,1)S(1)}, u32[]{:S(2)}, u32[]{:S(2)}) collective-permute-start(bf16[16,1280]{1,0:T(8,128)(2,1)S(1)} %get-tuple-element.118), channel_id=1, source_target_pairs={{8,4},{12,8},{9,5},{13,9},{10,6},{14,10},{11,7},{15,11},{24,20},{2... | collective-permute-start | bytes 122888 | tf_op jit(solution)/shard_map/ppermute | solution.py:808
  49.5 1.2 %collective-permute-start.9 = (f32[8,384]{1,0:T(8,128)S(1)}, f32[8,384]{1,0:T(8,128)S(1)}, u32[]{:S(2)}, u32[]{:S(2)}) collective-permute-start(f32[8,384]{1,0:T(8,128)S(1)} %get-tuple-element.134.small_ref), channel_id=1, source_target_pairs={{0,1},{1,0},{2,3},{3,2},{4,5},{5,4},{6,7},{7,6},{8,9},{9,8},{10,11... | collective-permute-start | bytes 36872 | tf_op jit(solution)/shard_map/ppermute | solution.py:894
  50.8 5.8 %collective-permute-start.11 = (bf16[272,256]{1,0:T(8,128)(2,1)S(1)}, bf16[272,256]{1,0:T(8,128)(2,1)S(1)}, u32[]{:S(2)}, u32[]{:S(2)}) collective-permute-start(bf16[272,256]{1,0:T(8,128)(2,1)S(1)} %get-tuple-element.135.refs_5_), channel_id=1, source_target_pairs={{0,2},{2,0},{1,3},{3,1},{4,6},{6,4},{5,7},{7,5},{8,10},{10,8},{9,1... | collective-permute-start | bytes 417800 | tf_op jit(solution)/shard_map/ppermute | solution.py:900
  54.7 1.3 %collective-permute-start.10 = (f32[8,2560]{1,0:T(8,128)S(1)}, f32[8,2560]{1,0:T(8,128)S(1)}, u32[]{:S(2)}, u32[]{:S(2)}) collective-permute-start(f32[8,2560]{1,0:T(8,128)S(1)} %get-tuple-element.142.refs_0_), channel_id=1, source_target_pairs={{0,1},{1,0},{2,3},{3,2},{4,5},{5,4},{6,7},{7,6},{8,9},{9,8},{10,11... | collective-permute-start | bytes 245768 | tf_op jit(solution)/shard_map/ppermute | solution.py:902
  56.6 6.6 %collective-permute-start.14 = (bf16[8,1664]{1,0:T(8,128)(2,1)S(1)}, bf16[8,1664]{1,0:T(8,128)(2,1)S(1)}, u32[]{:S(2)}, u32[]{:S(2)}) collective-permute-start(bf16[8,1664]{1,0:T(8,128)(2,1)S(1)} %get-tuple-element.144._.refs_1_), channel_id=1, source_target_pairs={{0,12},{4,0},{8,4},{12,8},{1,13},{5,1},{9,5},{13,9},{2,14},{6,2},{... | collective-permute-start | bytes 79880 | tf_op jit(solution)/shard_map/ppermute | solution.py:912
  61.6 4.7 %collective-permute-start.13 = (bf16[8,1664]{1,0:T(8,128)(2,1)S(1)}, bf16[8,1664]{1,0:T(8,128)(2,1)S(1)}, u32[]{:S(2)}, u32[]{:S(2)}) collective-permute-start(bf16[8,1664]{1,0:T(8,128)(2,1)S(1)} %get-tuple-element.144._.refs_1_), channel_id=1, source_target_pairs={{0,8},{4,12},{8,0},{12,4},{1,9},{5,13},{9,1},{13,5},{2,10},{6,14},... | collective-permute-start | bytes 79880 | tf_op jit(solution)/shard_map/ppermute | solution.py:912
  61.6 5.6 %collective-permute-start.12 = (bf16[8,1664]{1,0:T(8,128)(2,1)S(1)}, bf16[8,1664]{1,0:T(8,128)(2,1)S(1)}, u32[]{:S(2)}, u32[]{:S(2)}) collective-permute-start(bf16[8,1664]{1,0:T(8,128)(2,1)S(1)} %get-tuple-element.144._.refs_1_), channel_id=1, source_target_pairs={{0,4},{4,8},{8,12},{12,0},{1,5},{5,9},{9,13},{13,1},{2,6},{6,10},{... | collective-permute-start | bytes 79880 | tf_op jit(solution)/shard_map/ppermute | solution.py:912

commit v4 on v3

v4 whole, which is shorter than its diff:
```python
import functools

import jax
import jax.numpy as jnp
from jax import lax
from jax.experimental import pallas as pl
from jax.experimental.pallas import tpu as pltpu
from jax.sharding import PartitionSpec as P

BLOCK_LEN = 256
LANES = 128
HALO = 8
NEG = -1e30
f32 = jnp.float32
bf16 = jnp.bfloat16
HIGHEST = lax.Precision.HIGHEST
ROWS16 = 16
VMEM_LIMIT = 24 * 1024 * 1024


def dot(a, b, precision=None):
    return jnp.dot(a, b, preferred_element_type=f32, precision=precision)


def dot_nt(a, b):
    return lax.dot_general(a, b, (((1,), (1,)), ((), ())), preferred_element_type=f32)


def sigmoid(v):
    return 0.5 * jnp.tanh(0.5 * v) + 0.5


def conv_rows(pad_ref, weights, rows):
    first = HALO - len(weights) + 1
    total = None
    for k, weight in enumerate(weights):
        term = weight * pad_ref[first + k : first + k + rows, :]
        total = term if total is None else total + term
    return total


def tap_rows(ref, lanes):
    block = ref[:, lanes]
    return [block[k : k + 1] for k in range(block.shape[0])]


def silu_grad(pre):
    sg = sigmoid(pre)
    return sg * (1.0 + pre * (1.0 - sg))


def spread(row_a, row_b):
    half, rows = LANES // 2, row_a.shape[1]
    both = jnp.concatenate(
        [jnp.broadcast_to(row_a, (half, rows)), jnp.broadcast_to(row_b, (half, rows))], axis=0
    )
    return both.T


def column(row):
    return jnp.broadcast_to(row, (LANES, row.shape[1])).T


def running_sum(dec):
    rows = dec.shape[1]
    before = lax.broadcasted_iota(jnp.int32, (rows, rows), 0)
    after = lax.broadcasted_iota(jnp.int32, (rows, rows), 1)
    upper = (before <= after).astype(f32)
    return dot(jnp.log(dec), upper, HIGHEST)


def gain_of(dec):
    return jnp.sqrt((1.0 - dec) * (1.0 + dec))


def tail_of(cum):
    return jnp.exp(cum[:, -1:] - cum)


def put_padded(pad_ref, halo, block):
    pad_ref[0:HALO, :] = halo
    pad_ref[HALO : HALO + block.shape[0], :] = block.astype(f32)


def lane_blocks(width):
    return [slice(at, at + LANES) for at in range(0, width, LANES)]


def run_copies(copies):
    for copy in copies:
        copy.start()
    for copy in copies:
        copy.wait()


def early_load_kernel(count, *refs):
    place_ref, x_hbm, g_hbm = refs[:3]
    small = (len(refs) - 9) // 2
    sources, (xa, ga) = refs[3 : 3 + small], refs[3 + small : 5 + small]
    kept, (tails_ref, x16, bc16, sems) = refs[5 + small : -4], refs[-4:]
    bc_hbm = sources[2]
    rows, width = x_hbm.shape
    place = place_ref[0]
    chunk = pl.ds(0, xa.shape[1])
    last = pl.ds(rows - ROWS16, ROWS16)
    tails = [
        pltpu.make_async_copy(x_hbm.at[last, :], x16, sems.at[small + 2]),
        pltpu.make_async_copy(bc_hbm.at[last, :], bc16, sems.at[small + 3]),
    ]
    copies = [pltpu.make_async_copy(sources[i], kept[i], sems.at[i]) for i in range(small)]
    for copy in tails:
        copy.start()

    @pl.when(place == 0)
    def _():
        run_copies(copies + [pltpu.make_async_copy(x_hbm.at[:, chunk], xa, sems.at[small])])

    @pl.when(place == count - 1)
    def _():
        run_copies(copies + [pltpu.make_async_copy(g_hbm.at[:, chunk], ga, sems.at[small + 1])])

    for copy in tails:
        copy.wait()
    tails_ref[:, :width] = x16[...].astype(f32)[ROWS16 - HALO :].astype(bf16)
    tails_ref[:, width:] = bc16[...].astype(f32)[ROWS16 - HALO :].astype(bf16)


def load_kernel(*refs):
    count = (len(refs) - 2) // 2
    sources, kept, sems = refs[:count], refs[count + 1 : -1], refs[-1]
    run_copies(
        [pltpu.make_async_copy(sources[i], kept[i], sems.at[i]) for i in range(count)]
    )


def head_rows(ref, h):
    return ref[pl.ds(h, 1), :], ref[pl.ds(h + 1, 1), :]


def state_of(bc_rows, factors):
    over = (((0,), (0,)), ((), ()))
    return lax.dot_general(bc_rows, factors, over, preferred_element_type=f32)


def weighted_tails(start, heads_at, x_ref, wx_ref, halo, gt, pad, lw):
    rows, width = lw.shape
    for q, lanes in enumerate(lane_blocks(width)):
        full = slice(start + q * LANES, start + (q + 1) * LANES)
        one = pad.at[q]
        put_padded(one, halo(full), x_ref[:, full])
        pre = conv_rows(one, tap_rows(wx_ref, full), rows)
        inner = (pre * sigmoid(pre)).astype(bf16).astype(f32)
        factor = spread(*head_rows(gt, heads_at + 2 * q))
        lw[:, lanes] = (inner * factor).astype(bf16)


def led_gradients(start, heads_at, g_ref, sl, lg):
    for q, lanes in enumerate(lane_blocks(lg.shape[1])):
        full = slice(start + q * LANES, start + (q + 1) * LANES)
        lead = spread(*head_rows(sl, heads_at + 2 * q))
        lg[:, lanes] = (g_ref[:, full].astype(f32) * lead).astype(bf16)


def mapped_half(half, state, rows, bc_block, halo, wbc_ref, bcpad):
    lanes = slice(half * state, (half + 1) * state)
    put_padded(bcpad, halo, bc_block)
    pre = conv_rows(bcpad, tap_rows(wbc_ref, lanes), rows)
    return (pre * sigmoid(pre)).astype(bf16)


def put_first_rows(pay_ref, lg, bc_ref, taps):
    state = pay_ref.shape[0] - ROWS16
    width, bcw = lg.shape[1], bc_ref.shape[1]
    bc8 = bc_ref[0:ROWS16, :].astype(f32)[0:8]
    bc8 = jnp.concatenate([bc8, jnp.zeros((8, width - bcw), f32)], axis=1)
    lg8 = lg[0:ROWS16, :].astype(f32)[0:8]
    pay_ref[state:, :] = jnp.concatenate([lg8, bc8], axis=0).astype(bf16)


def first_rows_state(more, bc_ref, wbc_ref, bcpad):
    rows, bcw = bc_ref.shape
    state = bcw // 2
    taps = wbc_ref.shape[0]
    zeros = jnp.zeros((8, state), f32)
    edge = bc_ref[rows - ROWS16 :, state:].astype(f32)[ROWS16 - HALO :]
    block = jnp.concatenate([more[8:16, state:bcw], zeros], axis=0)
    c = mapped_half(1, state, ROWS16, block, edge, wbc_ref, bcpad)
    early = lax.broadcasted_iota(jnp.int32, c.shape, 0) < taps - 1
    lg = jnp.concatenate([more[0:8, :], jnp.zeros((8, more.shape[1]), f32)], axis=0)
    return state_of(jnp.where(early, c, jnp.zeros_like(c)), lg.astype(bf16))


def first_state_kernel(count, scale, *refs):
    place_ref, dec_ref, xa_ref, ga_ref, wx_ref, bc_ref, wbc_ref, tails_ref = refs[:8]
    pay_ref, pad, gt, sl, lw, lg, bcpad, tails, more = refs[8:]
    rows, width = xa_ref.shape
    taps, bcw = wbc_ref.shape
    state = bcw // 2
    place = place_ref[0]
    none = jnp.zeros((HALO, LANES), f32)

    @pl.when(place == 0)
    def _():
        dec = dec_ref[...]
        gt[...] = gain_of(dec) * tail_of(running_sum(dec))
        b = mapped_half(0, state, rows, bc_ref[:, :state], none, wbc_ref, bcpad)
        weighted_tails(0, 0, xa_ref, wx_ref, lambda _: none, gt, pad, lw)
        pay_ref[0:state, :] = state_of(b, lw[...]).astype(bf16)
        tails[...] = tails_ref[...].astype(f32)
        more[0:8, :] = tails[:, 0:width]
        more[8:16, :] = tails[:, width : 2 * width]
        more[8 : 7 + taps, 0:bcw] = tails[HALO - taps + 1 :, 2 * width :]
        pay_ref[state:, :] = more[...].astype(bf16)

    @pl.when(place == count - 1)
    def _():
        sl[...] = scale * jnp.exp(running_sum(dec_ref[...]))
        c = mapped_half(1, state, rows, bc_ref[:, state:], none, wbc_ref, bcpad)
        late = lax.broadcasted_iota(jnp.int32, c.shape, 0) >= taps - 1
        led_gradients(0, 0, ga_ref, sl, lg)
        pay_ref[0:state, :] = state_of(jnp.where(late, c, jnp.zeros_like(c)), lg[...]).astype(bf16)
        put_first_rows(pay_ref, lg, bc_ref, taps)


def middle_first_kernel(count, scale, *refs):
    place_ref, dec_ref, x_ref, g_ref, wx_ref, bc_ref, wbc_ref, _ = refs[:8]
    cum_ref, map_ref, u_ref, v_ref, tot_ref, gt16_ref, lg16_ref = refs[8:15]
    pad, gt, sl, lw, lg, bcpad = refs[15:]
    rows, bcw = bc_ref.shape
    state = bcw // 2
    none = jnp.zeros((HALO, LANES), f32)
    dec = dec_ref[...]
    cum = running_sum(dec)
    cum_ref[...] = cum
    for half in range(2):
        lanes = slice(half * state, (half + 1) * state)
        made = mapped_half(half, state, rows, bc_ref[:, lanes], none, wbc_ref, bcpad.at[half])
        map_ref[:, lanes] = made
    place = place_ref[0]

    @pl.when(jnp.logical_and(place > 0, place < count - 1))
    def _():
        gt[...] = gain_of(dec) * tail_of(cum)
        lead = jnp.exp(cum)
        sl[...] = scale * lead
        weighted_tails(0, 0, x_ref, wx_ref, lambda _: none, gt, pad, lw)
        led_gradients(0, 0, g_ref, sl, lg)
        lane_totals(lead, 0, tot_ref)
        for q, lanes in enumerate(lane_blocks(lw.shape[1])):
            half = LANES // 2
            a, b = (row[:, 0:LANES] for row in head_rows(gt, 2 * q))
            both = [jnp.broadcast_to(row, (half, LANES)) for row in (a, b)]
            gt16_ref[:, lanes] = jnp.concatenate(both, axis=0).T[0:ROWS16]
        lg16_ref[...] = lg[0:ROWS16, :]
        late = lax.broadcasted_iota(jnp.int32, (rows, state), 0) >= ROWS16
        zero = jnp.zeros((rows, state), bf16)
        u_ref[...] = state_of(jnp.where(late, map_ref[:, :state], zero), lw[...])
        v_ref[...] = state_of(jnp.where(late, map_ref[:, state:], zero), lg[...])


def fix_kernel(count, *refs):
    place_ref, halo_in, came_ref, x_ref, wx_ref, bc_ref, wbc_ref, map_in = refs[:8]
    u_in, v_in, tot_ref, gt16_ref, lg16_ref, _ = refs[8:14]
    halo_ref, map_ref, u_ref, v_ref, came_out, pay_ref, halo, more, pad, bcpad = refs[14:]
    rows, bcw = bc_ref.shape
    state = bcw // 2
    taps = wbc_ref.shape[0]
    width = u_in.shape[1]
    place = place_ref[0]
    more[...] = came_ref[state:, :].astype(f32)
    halo[...] = halo_in[...].astype(f32)

    @pl.when(place == 1)
    def _():
        halo[:, 0:width] = more[0:8, :]
        halo[:, width : 2 * width] = more[8:16, :]
        halo[HALO - taps + 1 :, 2 * width :] = more[8 : 7 + taps, 0:bcw]

    halo_ref[...] = halo[...].astype(bf16)
    map_ref[...] = map_in[...]
    for half in range(2):
        lanes = slice(half * state, (half + 1) * state)
        edge = halo[:, 2 * width + half * state : 2 * width + (half + 1) * state]
        one = bcpad.at[half]
        made = mapped_half(half, state, ROWS16, bc_ref[0:ROWS16, lanes], edge, wbc_ref, one)
        map_ref[0:ROWS16, lanes] = made
    came_out[...] = came_ref[0:state, :]
    tot = tot_ref[0:1, :]

    @pl.when(jnp.logical_and(place > 0, place < count - 1))
    def _():
        lw16 = []
        for q, lanes in enumerate(lane_blocks(width)):
            one = pad.at[q]
            put_padded(one, halo[:, lanes], x_ref[0:ROWS16, lanes])
            pre = conv_rows(one, tap_rows(wx_ref, lanes), ROWS16)
            inner = (pre * sigmoid(pre)).astype(bf16).astype(f32)
            lw16.append((inner * gt16_ref[:, lanes]).astype(bf16))
        lw16 = jnp.concatenate(lw16, axis=1)
        u_ref[...] = u_in[...] + state_of(map_ref[0:ROWS16, :state], lw16)
        v_ref[...] = v_in[...] + state_of(map_ref[0:ROWS16, state:], lg16_ref[...])

    @pl.when(place == 1)
    def _():
        pay_ref[...] = (u_ref[...] + tot * came_ref[0:state, :].astype(f32)).astype(bf16)

    @pl.when(place == count - 2)
    def _():
        extra = first_rows_state(more, bc_ref, wbc_ref, bcpad.at[0])
        came = came_ref[0:state, :].astype(f32) + extra
        came_out[...] = came.astype(bf16)
        pay_ref[...] = (v_ref[...] + tot * came).astype(bf16)


def lane_totals(lead, heads_at, tot_ref):
    rows = lead.shape[1]
    for q, lanes in enumerate(lane_blocks(tot_ref.shape[1])):
        low = lax.broadcasted_iota(jnp.int32, (8, LANES), 1) < LANES // 2
        a, b = (lead[heads_at + 2 * q + i :, rows - 1 :][:1] for i in range(2))
        tot_ref[:, lanes] = jnp.where(low, a, b)


def middle_state_kernel(count, start, heads_at, scale, *refs):
    place_ref, dec_ref, x_ref, g_ref, halo_ref, wx_ref, cum_ref, map_ref, _ = refs[:9]
    u_ref, v_ref, tot_ref = refs[9:12]
    pad, gt, sl, lw, lg = refs[12:]
    state = map_ref.shape[1] // 2
    place = place_ref[0]

    @pl.when(jnp.logical_and(place > 0, place < count - 1))
    def _():
        cum = cum_ref[...]
        gt[...] = gain_of(dec_ref[...]) * tail_of(cum)
        lead = jnp.exp(cum)
        sl[...] = scale * lead

        def halo(full):
            return halo_ref[:, full].astype(f32)

        weighted_tails(start, heads_at, x_ref, wx_ref, halo, gt, pad, lw)
        led_gradients(start, heads_at, g_ref, sl, lg)
        lane_totals(lead, heads_at, tot_ref)
        u_ref[...] = state_of(map_ref[:, :state], lw[...])
        v_ref[...] = state_of(map_ref[:, state:], lg[...])


def end_state_kernel(count, start, heads_at, scale, *refs):
    place_ref, dec_ref, x_ref, g_ref, wx_ref, bc_ref, cum_ref, map_ref, _ = refs[:9]
    pay_ref, pad, gt, sl, lw, lg = refs[9:]
    state = map_ref.shape[1] // 2
    taps = wx_ref.shape[0]
    place = place_ref[0]

    @pl.when(place == 0)
    def _():
        gt[...] = gain_of(dec_ref[...]) * tail_of(cum_ref[...])
        none = jnp.zeros((HALO, LANES), f32)
        weighted_tails(start, heads_at, x_ref, wx_ref, lambda _: none, gt, pad, lw)
        pay_ref[0:state, :] = state_of(map_ref[:, :state], lw[...]).astype(bf16)

    @pl.when(place == count - 1)
    def _():
        sl[...] = scale * jnp.exp(cum_ref[...])
        led_gradients(start, heads_at, g_ref, sl, lg)
        c = map_ref[:, state:]
        late = lax.broadcasted_iota(jnp.int32, c.shape, 0) >= taps - 1
        pay_ref[0:state, :] = state_of(jnp.where(late, c, jnp.zeros_like(c)), lg[...]).astype(bf16)
        put_first_rows(pay_ref, lg, bc_ref, taps)


def message_kernel(hop, place_ref, u_ref, v_ref, tot_ref, came_ref, _, out_ref):
    own = jnp.where(place_ref[0] == hop, u_ref[...], v_ref[...])
    out_ref[...] = (own + tot_ref[0:1, :] * came_ref[...].astype(f32)).astype(bf16)


def fix_message_kernel(count, *refs):
    place_ref, u_ref, v_ref, tot_ref, came_ref, bc_ref, wbc_ref, _ = refs[:8]
    came_out, out_ref, more, bcpad = refs[8:]
    state = u_ref.shape[0]
    place = place_ref[0]
    tot = tot_ref[0:1, :]
    came_out[...] = came_ref[0:state, :]

    @pl.when(place == 1)
    def _():
        out_ref[...] = (u_ref[...] + tot * came_ref[0:state, :].astype(f32)).astype(bf16)

    @pl.when(place == count - 2)
    def _():
        more[...] = came_ref[state:, :].astype(f32)
        extra = first_rows_state(more, bc_ref, wbc_ref, bcpad)
        came = came_ref[0:state, :].astype(f32) + extra
        came_out[...] = came.astype(bf16)
        out_ref[...] = (v_ref[...] + tot * came).astype(bf16)


def edge_kernel(count, spans, parts, *refs):
    hops = count - 2
    place_ref, map_ref = refs[:2]
    blocks, refs = refs[3 : 3 + 2 * parts], refs[3 + 2 * parts :]
    came, (out_ref, edge) = refs[: 2 * hops], refs[2 * hops :]
    state = map_ref.shape[1] // 2
    b = map_ref[0:ROWS16, :state]
    per = len(spans) // 2
    for c in range(2):
        wanted = came[c * hops : (c + 1) * hops]
        grad = pick(place_ref[0], wanted, lambda hop: count - 2 - hop, state)
        extra = dot(b, grad)
        for q in range(per):
            part, lanes = spans[c * per + q]
            dx_ref, q_ref = blocks[2 * part : 2 * part + 2]
            here = slice(q * LANES, (q + 1) * LANES)
            rows = dx_ref[0:ROWS16, lanes] + q_ref[0:ROWS16, lanes].astype(f32) * extra[:, here]
            edge[4 * c : 4 * c + 4, here] = rows[0:4]
    out_ref[...] = edge[...].astype(bf16)


def intra_kernel(first, start, pairs, head_dim, scale, *refs):
    x_ref, g_ref, halo_ref, wx_ref, dec_ref, cum_ref, map_ref, skip_ref, _ = refs[:9]
    refs = refs[9:]
    if not first:
        dsim_in, gs_in = refs[:2]
        refs = refs[2:]
    y0_ref, dx_ref, q_ref, ls_ref, lw_ref, lg_ref, dsim_ref, gs_ref = refs[:8]
    pad, sim, gain = refs[8:]
    rows = x_ref.shape[0]
    state = map_ref.shape[1] // 2
    half = rows // 2
    gain[...] = gain_of(dec_ref[...])
    sim[...] = dot_nt(map_ref[:, state:], map_ref[:, :state])
    if first:
        dsim_ref[...] = jnp.zeros(dsim_ref.shape, f32)
        gs_ref[...] = jnp.zeros(gs_ref.shape, f32)
    else:
        dsim_ref[...] = dsim_in[...]
        gs_ref[...] = gs_in[...]
    lane = lax.broadcasted_iota(jnp.int32, (1, LANES), 1)
    low = lane < head_dim
    r_i = lax.broadcasted_iota(jnp.int32, (half, half), 0)
    c_i = lax.broadcasted_iota(jnp.int32, (half, half), 1)
    lower = r_i >= c_i

    def pair(q):
        lanes = slice(q * LANES, (q + 1) * LANES)
        full = slice(start + q * LANES, start + (q + 1) * LANES)
        h = start // head_dim + 2 * q
        one = pad.at[q]
        put_padded(one, halo_ref[:, full].astype(f32), x_ref[:, full])
        pre = conv_rows(one, tap_rows(wx_ref, full), rows)
        sg = sigmoid(pre)
        inner = (pre * sg).astype(bf16).astype(f32)
        sgrad = sg * (1.0 + pre * (1.0 - sg))
        gn = spread(*head_rows(gain, h))
        cums = head_rows(cum_ref, h)
        cols = [column(row) for row in cums]
        both = jnp.where(low, cols[0], cols[1])
        tl = jnp.exp(both[rows - 1 :] - both)
        ls = scale * jnp.exp(both)
        w = (inner * gn).astype(bf16)
        g = g_ref[:, full]
        gf = g.astype(f32)
        g_t = gf.T.astype(bf16)
        y = ds = None
        dw_t = []
        for a in range(2):
            row, col = cums[a], cols[a]
            keep = low if a == 0 else jnp.logical_not(low)
            d00 = jnp.exp(jnp.where(lower, col[:half] - row[:, :half], NEG))
            d10 = jnp.exp(col[half:] - row[:, :half])
            d11 = jnp.exp(jnp.where(lower, col[half:] - row[:, half:], NEG))
            m00 = (d00 * sim[0:half, 0:half]).astype(bf16)
            m10 = (d10 * sim[half:rows, 0:half]).astype(bf16)
            m11 = (d11 * sim[half:rows, half:rows]).astype(bf16)
            w_a = jnp.where(keep, w, jnp.zeros_like(w))
            top = dot(m00, w_a[:half])
            bot = dot(jnp.concatenate([m10, m11], axis=1), w_a)
            y_a = jnp.concatenate([top, bot], axis=0)
            y = y_a if y is None else y + y_a
            g_at = g_t[a * head_dim : (a + 1) * head_dim]
            left = dot(g_at, jnp.concatenate([m00, m10], axis=0))
            right = dot(g_at[:, half:], m11)
            dw_t.append(jnp.concatenate([left, right], axis=1))
            mix_top = dot_nt(g[:half], w_a[:half])
            mix_bot = dot_nt(g[half:], w_a)
            now = (d00 * mix_top, d10 * mix_bot[:, :half], d11 * mix_bot[:, half:])
            ds = now if ds is None else [one + two for one, two in zip(ds, now)]
        dsim_ref[0:half, 0:half] += ds[0]
        dsim_ref[half:rows, 0:half] += ds[1]
        dsim_ref[half:rows, half:rows] += ds[2]
        dw = scale * jnp.concatenate(dw_t, axis=0).T
        skip = jnp.where(low, skip_ref[:, h : h + 1], skip_ref[:, h + 1 : h + 2])
        y0_ref[:, lanes] = scale * y + skip * inner
        dx_ref[:, lanes] = (gn * dw + skip * gf) * sgrad
        q_ref[:, lanes] = (gn * tl * sgrad).astype(bf16)
        ls_ref[:, lanes] = ls.astype(bf16)
        lw_ref[:, lanes] = (inner * gn * tl).astype(bf16)
        lg_ref[:, lanes] = (gf * ls).astype(bf16)
        gi = jnp.sum(gf * inner, axis=0, keepdims=True)
        sum_a = jnp.sum(jnp.where(low, gi, 0.0), axis=1, keepdims=True)
        sum_b = jnp.sum(jnp.where(low, 0.0, gi), axis=1, keepdims=True)
        gs_ref[...] += jnp.where(lane == h, sum_a, 0.0) + jnp.where(lane == h + 1, sum_b, 0.0)

    for q in range(pairs):
        pair(q)


def pick(place, parts, wanted, state):
    total = jnp.zeros((state, parts[0].shape[1]), bf16)
    for hop, ref in enumerate(parts):
        total = jnp.where(place == wanted(hop), ref[0:state, :], total)
    return total


def add_states(spans, blocks, which, states, total):
    done = 0
    while done < len(spans):
        part, lanes = spans[done]
        size = 1
        while done + size < len(spans) and spans[done + size][0] == part:
            size += 1
        mine = slice(lanes.start, lanes.start + size * LANES)
        here = slice(done * LANES, (done + size) * LANES)
        made = dot_nt(blocks[2 * part + which][:, mine], states[:, here])
        total = made if total is None else total + made
        done += size
    return total


def before_silu(half, total, bc_ref, halo_ref, wbc_ref, bcpad):
    rows, bcw = bc_ref.shape
    state = bcw // 2
    taps = wbc_ref.shape[0]
    inner = halo_ref.shape[1] - bcw
    lanes = slice(half * state, (half + 1) * state)
    edge = halo_ref[:, inner + half * state : inner + (half + 1) * state].astype(f32)
    put_padded(bcpad, edge, bc_ref[:, lanes])
    dpre = total * silu_grad(conv_rows(bcpad, tap_rows(wbc_ref, lanes), rows))
    sums = []
    for k in range(taps):
        moved = bcpad[HALO - taps + 1 + k : HALO - taps + 1 + k + rows, :]
        sums.append(jnp.sum(dpre * moved, axis=0, keepdims=True))
    return dpre, jnp.concatenate(sums + [jnp.zeros((8 - taps, state), f32)], axis=0)


def finish_bc_kernel(count, first, spans, parts, scale, *refs):
    hops = count - 1
    place_ref, map_ref, sum_in = refs[:3]
    blocks, refs = refs[4 : 4 + 2 * parts], refs[4 + 2 * parts :]
    came, refs = refs[:hops], refs[hops:]
    bcw = map_ref.shape[1]
    state = bcw // 2
    place = place_ref[0]
    enter = pick(place, came, lambda hop: hop + 1, state)
    grad = pick(place, came, lambda hop: count - 2 - hop, state)
    if first:
        ds = scale * sum_in[...]
        high = ds.astype(bf16)
        rest = (ds - high.astype(f32)).astype(bf16)
        ds_t = ds.T
        high_t = ds_t.astype(bf16)
        rest_t = (ds_t - high_t.astype(f32)).astype(bf16)
        b, c = map_ref[:, :state], map_ref[:, state:]
        d_b = dot(high_t, c) + dot(rest_t, c)
        d_c = dot(high, b) + dot(rest, b)
    else:
        d_b, d_c = sum_in[:, :state], sum_in[:, state:]
    d_b = add_states(spans, blocks, 0, grad, d_b)
    d_c = add_states(spans, blocks, 1, enter, d_c)
    if first:
        (dbc_ref,) = refs
        dbc_ref[:, :state] = d_b
        dbc_ref[:, state:] = d_c
        return
    bc_ref, halo_ref, wbc_ref, gs_ref, own_ref, small_ref, bcpad = refs
    for half in range(2):
        lanes = slice(half * state, (half + 1) * state)
        made = before_silu(half, (d_b, d_c)[half], bc_ref, halo_ref, wbc_ref, bcpad.at[half])
        own_ref[:, lanes], small_ref[:, lanes] = made
    small_ref[:, bcw:] = gs_ref[...]


def finish_kernel(count, start, spans, parts, pieces, *refs):
    hops = count - 1
    place_ref, x_ref, wx_ref, map_ref = refs[:4]
    blocks, refs = refs[5 : 5 + 4 * parts], refs[5 + 4 * parts :]
    came, refs = refs[:hops], refs[hops:]
    if start:
        refs = refs[2:]
    y_hbm, gx_hbm, taps_ref, end_ref, enter, grad, pad, y_ref, gx_ref, sems = refs
    rows = x_ref.shape[0]
    taps = wx_ref.shape[0]
    state = enter.shape[0]
    place = place_ref[0]
    b, c = map_ref[:, :state], map_ref[:, state:]
    enter[...] = pick(place, came, lambda hop: hop + 1, state)
    grad[...] = pick(place, came, lambda hop: count - 2 - hop, state)
    copies = []
    first = 0
    for number, size in enumerate(pieces):
        for q in range(first, first + size):
            part, mine = spans[q]
            y0_ref, dx_ref, q_ref, ls_ref = blocks[4 * part : 4 * part + 4]
            lanes = slice(q * LANES, (q + 1) * LANES)
            full = slice(start + q * LANES, start + (q + 1) * LANES)
            inter = dot(c, enter[:, lanes])
            y_ref[:, lanes] = (y0_ref[:, mine] + ls_ref[:, mine].astype(f32) * inter).astype(bf16)
            one = pad.at[q]
            inter = dot(b, grad[:, lanes])
            one[0:rows, :] = dx_ref[:, mine] + q_ref[:, mine].astype(f32) * inter
            one[rows : rows + HALO, :] = jnp.zeros((HALO, LANES), f32)
            x = x_ref[:, full].astype(f32)
            total = None
            sums = []
            for k, weight in enumerate(tap_rows(wx_ref, full)):
                shifted = one[taps - 1 - k : taps - 1 - k + rows, :]
                term = weight * shifted
                total = term if total is None else total + term
                sums.append(jnp.sum(shifted * x, axis=0, keepdims=True))
            gx_ref[:, lanes] = total.astype(bf16)
            end_ref[:, lanes] = total[rows - ROWS16 :]
            sums = jnp.concatenate(sums + [jnp.zeros((8 - taps, LANES), f32)], axis=0)
            taps_ref[:, lanes] = sums
        lanes = slice(first * LANES, (first + size) * LANES)
        full = slice(start + first * LANES, start + (first + size) * LANES)
        for i, (made, out) in enumerate(((y_ref, y_hbm), (gx_ref, gx_hbm))):
            copy = pltpu.make_async_copy(made.at[:, lanes], out.at[:, full], sems.at[number, i])
            copy.start()
            copies.append(copy)
        first += size
    for copy in copies:
        copy.wait()


def sums_kernel(halo_ref, edge_ref, taps_a, taps_b, sums_ref, halo):
    taps, width = 4, taps_a.shape[1]
    edge = edge_ref[...].astype(f32)
    halo[...] = halo_ref[:, 0 : 2 * width].astype(f32)
    for c, own in enumerate((taps_a, taps_b)):
        lanes = slice(c * width, (c + 1) * width)
        sums_ref[:, lanes] = own[...]
        for k in range(taps - 1):
            added = None
            for j in range(taps - 1 - k):
                at = HALO - taps + 1 + k + j
                term = edge[4 * c + j : 4 * c + j + 1] * halo[at : at + 1, lanes]
                added = term if added is None else added + term
            sums_ref[k : k + 1, lanes] += added


def write_kernel(wx_ref, edge_ref, end_a, end_b, _, gx_in, gx_hbm, gx16, sem):
    taps = wx_ref.shape[0]
    rows = gx_hbm.shape[0]
    width = end_a.shape[1]
    edge = edge_ref[...].astype(f32)
    row = lax.broadcasted_iota(jnp.int32, (ROWS16, width), 0)
    for c, end_ref in enumerate((end_a, end_b)):
        lanes = slice(c * width, (c + 1) * width)
        end = end_ref[...]
        for k in range(taps - 1):
            for j in range(taps - 1 - k):
                at = ROWS16 - (taps - 1 - k) + j
                here = wx_ref[k : k + 1, lanes] * edge[4 * c + j : 4 * c + j + 1]
                end = end + jnp.where(row == at, here, 0.0)
        gx16[:, lanes] = end.astype(bf16)
    tail = pl.ds(rows - ROWS16, ROWS16)
    run_copies([pltpu.make_async_copy(gx16, gx_hbm.at[tail, :], sem.at[0])])


def pack_kernel(own_ref, small_ref, small_dp, small_out, head_ref):
    rows, bcw = own_ref.shape
    small = small_ref[...] + small_dp[...]
    small_out[...] = small
    head_ref[0:rows, :] = own_ref[...].astype(bf16)
    sums = small[:, :bcw]
    head_ref[rows:, :] = jnp.concatenate([sums, jnp.zeros_like(sums)], axis=0).astype(bf16)


def merge_kernel(heads, *refs):
    sums_ref, sums_dp, small_ref, own_ref = refs[:4]
    others, (full_ref, out_ref, send_ref) = refs[4 : 3 + heads], refs[3 + heads :]
    rows, bc = own_ref.shape
    total = sums_ref[...] + sums_dp[...]
    half = total.shape[1] // 2
    full = own_ref[...]
    taps_bc = small_ref[:, :bc]
    for other in others:
        block = other[...].astype(f32)
        full = full + block[:rows]
        taps_bc = taps_bc + block[rows : rows + 8]
    full_ref[...] = full
    send_ref[0:4, 0:half] = total[0:4, :half]
    send_ref[4:8, 0:half] = total[0:4, half:]
    send_ref[0:4, half : half + bc] = taps_bc[0:4]
    send_ref[4:8, half : half + bc] = full[0:4]
    send_ref[:, half + bc :] = small_ref[:, bc:]
    out_ref[...] = send_ref[...].astype(bf16)


def conv_bc_kernel(full_ref, wbc_ref, _, out_ref, pad):
    taps = wbc_ref.shape[0]
    rows, bcw = full_ref.shape
    for half in range(2):
        lanes = slice(half * bcw // 2, (half + 1) * bcw // 2)
        one = pad.at[half]
        one[0:rows, :] = full_ref[:, lanes]
        one[rows:, :] = jnp.zeros((HALO, bcw // 2), f32)
        out = None
        for k, weight in enumerate(tap_rows(wbc_ref, lanes)):
            term = weight * one[taps - 1 - k : taps - 1 - k + rows, :]
            out = term if out is None else out + term
        out_ref[:, lanes] = out


def last_kernel(count, norm_tokens, norm_skip, *refs):
    place_ref, sums_ref, conv_ref, wbc_ref = refs[:4]
    parts = refs[4 : 3 + count]
    gbc_ref, tx_ref, tbc_ref, skip_ref = refs[3 + count :]
    taps, bc = wbc_ref.shape
    rows = conv_ref.shape[0]
    half = tx_ref.shape[1] // 2
    total = sums_ref[...].astype(f32)
    edge = jnp.zeros((4, bc), f32)
    for hop, ref in enumerate(parts):
        block = ref[...].astype(f32)
        total = total + block
        if hop == count - 2:
            edge = jnp.where(place_ref[0] < count - 1, block[4:8, half : half + bc], 0.0)
    tx_ref[:, :half] = total[0:taps, 0:half] * norm_tokens
    tx_ref[:, half:] = total[4 : 4 + taps, 0:half] * norm_tokens
    tbc_ref[...] = total[0:taps, half : half + bc] * norm_tokens
    skip_ref[...] = total[0:1, half + bc : half + bc + skip_ref.shape[1]] * norm_skip
    gbc_ref[0 : rows - ROWS16, :] = conv_ref[0 : rows - ROWS16, :].astype(bf16)
    row = lax.broadcasted_iota(jnp.int32, (ROWS16, bc), 0)
    end = conv_ref[rows - ROWS16 :, :]
    for k in range(taps - 1):
        for j in range(taps - 1 - k):
            at = ROWS16 - (taps - 1 - k) + j
            end = end + jnp.where(row == at, wbc_ref[k : k + 1, :] * edge[j : j + 1], 0.0)
    gbc_ref[rows - ROWS16 :, :] = end.astype(bf16)


COST_US = {"middle_state": 1.5, "inside_block": 2.7, "sums": 0.8, "write": 0.8}
BYTES_PER_US = 3_500_000


def call(kernel, name, ins, outs, scratch=(), grid=(1,), kept=()):
    def spec(item):
        if not isinstance(item, tuple):
            whole = item.shape
            return pl.BlockSpec(whole, lambda *_: (0,) * len(whole))
        if item[1] == "smem":
            return pl.BlockSpec(memory_space=pltpu.SMEM)
        if item[1] == "any":
            return pl.BlockSpec(memory_space=pl.ANY)
        if item[1] == "hbm":
            return pl.BlockSpec(memory_space=pltpu.HBM)
        return pl.BlockSpec(item[1], item[2])

    def array(item):
        return item[0] if isinstance(item, tuple) else item

    return pl.pallas_call(
        kernel,
        grid=grid,
        in_specs=[spec(i) for i in ins],
        out_specs=[spec(o) for o in outs],
        out_shape=[array(o) for o in outs],
        scratch_shapes=list(scratch),
        compiler_params=pltpu.CompilerParams(vmem_limit_bytes=VMEM_LIMIT),
        cost_estimate=pl.CostEstimate(
            flops=0, bytes_accessed=int(COST_US.get(name, 0.01) * BYTES_PER_US), transcendentals=0
        ),
        input_output_aliases=dict(kept),
        name=name,
    )(*[array(i) for i in ins])


def chain_routes(count, hop):
    return [(hop, hop + 1), (count - 1 - hop, count - 2 - hop)]


def shape(s, d=f32):
    return jax.ShapeDtypeStruct(s, d)


def local(x_input, bc_input, decays, conv_x, conv_bc, skip_gain, grad_out):
    x, bc, dec, g = x_input[0], bc_input[0], decays[0], grad_out[0]
    rows, inner = x.shape
    taps = conv_x.shape[0]
    heads = dec.shape[0]
    head_dim = inner // heads
    bcw = bc.shape[1]
    state = bcw // 2
    scale = state ** (-0.5)
    count = lax.axis_size("seq")
    head_count = lax.axis_size("head")
    dp_count = lax.axis_size("dp")
    assert rows == BLOCK_LEN and 2 * head_dim == LANES and taps == 4
    assert count % 2 == 0 and count > 2 and dp_count == 2
    width = inner // 2
    chunks = (0, 1)
    block = 640 if width % 640 == 0 else LANES
    per = width // block
    pairs = width // LANES
    split = (pairs // 2, pairs + pairs // 5, pairs - pairs // 2 - pairs // 5)
    spans = [
        (part, slice(at * LANES, (at + 1) * LANES))
        for part, size in enumerate(split)
        for at in range(size)
    ]
    place = lax.axis_index("seq").astype(jnp.int32).reshape(1)
    where_am_i = (place, "smem")

    def vmem(s, d=f32):
        return pltpu.VMEM(s, d)

    def in_hbm(a):
        return (pltpu.with_memory_space_constraint(a, pltpu.HBM), "hbm")

    def padded(blocks, length=rows):
        return vmem((blocks, length + HALO, LANES))

    state_scratch = [
        padded(pairs),
        vmem((heads, rows)),
        vmem((heads, rows)),
        vmem((rows, width), bf16),
        vmem((rows, width), bf16),
    ]
    received = [[], []]

    def hop_on(c, message):
        routes = chain_routes(count, len(received[c]))
        received[c].append(lax.ppermute(message, "seq", routes))

    skip = skip_gain.reshape(1, heads)
    sources = [dec, conv_x, bc, conv_bc]
    xa, ga, *made, tails = call(
        functools.partial(early_load_kernel, count),
        "early_load",
        [where_am_i, in_hbm(x), in_hbm(g)] + [in_hbm(a) for a in sources],
        [shape((rows, width), bf16), shape((rows, width), bf16)]
        + [shape(a.shape, a.dtype) for a in sources]
        + [shape((HALO, inner + bcw), bf16)],
        [
            vmem((ROWS16, inner), bf16),
            vmem((ROWS16, bcw), bf16),
            pltpu.SemaphoreType.DMA((len(sources) + 4,)),
        ],
    )
    pay = call(
        functools.partial(first_state_kernel, count, scale),
        "first_state",
        [where_am_i, made[0], xa, ga, *made[1:], tails],
        [shape((state + ROWS16, width), bf16)],
        state_scratch
        + [vmem((rows + HALO, LANES)), vmem((HALO, inner + bcw)), vmem((ROWS16, width))],
    )[0]
    hop_on(0, pay)
    sources = [x, bc, g, dec, conv_x, conv_bc, skip]
    x, bc, g, dec, conv_x, conv_bc, skip = call(
        load_kernel,
        "load",
        [in_hbm(a) for a in sources] + [(pay, "any")],
        [shape(a.shape, a.dtype) for a in sources],
        [pltpu.SemaphoreType.DMA((len(sources),))],
    )
    halo = lax.ppermute(tails, "seq", [(i, i + 1) for i in range(1, count - 1)])

    states = [None, None]

    def middle_state(c, after):
        start = c * width
        states[c] = call(
            functools.partial(middle_state_kernel, count, start, start // head_dim, scale),
            "middle_state",
            [where_am_i, dec, x, g, halo, conv_x, cum, mapped, (after, "any")],
            [shape((state, width)), shape((state, width)), shape((8, width))],
            state_scratch,
        )
        return states[c][0]

    def message(c, after):
        return call(
            functools.partial(message_kernel, len(received[c])),
            "message",
            [where_am_i, *states[c], received[c][-1], (after, "any")],
            [shape((state, width), bf16)],
        )[0]

    parts = []
    carried = []

    def inside(number, after):
        first = number == 0
        start = sum(split[:number]) * LANES
        span = split[number] * LANES
        ins = [x, g, halo, conv_x, dec, cum, mapped, skip, (after, "any")]
        if not first:
            ins += carried
        made = call(
            functools.partial(intra_kernel, first, start, split[number], head_dim, scale),
            "inside_block",
            ins,
            [
                shape((rows, span)),
                shape((rows, span)),
                shape((rows, span), bf16),
                shape((rows, span), bf16),
                shape((rows, span), bf16),
                shape((rows, span), bf16),
                shape((rows, rows)),
                shape((8, LANES)),
            ],
            [padded(split[number]), vmem((rows, rows)), vmem((heads, rows))],
        )
        parts.append(made[:6])
        carried[:] = made[6:8]
        return made[0]

    def chunk_parts(c):
        mine = spans[c * pairs : (c + 1) * pairs]
        used = sorted({part for part, _ in mine})
        return [(used.index(part), at) for part, at in mine], [parts[p] for p in used]

    cum, mapped, u, v, tot, gt16, lg16 = call(
        functools.partial(middle_first_kernel, count, scale),
        "middle_first",
        [where_am_i, dec, x, g, conv_x, bc, conv_bc, (tails, "any")],
        [
            shape((heads, rows)),
            shape((rows, bcw), bf16),
            shape((state, width)),
            shape((state, width)),
            shape((8, width)),
            shape((ROWS16, width)),
            shape((ROWS16, width), bf16),
        ],
        state_scratch + [padded(2)],
    )
    after = call(
        functools.partial(end_state_kernel, count, width, width // head_dim, scale),
        "end_state",
        [where_am_i, dec, x, g, conv_x, bc, cum, mapped, (u, "any")],
        [shape((state + ROWS16, width), bf16)],
        state_scratch,
    )[0]
    hop_on(1, after)
    halo, mapped, u, v, came, after = call(
        functools.partial(fix_kernel, count),
        "fix_first_rows",
        [where_am_i, halo, received[0][0], x, conv_x, bc, conv_bc, mapped]
        + [u, v, tot, gt16, lg16, (after, "any")],
        [
            shape((HALO, inner + bcw), bf16),
            shape((rows, bcw), bf16),
            shape((state, width)),
            shape((state, width)),
            shape((state, width), bf16),
            shape((state, width), bf16),
        ],
        [
            vmem((HALO, inner + bcw)),
            vmem((ROWS16, width)),
            padded(pairs, ROWS16),
            padded(2, ROWS16),
        ],
    )
    states[0] = (u, v, tot)
    received[0][0] = came
    hop_on(0, after)
    after = middle_state(1, after)
    after = inside(0, after)
    for hop in range(1, count - 1):
        for c in chunks:
            if hop > 1:
                after = message(c, after)
                hop_on(c, after)
            elif c:
                came, after = call(
                    functools.partial(fix_message_kernel, count),
                    "message",
                    [where_am_i, *states[1], received[1][0], bc, conv_bc, (after, "any")],
                    [shape((state, width), bf16), shape((state, width), bf16)],
                    [vmem((ROWS16, width)), vmem((ROWS16 + HALO, LANES))],
                )
                received[1][0] = came
                hop_on(1, after)
            if hop == count - 2:
                after = inside(1 + c, after)
    dsim, gsum = carried
    ins = [where_am_i, mapped, (after, "any")]
    for made in parts:
        ins += made[1:3]
    edge = call(
        functools.partial(edge_kernel, count, spans, len(parts)),
        "edge",
        ins + received[0][: count - 2] + received[1][: count - 2],
        [shape((8, width), bf16)],
        [vmem((8, width))],
    )[0]

    edges = lax.ppermute(edge, "seq", [(i + 1, i) for i in range(count - 1)])

    def finish_bc(c, base, after):
        where, used = chunk_parts(c)
        ins = [where_am_i, mapped, base, (after, "any")]
        for made in used:
            ins += made[4:6]
        ins += received[c]
        outs = [shape((rows, bcw))]
        scratch = []
        if c:
            ins += [bc, halo, conv_bc, gsum]
            outs += [shape((8, bcw + LANES))]
            scratch = [padded(2)]
        kernel = functools.partial(finish_bc_kernel, count, c == 0, where, len(used), scale)
        return call(kernel, "finish_bc", ins, outs, scratch)

    def finish(c, after, kept_y):
        start = c * width
        where, used = chunk_parts(c)
        pieces = (4, 4, 2) if pairs == 10 else (pairs - 1, 1)
        ins = [where_am_i, x, conv_x, mapped, (after, "any")]
        for made in used:
            ins += made[:4]
        ins += received[c]
        kept = ()
        if kept_y:
            kept = ((len(ins), 0), (len(ins) + 1, 1))
            ins += [(a, "hbm") for a in kept_y]
        made = call(
            functools.partial(finish_kernel, count, start, where, len(used), pieces),
            "finish",
            ins,
            [(shape((rows, inner), bf16), "hbm"), (shape((rows, inner), bf16), "hbm")]
            + [shape((8, width)), shape((ROWS16, width))],
            [
                vmem((state, width), bf16),
                vmem((state, width), bf16),
                padded(pairs),
                vmem((rows, width), bf16),
                vmem((rows, width), bf16),
                pltpu.SemaphoreType.DMA((len(pieces), 2)),
            ],
            kept=kept,
        )
        return made[:2], made[2], made[3]

    outs, taps_a, end_a = finish(0, edge, None)
    dbc = finish_bc(0, dsim, taps_a)[0]
    own, small = finish_bc(1, dbc, edges)

    swap = [(0, 1), (1, 0)]
    turns = [[(i, (i + k) % head_count) for i in range(head_count)] for k in range(1, head_count)]
    small, to_heads = call(
        pack_kernel,
        "pack",
        [own, small, lax.ppermute(small, "dp", swap)],
        [shape(small.shape), shape((rows + ROWS16, bcw), bf16)],
    )
    others = [lax.ppermute(to_heads, "head", turn) for turn in turns]

    (y, gx), taps_b, end_b = finish(1, to_heads, outs)
    sums = call(
        sums_kernel,
        "sums",
        [halo, edge, taps_a, taps_b],
        [shape((8, inner))],
        [vmem((HALO, inner))],
    )[0]
    sums_dp = lax.ppermute(sums, "dp", swap)
    send_width = inner // 2 + bcw + LANES
    full, to_seq = call(
        functools.partial(merge_kernel, head_count),
        "merge",
        [sums, sums_dp, small, own] + others,
        [shape((rows, bcw)), shape((8, send_width), bf16)],
        [vmem((8, send_width))],
    )
    gx = call(
        write_kernel,
        "write",
        [conv_x, edges, end_a, end_b, (to_seq, "any"), (gx, "hbm")],
        [(shape((rows, inner), bf16), "hbm")],
        [vmem((ROWS16, inner), bf16), pltpu.SemaphoreType.DMA((1,))],
        kept=((5, 0),),
    )[0]
    from_seq = [
        lax.ppermute(to_seq, "seq", [(i, (i + k) % count) for i in range(count)])
        for k in range(1, count)
    ]
    token_count = rows * count * dp_count
    norm_tokens = float(token_count) ** (-0.5)
    norm_skip = float(token_count * head_dim) ** (-0.5)
    conv = call(
        conv_bc_kernel,
        "conv_bc",
        [full, conv_bc, (to_seq, "any")],
        [shape((rows, bcw))],
        [padded(2)],
    )[0]
    gbc, tx, tbc, skip = call(
        functools.partial(last_kernel, count, norm_tokens, norm_skip),
        "last",
        [where_am_i, to_seq, conv, conv_bc] + from_seq,
        [
            shape((rows, bcw), bf16),
            shape((taps, inner)),
            shape((taps, bcw)),
            shape((1, heads)),
        ],
    )
    return y[None], gx[None], gbc[None], tx, tbc, skip.reshape(heads)


def solution(mesh):
    return jax.shard_map(
        local,
        mesh=mesh,
        in_specs=(
            P(("groups", "dp"), "seq", "head"),
            P(("groups", "dp"), "seq", None),
            P(("groups", "dp"), "head", "seq"),
            P(None, "head"),
            P(),
            P("head"),
            P(("groups", "dp"), "seq", "head"),
        ),
        out_specs=(
            P(("groups", "dp"), "seq", "head"),
            P(("groups", "dp"), "seq", "head"),
            P(("groups", "dp"), "seq", None),
            P("groups", "head"),
            P("groups", None),
            P(("groups", "head")),
        ),
        check_vma=False,
    )
```

time: 68.3 us -> 60.4 us (0.88)
  starting transfers between devices: 22.4 us -> 16.4 us
  Pallas kernels: 25.7 us -> 23.7 us
  waiting for transfers between devices: 18.4 us -> 19.1 us
    ppermute x4 -> x3, waiting for transfers between devices: 0.56 us -> 5.32 us  [the longest x1 4.78 us: local(): edges = lax.ppermute(edge, 'seq', [(i + 1, i) for i in range(count - 1)])]
    ppermute x4 -> x3, starting transfers between devices: 7.81 us -> 3.51 us  [the longest x1 1.56 us: local(): others = [lax.ppermute(to_heads, 'head', turn) for turn in turns]]
    ppermute x3, waiting for transfers between devices: 4.69 us -> 1.54 us  [local(): lax.ppermute(to_seq, 'seq', [(i, (i + k) % count) for i in range(count)])]
    ppermute x3, starting transfers between devices: 5.86 us -> 3.87 us  [local(): lax.ppermute(to_seq, 'seq', [(i, (i + k) % count) for i in range(count)])]
    pallas_call x24, Pallas kernels: 25.7 us -> 23.7 us  [call(): pl.pallas_call(kernel, grid=grid, in_specs=[spec(i) for i in ins], out_sp...]
    ppermute x6, waiting for transfers between devices: 10.7 us -> 9.79 us  [hop_on(): received[c].append(lax.ppermute(message, 'seq', routes))]
  transfers between devices with their start and end apart: 15 -> 14, of which waited for: 9 -> 9; matrix products, arithmetic and copies ran while one was open for 0% -> 0% of each run, Pallas kernels for 34% -> 32%
where the time goes in v4:
time: 60.4 us; the launch traced here: 60.1 us
  Pallas kernels  23.7 us (39%)
  waiting for transfers between devices  19.1 us (32%)
  starting transfers between devices  16.4 us (27%)
  between operations  0.89 us (1%)
    pallas_call x24, Pallas kernels, call(): pl.pallas_call(kernel, grid=grid, in_specs=[spec(i) for i in ins], out_sp...  23.7 us
    ppermute x6, waiting for transfers between devices, hop_on(): received[c].append(lax.ppermute(message, 'seq', routes))  9.79 us
    ppermute x6, starting transfers between devices, hop_on(): received[c].append(lax.ppermute(message, 'seq', routes))  8.89 us
    ppermute x1, waiting for transfers between devices, local(): edges = lax.ppermute(edge, 'seq', [(i + 1, i) for i in range(count - 1)])  4.78 us
    ppermute x3, starting transfers between devices, local(): lax.ppermute(to_seq, 'seq', [(i, (i + k) % count) for i in range(count)])  3.87 us
    ppermute x1, starting transfers between devices, local(): others = [lax.ppermute(to_heads, 'head', turn) for turn in turns]  1.56 us
    ppermute x3, waiting for transfers between devices, local(): lax.ppermute(to_seq, 'seq', [(i, (i + k) % count) for i in range(count)])  1.54 us
    ppermute x1, starting transfers between devices, local(): edges = lax.ppermute(edge, 'seq', [(i + 1, i) for i in range(count - 1)])  1.29 us
  transfers between devices with their start and end apart: 14, of which 9 were waited for; matrix products, arithmetic and copies ran while one was open for 0% of the time, Pallas kernels for 32%

profile of v4, /device:TPU:0, one launch (start us, length us, event | category | flops | bytes accessed | tf_op | source)
XLA Modules:
  0.0 60.1 jit_solution(15788462063871743410)
XLA Ops:
  0.6 1.4 %early_load.1 = (bf16[256,1280]{1,0:T(8,128)(2,1)S(1)}, bf16[256,1280]{1,0:T(8,128)(2,1)S(1)}, f32[40,256]{1,0:T(8,128)S(1)}, f32[4,2560]{1,0:T(4,128)S(1)}, bf1...) custom-call(s32[1]{0:T(128)} %bitcast.refs_0_.place_ref, bf16[256,2560]{1,0:T(8,128)(2,1)} %bitcast.10, ...), custom_call_target="tpu_custom_call" | custom-call | bytes 35000 | tf_op jit(solution)/shard_map/early_load/pallas_call | solution.py:762
  2.0 1.5 %first_state.1.refs_7_ = bf16[144,1280]{1,0:T(8,128)(2,1)S(1)} custom-call(s32[1]{0:T(128)} %bitcast.refs_0_.place_ref, f32[40,256]{1,0:T(8,128)S(1)} %get-tuple-element.80.refs_1_, bf16[256,1280]{1,0:T(8,128)(2,1)S(1)} %get-tuple-element.81.refs_2_, bf16[256,1280]{1,0:T(8,128)(2,1)S(1)} %get-tuple-element.82.refs_3_, ...), custom_call_target="tpu_custom_call" | custom-call | bytes 35000 | tf_op jit(solution)/shard_map/first_state/pallas_call | solution.py:762
  3.5 3.1 %collective-permute-start.1 = (bf16[144,1280]{1,0:T(8,128)(2,1)S(1)}, bf16[144,1280]{1,0:T(8,128)(2,1)S(1)}, u32[]{:S(2)}, u32[]{:S(2)}) collective-permute-start(bf16[144,1280]{1,0:T(8,128)(2,1)S(1)} %first_state.1.refs_7_), channel_id=1, source_target_pairs={{0,4},{12,8},{1,5},{13,9},{2,6},{14,10},{3,7},{15,11},{16,20},{28,... | collective-permute-start | bytes 1105928 | tf_op jit(solution)/shard_map/ppermute | solution.py:834
  6.6 1.8 %load.1 = (bf16[256,2560]{1,0:T(8,128)(2,1)S(1)}, bf16[256,256]{1,0:T(8,128)(2,1)S(1)}, bf16[256,2560]{1,0:T(8,128)(2,1)S(1)}, f32[40,256]{1,0:T(8,128)S(1)}, f3...) custom-call(bf16[256,2560]{1,0:T(8,128)(2,1)} %bitcast.11, bf16[256,256]{1,0:T(8,128)(2,1)} %bitcast.17, ...), custom_call_target="tpu_custom_call" | custom-call | bytes 35000 | tf_op jit(solution)/shard_map/load/pallas_call | solution.py:762
  8.7 1.1 %end_state.1.refs_13_ = bf16[144,1280]{1,0:T(8,128)(2,1)S(1)} custom-call(s32[1]{0:T(128)} %bitcast.refs_0_.place_ref, f32[40,256]{1,0:T(8,128)S(1)} %get-tuple-element.91.refs_1_.refs_4_, bf16[256,2560]{1,0:T(8,128)(2,1)S(1)} %get-tuple-element.87.refs_2_.refs_3_.refs_0_.refs_1_, bf16[256,2560]{1,0:T(8,128)(2,1)S(1)} %get-tuple-element.92.refs_3_.refs_1_, ...), custom_call_target="tpu_custom_call" | custom-call | bytes 35000 | tf_op jit(solution)/shard_map/end_state/pallas_call | solution.py:762
  9.9 1.7 %collective-permute-start.2 = (bf16[144,1280]{1,0:T(8,128)(2,1)S(1)}, bf16[144,1280]{1,0:T(8,128)(2,1)S(1)}, u32[]{:S(2)}, u32[]{:S(2)}) collective-permute-start(bf16[144,1280]{1,0:T(8,128)(2,1)S(1)} %end_state.1.refs_13_), channel_id=1, source_target_pairs={{0,4},{12,8},{1,5},{13,9},{2,6},{14,10},{3,7},{15,11},{16,20},{28,... | collective-permute-start | bytes 1105928 | tf_op jit(solution)/shard_map/ppermute | solution.py:834
  12.3 3.3 %collective-permute-done.1.refs_2_ = bf16[144,1280]{1,0:T(8,128)(2,1)S(1)} collective-permute-done((bf16[144,1280]{1,0:T(8,128)(2,1)S(1)}, bf16[144,1280]{1,0:T(8,128)(2,1)S(1)}, u32[]{:S(2)}, u32[]{:S(2)}) %collective-permute-start.1) | collective-permute-done | bytes 368672 | tf_op jit(solution)/shard_map/ppermute | solution.py:834
  16.3 2.2 %inside_block.3 = (f32[256,640]{1,0:T(8,128)S(1)}, f32[256,640]{1,0:T(8,128)S(1)}, bf16[256,640]{1,0:T(8,128)(2,1)S(1)}, bf16[256,640]{1,0:T(8,128)(2,1)S(1)}, b...) custom-call(bf16[256,2560]{1,0:T(8,128)(2,1)S(1)} %get-tuple-element., ...), custom_call_target="tpu_custom_call" | custom-call | bytes 9450000 | tf_op jit(solution)/shard_map/inside_block/pallas_call | solution.py:762
  18.6 3.7 %collective-permute-done.2.refs_4_ = bf16[144,1280]{1,0:T(8,128)(2,1)S(1)} collective-permute-done((bf16[144,1280]{1,0:T(8,128)(2,1)S(1)}, bf16[144,1280]{1,0:T(8,128)(2,1)S(1)}, u32[]{:S(2)}, u32[]{:S(2)}) %collective-permute-start.2) | collective-permute-done | bytes 368672 | tf_op jit(solution)/shard_map/ppermute | solution.py:834
  23.1 1.5 %collective-permute-start.5 = (bf16[128,1280]{1,0:T(8,128)(2,1)S(1)}, bf16[128,1280]{1,0:T(8,128)(2,1)S(1)}, u32[]{:S(2)}, u32[]{:S(2)}) collective-permute-start(bf16[128,1280]{1,0:T(8,128)(2,1)S(1)} %message.4.refs_8_), channel_id=1, source_target_pairs={{8,12},{4,0},{9,13},{5,1},{10,14},{6,2},{11,15},{7,3},{24,28},{20,... | collective-permute-start | bytes 983048 | tf_op jit(solution)/shard_map/ppermute | solution.py:834
  24.6 5.8 %inside_block.4 = (f32[256,1536]{1,0:T(8,128)S(1)}, f32[256,1536]{1,0:T(8,128)S(1)}, bf16[256,1536]{1,0:T(8,128)(2,1)S(1)}, bf16[256,1536]{1,0:T(8,128)(2,1)S(1)...) custom-call(bf16[256,2560]{1,0:T(8,128)(2,1)S(1)} %get-tuple-element, ...), custom_call_target="tpu_custom_call" | custom-call | bytes 9450000 | tf_op jit(solution)/shard_map/inside_block/pallas_call | solution.py:762
  30.5 1.3 %collective-permute-start.7 = (bf16[128,1280]{1,0:T(8,128)(2,1)S(1)}, bf16[128,1280]{1,0:T(8,128)(2,1)S(1)}, u32[]{:S(2)}, u32[]{:S(2)}) collective-permute-start(bf16[128,1280]{1,0:T(8,128)(2,1)S(1)} %message.5.refs_8_), channel_id=1, source_target_pairs={{8,12},{4,0},{9,13},{5,1},{10,14},{6,2},{11,15},{7,3},{24,28},{20,... | collective-permute-start | bytes 983048 | tf_op jit(solution)/shard_map/ppermute | solution.py:834
  31.8 1.3 %inside_block.5 = (f32[256,384]{1,0:T(8,128)S(1)}, f32[256,384]{1,0:T(8,128)S(1)}, bf16[256,384]{1,0:T(8,128)(2,1)S(1)}, bf16[256,384]{1,0:T(8,128)(2,1)S(1)}, b...) custom-call(bf16[256,2560]{1,0:T(8,128)(2,1)S(1)} %get-tuple-element., ...), custom_call_target="tpu_custom_call" | custom-call | bytes 9450000 | tf_op jit(solution)/shard_map/inside_block/pallas_call | solution.py:762
  33.4 1.3 %collective-permute-start.6 = (bf16[8,1280]{1,0:T(8,128)(2,1)S(1)}, bf16[8,1280]{1,0:T(8,128)(2,1)S(1)}, u32[]{:S(2)}, u32[]{:S(2)}) collective-permute-start(bf16[8,1280]{1,0:T(8,128)(2,1)S(1)} %edge.1.refs_4_.edge_ref), channel_id=1, source_target_pairs={{4,0},{8,4},{12,8},{5,1},{9,5},{13,9},{6,2},{10,6},{14,10},{7,3},{... | collective-permute-start | bytes 61448 | tf_op jit(solution)/shard_map/ppermute | solution.py:1003
  34.7 2.8 %collective-permute-done.5.refs_15_.refs_10_ = bf16[128,1280]{1,0:T(8,128)(2,1)S(1)} collective-permute-done((bf16[128,1280]{1,0:T(8,128)(2,1)S(1)}, bf16[128,1280]{1,0:T(8,128)(2,1)S(1)}, u32[]{:S(2)}, u32[]{:S(2)}) %collective-permute-start.5) | collective-permute-done | bytes 327712 | tf_op jit(solution)/shard_map/ppermute | solution.py:834
  37.5 2.3 %finish.2 = (bf16[256,2560]{1,0:T(8,128)(2,1)}, bf16[256,2560]{1,0:T(8,128)(2,1)}, f32[8,1280]{1,0:T(8,128)S(1)}, f32[16,1280]{1,0:T(8,128)S(1)}) custom-call(s32[1]{0:T(128)} %bitcast.refs_0_.place_ref, bf16[256,2560]{1,0:T(8,128)(2,1)S(1)} %get-tuple-element.87.refs_2_.refs_3_.refs_0_.refs_1_, ...), custom_call_target="tpu_custom_call" | custom-call | bytes 35000 | tf_op jit(solution)/shard_map/finish/pallas_call | solution.py:762
  40.6 4.8 %collective-permute-done.6.refs_3_.edge_ref = bf16[8,1280]{1,0:T(8,128)(2,1)S(1)} collective-permute-done((bf16[8,1280]{1,0:T(8,128)(2,1)S(1)}, bf16[8,1280]{1,0:T(8,128)(2,1)S(1)}, u32[]{:S(2)}, u32[]{:S(2)}) %collective-permute-start.6) | collective-permute-done | bytes 20512 | tf_op jit(solution)/shard_map/ppermute | solution.py:1003
  46.1 1.2 %collective-permute-done.8.small_dp = f32[8,384]{1,0:T(8,128)S(1)} collective-permute-done((f32[8,384]{1,0:T(8,128)S(1)}, f32[8,384]{1,0:T(8,128)S(1)}, u32[]{:S(2)}, u32[]{:S(2)}) %collective-permute-start.8) | collective-permute-done | bytes 12320 | tf_op jit(solution)/shard_map/ppermute | solution.py:1059
  47.3 1.6 %collective-permute-start.10 = (bf16[272,256]{1,0:T(8,128)(2,1)S(1)}, bf16[272,256]{1,0:T(8,128)(2,1)S(1)}, u32[]{:S(2)}, u32[]{:S(2)}) collective-permute-start(bf16[272,256]{1,0:T(8,128)(2,1)S(1)} %get-tuple-element.138.refs_4_), channel_id=1, source_target_pairs={{0,2},{2,0},{1,3},{3,1},{4,6},{6,4},{5,7},{7,5},{8,10},{10,8},{9,1... | collective-permute-start | bytes 417800 | tf_op jit(solution)/shard_map/ppermute | solution.py:1062
  48.8 2.3 %finish.3 = (bf16[256,2560]{1,0:T(8,128)(2,1)}, bf16[256,2560]{1,0:T(8,128)(2,1)}, f32[8,1280]{1,0:T(8,128)S(1)}, f32[16,1280]{1,0:T(8,128)S(1)}) custom-call(s32[1]{0:T(128)} %bitcast.refs_0_.place_ref, bf16[256,2560]{1,0:T(8,128)(2,1)S(1)} %get-tuple-element.87.refs_2_.refs_3_.refs_0_.refs_1_, ...), custom_call_target="tpu_custom_call", output_to_operand_aliasing={{0}: (16, {}), {1}: (17, {})} | custom-call | bytes 35000 | tf_op jit(solution)/shard_map/finish/pallas_call | solution.py:762
  51.3 1.3 %collective-permute-done.9.refs_1_ = f32[8,2560]{1,0:T(8,128)S(1)} collective-permute-done((f32[8,2560]{1,0:T(8,128)S(1)}, f32[8,2560]{1,0:T(8,128)S(1)}, u32[]{:S(2)}, u32[]{:S(2)}) %collective-permute-start.9) | collective-permute-done | bytes 81952 | tf_op jit(solution)/shard_map/ppermute | solution.py:1072
  53.2 2.3 %collective-permute-start.12 = (bf16[8,1664]{1,0:T(8,128)(2,1)S(1)}, bf16[8,1664]{1,0:T(8,128)(2,1)S(1)}, u32[]{:S(2)}, u32[]{:S(2)}) collective-permute-start(bf16[8,1664]{1,0:T(8,128)(2,1)S(1)} %get-tuple-element.147._.refs_1_), channel_id=1, source_target_pairs={{0,8},{4,12},{8,0},{12,4},{1,9},{5,13},{9,1},{13,5},{2,10},{6,14},... | collective-permute-start | bytes 79880 | tf_op jit(solution)/shard_map/ppermute | solution.py:1090
  55.5 1.6 %collective-permute-start.13 = (bf16[8,1664]{1,0:T(8,128)(2,1)S(1)}, bf16[8,1664]{1,0:T(8,128)(2,1)S(1)}, u32[]{:S(2)}, u32[]{:S(2)}) collective-permute-start(bf16[8,1664]{1,0:T(8,128)(2,1)S(1)} %get-tuple-element.147._.refs_1_), channel_id=1, source_target_pairs={{0,12},{4,0},{8,4},{12,8},{1,13},{5,1},{9,5},{13,9},{2,14},{6,2},{... | collective-permute-start | bytes 79880 | tf_op jit(solution)/shard_map/ppermute | solution.py:1090
  57.9 1.0 %collective-permute-done.11.refs_4_ = bf16[8,1664]{1,0:T(8,128)(2,1)S(1)} collective-permute-done((bf16[8,1664]{1,0:T(8,128)(2,1)S(1)}, bf16[8,1664]{1,0:T(8,128)(2,1)S(1)}, u32[]{:S(2)}, u32[]{:S(2)}) %collective-permute-start.11) | collective-permute-done | bytes 26656 | tf_op jit(solution)/shard_map/ppermute | solution.py:1090
  (28 shorter events, 7.2 us)
Async XLA Ops:
  3.5 12.0 %collective-permute-start.1 = (bf16[144,1280]{1,0:T(8,128)(2,1)S(1)}, bf16[144,1280]{1,0:T(8,128)(2,1)S(1)}, u32[]{:S(2)}, u32[]{:S(2)}) collective-permute-start(bf16[144,1280]{1,0:T(8,128)(2,1)S(1)} %first_state.1.refs_7_), channel_id=1, source_target_pairs={{0,4},{12,8},{1,5},{13,9},{2,6},{14,10},{3,7},{15,11},{16,20},{28,... | collective-permute-start | bytes 1105928 | tf_op jit(solution)/shard_map/ppermute | solution.py:834
  9.9 12.4 %collective-permute-start.2 = (bf16[144,1280]{1,0:T(8,128)(2,1)S(1)}, bf16[144,1280]{1,0:T(8,128)(2,1)S(1)}, u32[]{:S(2)}, u32[]{:S(2)}) collective-permute-start(bf16[144,1280]{1,0:T(8,128)(2,1)S(1)} %end_state.1.refs_13_), channel_id=1, source_target_pairs={{0,4},{12,8},{1,5},{13,9},{2,6},{14,10},{3,7},{15,11},{16,20},{28,... | collective-permute-start | bytes 1105928 | tf_op jit(solution)/shard_map/ppermute | solution.py:834
  11.6 0.7 %collective-permute-start = (bf16[8,2816]{1,0:T(8,128)(2,1)S(1)}, bf16[8,2816]{1,0:T(8,128)(2,1)S(1)}, u32[]{:S(2)}, u32[]{:S(2)}) collective-permute-start(bf16[8,2816]{1,0:T(8,128)(2,1)S(1)} %get-tuple-element.86.refs_7_), channel_id=1, source_target_pairs={{4,8},{8,12},{5,9},{9,13},{6,10},{10,14},{7,11},{11,15},{20,24},{2... | collective-permute-start | bytes 135176 | tf_op jit(solution)/shard_map/ppermute | solution.py:868
  15.6 7.4 %collective-permute-start.4 = (bf16[128,1280]{1,0:T(8,128)(2,1)S(1)}, bf16[128,1280]{1,0:T(8,128)(2,1)S(1)}, u32[]{:S(2)}, u32[]{:S(2)}) collective-permute-start(bf16[128,1280]{1,0:T(8,128)(2,1)S(1)} %get-tuple-element.103.refs_8_), channel_id=1, source_target_pairs={{4,8},{8,4},{5,9},{9,5},{6,10},{10,6},{7,11},{11,7},{20,24},{24,20... | collective-permute-start | bytes 983048 | tf_op jit(solution)/shard_map/ppermute | solution.py:834
  22.3 8.1 %collective-permute-start.3 = (bf16[128,1280]{1,0:T(8,128)(2,1)S(1)}, bf16[128,1280]{1,0:T(8,128)(2,1)S(1)}, u32[]{:S(2)}, u32[]{:S(2)}) collective-permute-start(bf16[128,1280]{1,0:T(8,128)(2,1)S(1)} %get-tuple-element.108._), channel_id=1, source_target_pairs={{4,8},{8,4},{5,9},{9,5},{6,10},{10,6},{7,11},{11,7},{20,24},{24,20... | collective-permute-start | bytes 983048 | tf_op jit(solution)/shard_map/ppermute | solution.py:834
  23.1 14.4 %collective-permute-start.5 = (bf16[128,1280]{1,0:T(8,128)(2,1)S(1)}, bf16[128,1280]{1,0:T(8,128)(2,1)S(1)}, u32[]{:S(2)}, u32[]{:S(2)}) collective-permute-start(bf16[128,1280]{1,0:T(8,128)(2,1)S(1)} %message.4.refs_8_), channel_id=1, source_target_pairs={{8,12},{4,0},{9,13},{5,1},{10,14},{6,2},{11,15},{7,3},{24,28},{20,... | collective-permute-start | bytes 983048 | tf_op jit(solution)/shard_map/ppermute | solution.py:834
  30.5 14.8 %collective-permute-start.7 = (bf16[128,1280]{1,0:T(8,128)(2,1)S(1)}, bf16[128,1280]{1,0:T(8,128)(2,1)S(1)}, u32[]{:S(2)}, u32[]{:S(2)}) collective-permute-start(bf16[128,1280]{1,0:T(8,128)(2,1)S(1)} %message.5.refs_8_), channel_id=1, source_target_pairs={{8,12},{4,0},{9,13},{5,1},{10,14},{6,2},{11,15},{7,3},{24,28},{20,... | collective-permute-start | bytes 983048 | tf_op jit(solution)/shard_map/ppermute | solution.py:834
  33.4 11.9 %collective-permute-start.6 = (bf16[8,1280]{1,0:T(8,128)(2,1)S(1)}, bf16[8,1280]{1,0:T(8,128)(2,1)S(1)}, u32[]{:S(2)}, u32[]{:S(2)}) collective-permute-start(bf16[8,1280]{1,0:T(8,128)(2,1)S(1)} %edge.1.refs_4_.edge_ref), channel_id=1, source_target_pairs={{4,0},{8,4},{12,8},{5,1},{9,5},{13,9},{6,2},{10,6},{14,10},{7,3},{... | collective-permute-start | bytes 61448 | tf_op jit(solution)/shard_map/ppermute | solution.py:1003
  46.0 1.2 %collective-permute-start.8 = (f32[8,384]{1,0:T(8,128)S(1)}, f32[8,384]{1,0:T(8,128)S(1)}, u32[]{:S(2)}, u32[]{:S(2)}) collective-permute-start(f32[8,384]{1,0:T(8,128)S(1)} %get-tuple-element.137.small_ref), channel_id=1, source_target_pairs={{0,1},{1,0},{2,3},{3,2},{4,5},{5,4},{6,7},{7,6},{8,9},{9,8},{10,11... | collective-permute-start | bytes 36872 | tf_op jit(solution)/shard_map/ppermute | solution.py:1059
  47.3 5.8 %collective-permute-start.10 = (bf16[272,256]{1,0:T(8,128)(2,1)S(1)}, bf16[272,256]{1,0:T(8,128)(2,1)S(1)}, u32[]{:S(2)}, u32[]{:S(2)}) collective-permute-start(bf16[272,256]{1,0:T(8,128)(2,1)S(1)} %get-tuple-element.138.refs_4_), channel_id=1, source_target_pairs={{0,2},{2,0},{1,3},{3,1},{4,6},{6,4},{5,7},{7,5},{8,10},{10,8},{9,1... | collective-permute-start | bytes 417800 | tf_op jit(solution)/shard_map/ppermute | solution.py:1062
  51.2 1.3 %collective-permute-start.9 = (f32[8,2560]{1,0:T(8,128)S(1)}, f32[8,2560]{1,0:T(8,128)S(1)}, u32[]{:S(2)}, u32[]{:S(2)}) collective-permute-start(f32[8,2560]{1,0:T(8,128)S(1)} %sums.1.refs_0_), channel_id=1, source_target_pairs={{0,1},{1,0},{2,3},{3,2},{4,5},{5,4},{6,7},{7,6},{8,9},{9,8},{10,11... | collective-permute-start | bytes 245768 | tf_op jit(solution)/shard_map/ppermute | solution.py:1072
  53.1 5.7 %collective-permute-start.11 = (bf16[8,1664]{1,0:T(8,128)(2,1)S(1)}, bf16[8,1664]{1,0:T(8,128)(2,1)S(1)}, u32[]{:S(2)}, u32[]{:S(2)}) collective-permute-start(bf16[8,1664]{1,0:T(8,128)(2,1)S(1)} %get-tuple-element.147._.refs_1_), channel_id=1, source_target_pairs={{0,4},{4,8},{8,12},{12,0},{1,5},{5,9},{9,13},{13,1},{2,6},{6,10},{... | collective-permute-start | bytes 79880 | tf_op jit(solution)/shard_map/ppermute | solution.py:1090
  53.2 5.7 %collective-permute-start.12 = (bf16[8,1664]{1,0:T(8,128)(2,1)S(1)}, bf16[8,1664]{1,0:T(8,128)(2,1)S(1)}, u32[]{:S(2)}, u32[]{:S(2)}) collective-permute-start(bf16[8,1664]{1,0:T(8,128)(2,1)S(1)} %get-tuple-element.147._.refs_1_), channel_id=1, source_target_pairs={{0,8},{4,12},{8,0},{12,4},{1,9},{5,13},{9,1},{13,5},{2,10},{6,14},... | collective-permute-start | bytes 79880 | tf_op jit(solution)/shard_map/ppermute | solution.py:1090
  55.5 3.9 %collective-permute-start.13 = (bf16[8,1664]{1,0:T(8,128)(2,1)S(1)}, bf16[8,1664]{1,0:T(8,128)(2,1)S(1)}, u32[]{:S(2)}, u32[]{:S(2)}) collective-permute-start(bf16[8,1664]{1,0:T(8,128)(2,1)S(1)} %get-tuple-element.147._.refs_1_), channel_id=1, source_target_pairs={{0,12},{4,0},{8,4},{12,8},{1,13},{5,1},{9,5},{13,9},{2,14},{6,2},{... | collective-permute-start | bytes 79880 | tf_op jit(solution)/shard_map/ppermute | solution.py:1090

commit v5 on v4

--- a/solution.py
+++ b/solution.py
@@ -15,6 +15,7 @@
 bf16 = jnp.bfloat16
 HIGHEST = lax.Precision.HIGHEST
 ROWS16 = 16
+MORE = 8
 VMEM_LIMIT = 24 * 1024 * 1024
 
 
@@ -168,26 +169,30 @@
     return (pre * sigmoid(pre)).astype(bf16)
 
 
-def put_first_rows(pay_ref, lg, bc_ref, taps):
-    state = pay_ref.shape[0] - ROWS16
-    width, bcw = lg.shape[1], bc_ref.shape[1]
-    bc8 = bc_ref[0:ROWS16, :].astype(f32)[0:8]
-    bc8 = jnp.concatenate([bc8, jnp.zeros((8, width - bcw), f32)], axis=1)
-    lg8 = lg[0:ROWS16, :].astype(f32)[0:8]
-    pay_ref[state:, :] = jnp.concatenate([lg8, bc8], axis=0).astype(bf16)
+def put_first_rows(pay_ref, lg, bc_ref, more):
+    state = pay_ref.shape[0] - MORE
+    bcw = bc_ref.shape[1]
+    more[0:4, :] = lg[0:ROWS16, :].astype(f32)[0:4]
+    more[4:8, 0:bcw] = bc_ref[0:ROWS16, :].astype(f32)[0:4]
+    more[4:8, bcw:] = jnp.zeros((4, lg.shape[1] - bcw), f32)
+    pay_ref[state:, :] = more[...].astype(bf16)
 
 
 def first_rows_state(more, bc_ref, wbc_ref, bcpad):
     rows, bcw = bc_ref.shape
     state = bcw // 2
     taps = wbc_ref.shape[0]
-    zeros = jnp.zeros((8, state), f32)
+    zeros = jnp.zeros((ROWS16 - 4, state), f32)
     edge = bc_ref[rows - ROWS16 :, state:].astype(f32)[ROWS16 - HALO :]
-    block = jnp.concatenate([more[8:16, state:bcw], zeros], axis=0)
+    block = jnp.concatenate([more[4:8, state:bcw], zeros], axis=0)
     c = mapped_half(1, state, ROWS16, block, edge, wbc_ref, bcpad)
     early = lax.broadcasted_iota(jnp.int32, c.shape, 0) < taps - 1
-    lg = jnp.concatenate([more[0:8, :], jnp.zeros((8, more.shape[1]), f32)], axis=0)
+    lg = jnp.concatenate([more[0:4, :], jnp.zeros((ROWS16 - 4, more.shape[1]), f32)], axis=0)
     return state_of(jnp.where(early, c, jnp.zeros_like(c)), lg.astype(bf16))
+
+
+def bc_tail_place(r, taps, bcw):
+    return 2 * taps - 2 + r // 2, slice((r % 2) * bcw, (r % 2 + 1) * bcw)
 
 
 def first_state_kernel(count, scale, *refs):
@@ -207,9 +212,11 @@
         weighted_tails(0, 0, xa_ref, wx_ref, lambda _: none, gt, pad, lw)
         pay_ref[0:state, :] = state_of(b, lw[...]).astype(bf16)
         tails[...] = tails_ref[...].astype(f32)
-        more[0:8, :] = tails[:, 0:width]
-        more[8:16, :] = tails[:, width : 2 * width]
-        more[8 : 7 + taps, 0:bcw] = tails[HALO - taps + 1 :, 2 * width :]
+        more[0 : taps - 1, :] = tails[HALO - taps + 1 :, 0:width]
+        more[taps - 1 : 2 * taps - 2, :] = tails[HALO - taps + 1 :, width : 2 * width]
+        for r in range(taps - 1):
+            at, here = bc_tail_place(r, taps, bcw)
+            more[at : at + 1, here] = tails[HALO - taps + 1 + r :, 2 * width :][0:1]
         pay_ref[state:, :] = more[...].astype(bf16)
 
     @pl.when(place == count - 1)
@@ -219,7 +226,7 @@
         late = lax.broadcasted_iota(jnp.int32, c.shape, 0) >= taps - 1
         led_gradients(0, 0, ga_ref, sl, lg)
         pay_ref[0:state, :] = state_of(jnp.where(late, c, jnp.zeros_like(c)), lg[...]).astype(bf16)
-        put_first_rows(pay_ref, lg, bc_ref, taps)
+        put_first_rows(pay_ref, lg, bc_ref, more)
 
 
 def middle_first_kernel(count, scale, *refs):
@@ -272,9 +279,12 @@
 
     @pl.when(place == 1)
     def _():
-        halo[:, 0:width] = more[0:8, :]
-        halo[:, width : 2 * width] = more[8:16, :]
-        halo[HALO - taps + 1 :, 2 * width :] = more[8 : 7 + taps, 0:bcw]
+        halo[HALO - taps + 1 :, 0:width] = more[0 : taps - 1, :]
+        halo[HALO - taps + 1 :, width : 2 * width] = more[taps - 1 : 2 * taps - 2, :]
+        for r in range(taps - 1):
+            at, here = bc_tail_place(r, taps, bcw)
+            row = HALO - taps + 1 + r
+            halo[row : row + 1, 2 * width :] = more[at : at + 1, here]
 
     halo_ref[...] = halo[...].astype(bf16)
     map_ref[...] = map_in[...]
@@ -346,7 +356,7 @@
 
 def end_state_kernel(count, start, heads_at, scale, *refs):
     place_ref, dec_ref, x_ref, g_ref, wx_ref, bc_ref, cum_ref, map_ref, _ = refs[:9]
-    pay_ref, pad, gt, sl, lw, lg = refs[9:]
+    pay_ref, pad, gt, sl, lw, lg, more = refs[9:]
     state = map_ref.shape[1] // 2
     taps = wx_ref.shape[0]
     place = place_ref[0]
@@ -365,7 +375,7 @@
         c = map_ref[:, state:]
         late = lax.broadcasted_iota(jnp.int32, c.shape, 0) >= taps - 1
         pay_ref[0:state, :] = state_of(jnp.where(late, c, jnp.zeros_like(c)), lg[...]).astype(bf16)
-        put_first_rows(pay_ref, lg, bc_ref, taps)
+        put_first_rows(pay_ref, lg, bc_ref, more)
 
 
 def message_kernel(hop, place_ref, u_ref, v_ref, tot_ref, came_ref, _, out_ref):
@@ -666,7 +676,7 @@
     run_copies([pltpu.make_async_copy(gx16, gx_hbm.at[tail, :], sem.at[0])])
 
 
-def pack_kernel(own_ref, small_ref, small_dp, small_out, head_ref):
+def pack_kernel(own_ref, small_ref, small_dp, _, small_out, head_ref):
     rows, bcw = own_ref.shape
     small = small_ref[...] + small_dp[...]
     small_out[...] = small
@@ -852,9 +862,9 @@
         functools.partial(first_state_kernel, count, scale),
         "first_state",
         [where_am_i, made[0], xa, ga, *made[1:], tails],
-        [shape((state + ROWS16, width), bf16)],
+        [shape((state + MORE, width), bf16)],
         state_scratch
-        + [vmem((rows + HALO, LANES)), vmem((HALO, inner + bcw)), vmem((ROWS16, width))],
+        + [vmem((rows + HALO, LANES)), vmem((HALO, inner + bcw)), vmem((MORE, width))],
     )[0]
     hop_on(0, pay)
     sources = [x, bc, g, dec, conv_x, conv_bc, skip]
@@ -942,8 +952,8 @@
         functools.partial(end_state_kernel, count, width, width // head_dim, scale),
         "end_state",
         [where_am_i, dec, x, g, conv_x, bc, cum, mapped, (u, "any")],
-        [shape((state + ROWS16, width), bf16)],
-        state_scratch,
+        [shape((state + MORE, width), bf16)],
+        state_scratch + [vmem((MORE, width))],
     )[0]
     hop_on(1, after)
     halo, mapped, u, v, came, after = call(
@@ -961,7 +971,7 @@
         ],
         [
             vmem((HALO, inner + bcw)),
-            vmem((ROWS16, width)),
+            vmem((MORE, width)),
             padded(pairs, ROWS16),
             padded(2, ROWS16),
         ],
@@ -982,7 +992,7 @@
                     "message",
                     [where_am_i, *states[1], received[1][0], bc, conv_bc, (after, "any")],
                     [shape((state, width), bf16), shape((state, width), bf16)],
-                    [vmem((ROWS16, width)), vmem((ROWS16 + HALO, LANES))],
+                    [vmem((MORE, width)), vmem((ROWS16 + HALO, LANES))],
                 )
                 received[1][0] = came
                 hop_on(1, after)
@@ -1049,14 +1059,14 @@
 
     outs, taps_a, end_a = finish(0, edge, None)
     dbc = finish_bc(0, dsim, taps_a)[0]
-    own, small = finish_bc(1, dbc, edges)
+    own, small = finish_bc(1, dbc, dbc)
 
     swap = [(0, 1), (1, 0)]
     turns = [[(i, (i + k) % head_count) for i in range(head_count)] for k in range(1, head_count)]
     small, to_heads = call(
         pack_kernel,
         "pack",
-        [own, small, lax.ppermute(small, "dp", swap)],
+        [own, small, lax.ppermute(small, "dp", swap), (edges, "any")],
         [shape(small.shape), shape((rows + ROWS16, bcw), bf16)],
     )
     others = [lax.ppermute(to_heads, "head", turn) for turn in turns]

time: 60.4 us -> 59.8 us (0.990)
  waiting for transfers between devices: 19.1 us -> 18.3 us
    ppermute x1, waiting for transfers between devices: 4.78 us -> 0.01 us  [local(): edges = lax.ppermute(edge, 'seq', [(i + 1, i) for i in range(count - 1)])]
    ppermute x6, waiting for transfers between devices: 9.79 us -> 13.5 us  [hop_on(): received[c].append(lax.ppermute(message, 'seq', routes))]
  transfers between devices with their start and end apart: 14 -> 14, of which waited for: 9 -> 9; matrix products, arithmetic and copies ran while one was open for 0% -> 0% of each run, Pallas kernels for 32% -> 34%
where the time goes in v5:
time: 59.8 us; the launch traced here: 59.5 us
  Pallas kernels  23.7 us (40%)
  waiting for transfers between devices  18.3 us (31%)
  starting transfers between devices  16.6 us (28%)
  between operations  0.9 us (2%)
    pallas_call x24, Pallas kernels, call(): pl.pallas_call(kernel, grid=grid, in_specs=[spec(i) for i in ins], out_sp...  23.7 us
    ppermute x6, waiting for transfers between devices, hop_on(): received[c].append(lax.ppermute(message, 'seq', routes))  13.5 us
    ppermute x6, starting transfers between devices, hop_on(): received[c].append(lax.ppermute(message, 'seq', routes))  8.88 us
    ppermute x3, starting transfers between devices, local(): lax.ppermute(to_seq, 'seq', [(i, (i + k) % count) for i in range(count)])  4.02 us
    ppermute x3, waiting for transfers between devices, local(): lax.ppermute(to_seq, 'seq', [(i, (i + k) % count) for i in range(count)])  1.82 us
    ppermute x1, starting transfers between devices, local(): others = [lax.ppermute(to_heads, 'head', turn) for turn in turns]  1.56 us
    ppermute x1, starting transfers between devices, local(): edges = lax.ppermute(edge, 'seq', [(i + 1, i) for i in range(count - 1)])  1.29 us
    ppermute x1, waiting for transfers between devices, local(): sums_dp = lax.ppermute(sums, 'dp', swap)  1.26 us
  transfers between devices with their start and end apart: 14, of which 9 were waited for; matrix products, arithmetic and copies ran while one was open for 0% of the time, Pallas kernels for 34%

profile of v5, /device:TPU:0, one launch (start us, length us, event | category | flops | bytes accessed | tf_op | source)
XLA Modules:
  0.0 59.5 jit_solution(4701591412314540576)
XLA Ops:
  0.6 1.4 %early_load.1 = (bf16[256,1280]{1,0:T(8,128)(2,1)S(1)}, bf16[256,1280]{1,0:T(8,128)(2,1)S(1)}, f32[40,256]{1,0:T(8,128)S(1)}, f32[4,2560]{1,0:T(4,128)S(1)}, bf1...) custom-call(s32[1]{0:T(128)} %bitcast.refs_0_.place_ref, bf16[256,2560]{1,0:T(8,128)(2,1)} %bitcast.10, ...), custom_call_target="tpu_custom_call" | custom-call | bytes 35000 | tf_op jit(solution)/shard_map/early_load/pallas_call | solution.py:772
  2.0 1.5 %first_state.1.refs_7_ = bf16[136,1280]{1,0:T(8,128)(2,1)S(1)} custom-call(s32[1]{0:T(128)} %bitcast.refs_0_.place_ref, f32[40,256]{1,0:T(8,128)S(1)} %get-tuple-element.80.refs_1_, bf16[256,1280]{1,0:T(8,128)(2,1)S(1)} %get-tuple-element.81.refs_2_, bf16[256,1280]{1,0:T(8,128)(2,1)S(1)} %get-tuple-element.82.refs_3_, ...), custom_call_target="tpu_custom_call" | custom-call | bytes 35000 | tf_op jit(solution)/shard_map/first_state/pallas_call | solution.py:772
  3.5 3.1 %collective-permute-start.1 = (bf16[136,1280]{1,0:T(8,128)(2,1)S(1)}, bf16[136,1280]{1,0:T(8,128)(2,1)S(1)}, u32[]{:S(2)}, u32[]{:S(2)}) collective-permute-start(bf16[136,1280]{1,0:T(8,128)(2,1)S(1)} %first_state.1.refs_7_), channel_id=1, source_target_pairs={{0,4},{12,8},{1,5},{13,9},{2,6},{14,10},{3,7},{15,11},{16,20},{28,... | collective-permute-start | bytes 1044488 | tf_op jit(solution)/shard_map/ppermute | solution.py:844
  6.6 1.8 %load.1 = (bf16[256,2560]{1,0:T(8,128)(2,1)S(1)}, bf16[256,256]{1,0:T(8,128)(2,1)S(1)}, bf16[256,2560]{1,0:T(8,128)(2,1)S(1)}, f32[40,256]{1,0:T(8,128)S(1)}, f3...) custom-call(bf16[256,2560]{1,0:T(8,128)(2,1)} %bitcast.11, bf16[256,256]{1,0:T(8,128)(2,1)} %bitcast.17, ...), custom_call_target="tpu_custom_call" | custom-call | bytes 35000 | tf_op jit(solution)/shard_map/load/pallas_call | solution.py:772
  8.7 1.1 %end_state.1.refs_13_ = bf16[136,1280]{1,0:T(8,128)(2,1)S(1)} custom-call(s32[1]{0:T(128)} %bitcast.refs_0_.place_ref, f32[40,256]{1,0:T(8,128)S(1)} %get-tuple-element.91.refs_1_.refs_4_, bf16[256,2560]{1,0:T(8,128)(2,1)S(1)} %get-tuple-element.87.refs_2_.refs_3_.refs_0_.refs_1_, bf16[256,2560]{1,0:T(8,128)(2,1)S(1)} %get-tuple-element.92.refs_3_.refs_1_, ...), custom_call_target="tpu_custom_call" | custom-call | bytes 35000 | tf_op jit(solution)/shard_map/end_state/pallas_call | solution.py:772
  9.9 1.7 %collective-permute-start.2 = (bf16[136,1280]{1,0:T(8,128)(2,1)S(1)}, bf16[136,1280]{1,0:T(8,128)(2,1)S(1)}, u32[]{:S(2)}, u32[]{:S(2)}) collective-permute-start(bf16[136,1280]{1,0:T(8,128)(2,1)S(1)} %end_state.1.refs_13_), channel_id=1, source_target_pairs={{0,4},{12,8},{1,5},{13,9},{2,6},{14,10},{3,7},{15,11},{16,20},{28,... | collective-permute-start | bytes 1044488 | tf_op jit(solution)/shard_map/ppermute | solution.py:844
  12.3 2.8 %collective-permute-done.1.refs_2_ = bf16[136,1280]{1,0:T(8,128)(2,1)S(1)} collective-permute-done((bf16[136,1280]{1,0:T(8,128)(2,1)S(1)}, bf16[136,1280]{1,0:T(8,128)(2,1)S(1)}, u32[]{:S(2)}, u32[]{:S(2)}) %collective-permute-start.1) | collective-permute-done | bytes 348192 | tf_op jit(solution)/shard_map/ppermute | solution.py:844
  15.9 2.2 %inside_block.3 = (f32[256,640]{1,0:T(8,128)S(1)}, f32[256,640]{1,0:T(8,128)S(1)}, bf16[256,640]{1,0:T(8,128)(2,1)S(1)}, bf16[256,640]{1,0:T(8,128)(2,1)S(1)}, b...) custom-call(bf16[256,2560]{1,0:T(8,128)(2,1)S(1)} %get-tuple-element., ...), custom_call_target="tpu_custom_call" | custom-call | bytes 9450000 | tf_op jit(solution)/shard_map/inside_block/pallas_call | solution.py:772
  18.1 3.3 %collective-permute-done.2.refs_4_ = bf16[136,1280]{1,0:T(8,128)(2,1)S(1)} collective-permute-done((bf16[136,1280]{1,0:T(8,128)(2,1)S(1)}, bf16[136,1280]{1,0:T(8,128)(2,1)S(1)}, u32[]{:S(2)}, u32[]{:S(2)}) %collective-permute-start.2) | collective-permute-done | bytes 348192 | tf_op jit(solution)/shard_map/ppermute | solution.py:844
  22.3 1.5 %collective-permute-start.5 = (bf16[128,1280]{1,0:T(8,128)(2,1)S(1)}, bf16[128,1280]{1,0:T(8,128)(2,1)S(1)}, u32[]{:S(2)}, u32[]{:S(2)}) collective-permute-start(bf16[128,1280]{1,0:T(8,128)(2,1)S(1)} %message.4.refs_8_), channel_id=1, source_target_pairs={{8,12},{4,0},{9,13},{5,1},{10,14},{6,2},{11,15},{7,3},{24,28},{20,... | collective-permute-start | bytes 983048 | tf_op jit(solution)/shard_map/ppermute | solution.py:844
  23.8 5.8 %inside_block.4 = (f32[256,1536]{1,0:T(8,128)S(1)}, f32[256,1536]{1,0:T(8,128)S(1)}, bf16[256,1536]{1,0:T(8,128)(2,1)S(1)}, bf16[256,1536]{1,0:T(8,128)(2,1)S(1)...) custom-call(bf16[256,2560]{1,0:T(8,128)(2,1)S(1)} %get-tuple-element, ...), custom_call_target="tpu_custom_call" | custom-call | bytes 9450000 | tf_op jit(solution)/shard_map/inside_block/pallas_call | solution.py:772
  29.7 1.3 %collective-permute-start.6 = (bf16[128,1280]{1,0:T(8,128)(2,1)S(1)}, bf16[128,1280]{1,0:T(8,128)(2,1)S(1)}, u32[]{:S(2)}, u32[]{:S(2)}) collective-permute-start(bf16[128,1280]{1,0:T(8,128)(2,1)S(1)} %message.5.refs_8_), channel_id=1, source_target_pairs={{8,12},{4,0},{9,13},{5,1},{10,14},{6,2},{11,15},{7,3},{24,28},{20,... | collective-permute-start | bytes 983048 | tf_op jit(solution)/shard_map/ppermute | solution.py:844
  31.0 1.3 %inside_block.5 = (f32[256,384]{1,0:T(8,128)S(1)}, f32[256,384]{1,0:T(8,128)S(1)}, bf16[256,384]{1,0:T(8,128)(2,1)S(1)}, bf16[256,384]{1,0:T(8,128)(2,1)S(1)}, b...) custom-call(bf16[256,2560]{1,0:T(8,128)(2,1)S(1)} %get-tuple-element., ...), custom_call_target="tpu_custom_call" | custom-call | bytes 9450000 | tf_op jit(solution)/shard_map/inside_block/pallas_call | solution.py:772
  32.6 1.3 %collective-permute-start.8 = (bf16[8,1280]{1,0:T(8,128)(2,1)S(1)}, bf16[8,1280]{1,0:T(8,128)(2,1)S(1)}, u32[]{:S(2)}, u32[]{:S(2)}) collective-permute-start(bf16[8,1280]{1,0:T(8,128)(2,1)S(1)} %edge.1.refs_4_.edge_ref), channel_id=1, source_target_pairs={{4,0},{8,4},{12,8},{5,1},{9,5},{13,9},{6,2},{10,6},{14,10},{7,3},{... | collective-permute-start | bytes 61448 | tf_op jit(solution)/shard_map/ppermute | solution.py:1013
  33.9 2.8 %collective-permute-done.5.refs_15_.refs_10_ = bf16[128,1280]{1,0:T(8,128)(2,1)S(1)} collective-permute-done((bf16[128,1280]{1,0:T(8,128)(2,1)S(1)}, bf16[128,1280]{1,0:T(8,128)(2,1)S(1)}, u32[]{:S(2)}, u32[]{:S(2)}) %collective-permute-start.5) | collective-permute-done | bytes 327712 | tf_op jit(solution)/shard_map/ppermute | solution.py:844
  36.7 2.3 %finish.2 = (bf16[256,2560]{1,0:T(8,128)(2,1)}, bf16[256,2560]{1,0:T(8,128)(2,1)}, f32[8,1280]{1,0:T(8,128)S(1)}, f32[16,1280]{1,0:T(8,128)S(1)}) custom-call(s32[1]{0:T(128)} %bitcast.refs_0_.place_ref, bf16[256,2560]{1,0:T(8,128)(2,1)S(1)} %get-tuple-element.87.refs_2_.refs_3_.refs_0_.refs_1_, ...), custom_call_target="tpu_custom_call" | custom-call | bytes 35000 | tf_op jit(solution)/shard_map/finish/pallas_call | solution.py:772
  39.7 4.6 %collective-permute-done.6.refs_10_.refs_15_ = bf16[128,1280]{1,0:T(8,128)(2,1)S(1)} collective-permute-done((bf16[128,1280]{1,0:T(8,128)(2,1)S(1)}, bf16[128,1280]{1,0:T(8,128)(2,1)S(1)}, u32[]{:S(2)}, u32[]{:S(2)}) %collective-permute-start.6) | collective-permute-done | bytes 327712 | tf_op jit(solution)/shard_map/ppermute | solution.py:844
  45.0 1.2 %collective-permute-done.7.small_dp = f32[8,384]{1,0:T(8,128)S(1)} collective-permute-done((f32[8,384]{1,0:T(8,128)S(1)}, f32[8,384]{1,0:T(8,128)S(1)}, u32[]{:S(2)}, u32[]{:S(2)}) %collective-permute-start.7) | collective-permute-done | bytes 12320 | tf_op jit(solution)/shard_map/ppermute | solution.py:1069
  46.2 1.6 %collective-permute-start.10 = (bf16[272,256]{1,0:T(8,128)(2,1)S(1)}, bf16[272,256]{1,0:T(8,128)(2,1)S(1)}, u32[]{:S(2)}, u32[]{:S(2)}) collective-permute-start(bf16[272,256]{1,0:T(8,128)(2,1)S(1)} %get-tuple-element.138.refs_4_), channel_id=1, source_target_pairs={{0,2},{2,0},{1,3},{3,1},{4,6},{6,4},{5,7},{7,5},{8,10},{10,8},{9,1... | collective-permute-start | bytes 417800 | tf_op jit(solution)/shard_map/ppermute | solution.py:1072
  47.8 2.3 %finish.3 = (bf16[256,2560]{1,0:T(8,128)(2,1)}, bf16[256,2560]{1,0:T(8,128)(2,1)}, f32[8,1280]{1,0:T(8,128)S(1)}, f32[16,1280]{1,0:T(8,128)S(1)}) custom-call(s32[1]{0:T(128)} %bitcast.refs_0_.place_ref, bf16[256,2560]{1,0:T(8,128)(2,1)S(1)} %get-tuple-element.87.refs_2_.refs_3_.refs_0_.refs_1_, ...), custom_call_target="tpu_custom_call", output_to_operand_aliasing={{0}: (16, {}), {1}: (17, {})} | custom-call | bytes 35000 | tf_op jit(solution)/shard_map/finish/pallas_call | solution.py:772
  50.2 1.3 %collective-permute-done.9.refs_1_ = f32[8,2560]{1,0:T(8,128)S(1)} collective-permute-done((f32[8,2560]{1,0:T(8,128)S(1)}, f32[8,2560]{1,0:T(8,128)S(1)}, u32[]{:S(2)}, u32[]{:S(2)}) %collective-permute-start.9) | collective-permute-done | bytes 81952 | tf_op jit(solution)/shard_map/ppermute | solution.py:1082
  52.1 2.8 %collective-permute-start.12 = (bf16[8,1664]{1,0:T(8,128)(2,1)S(1)}, bf16[8,1664]{1,0:T(8,128)(2,1)S(1)}, u32[]{:S(2)}, u32[]{:S(2)}) collective-permute-start(bf16[8,1664]{1,0:T(8,128)(2,1)S(1)} %get-tuple-element.147._.refs_1_), channel_id=1, source_target_pairs={{0,8},{4,12},{8,0},{12,4},{1,9},{5,13},{9,1},{13,5},{2,10},{6,14},... | collective-permute-start | bytes 79880 | tf_op jit(solution)/shard_map/ppermute | solution.py:1100
  54.9 1.2 %collective-permute-start.13 = (bf16[8,1664]{1,0:T(8,128)(2,1)S(1)}, bf16[8,1664]{1,0:T(8,128)(2,1)S(1)}, u32[]{:S(2)}, u32[]{:S(2)}) collective-permute-start(bf16[8,1664]{1,0:T(8,128)(2,1)S(1)} %get-tuple-element.147._.refs_1_), channel_id=1, source_target_pairs={{0,12},{4,0},{8,4},{12,8},{1,13},{5,1},{9,5},{13,9},{2,14},{6,2},{... | collective-permute-start | bytes 79880 | tf_op jit(solution)/shard_map/ppermute | solution.py:1100
  57.8 1.0 %collective-permute-done.13.refs_6_ = bf16[8,1664]{1,0:T(8,128)(2,1)S(1)} collective-permute-done((bf16[8,1664]{1,0:T(8,128)(2,1)S(1)}, bf16[8,1664]{1,0:T(8,128)(2,1)S(1)}, u32[]{:S(2)}, u32[]{:S(2)}) %collective-permute-start.13) | collective-permute-done | bytes 26656 | tf_op jit(solution)/shard_map/ppermute | solution.py:1100
  (28 shorter events, 7.5 us)
Async XLA Ops:
  3.5 11.6 %collective-permute-start.1 = (bf16[136,1280]{1,0:T(8,128)(2,1)S(1)}, bf16[136,1280]{1,0:T(8,128)(2,1)S(1)}, u32[]{:S(2)}, u32[]{:S(2)}) collective-permute-start(bf16[136,1280]{1,0:T(8,128)(2,1)S(1)} %first_state.1.refs_7_), channel_id=1, source_target_pairs={{0,4},{12,8},{1,5},{13,9},{2,6},{14,10},{3,7},{15,11},{16,20},{28,... | collective-permute-start | bytes 1044488 | tf_op jit(solution)/shard_map/ppermute | solution.py:844
  9.9 11.5 %collective-permute-start.2 = (bf16[136,1280]{1,0:T(8,128)(2,1)S(1)}, bf16[136,1280]{1,0:T(8,128)(2,1)S(1)}, u32[]{:S(2)}, u32[]{:S(2)}) collective-permute-start(bf16[136,1280]{1,0:T(8,128)(2,1)S(1)} %end_state.1.refs_13_), channel_id=1, source_target_pairs={{0,4},{12,8},{1,5},{13,9},{2,6},{14,10},{3,7},{15,11},{16,20},{28,... | collective-permute-start | bytes 1044488 | tf_op jit(solution)/shard_map/ppermute | solution.py:844
  11.6 0.7 %collective-permute-start = (bf16[8,2816]{1,0:T(8,128)(2,1)S(1)}, bf16[8,2816]{1,0:T(8,128)(2,1)S(1)}, u32[]{:S(2)}, u32[]{:S(2)}) collective-permute-start(bf16[8,2816]{1,0:T(8,128)(2,1)S(1)} %get-tuple-element.86.refs_7_), channel_id=1, source_target_pairs={{4,8},{8,12},{5,9},{9,13},{6,10},{10,14},{7,11},{11,15},{20,24},{2... | collective-permute-start | bytes 135176 | tf_op jit(solution)/shard_map/ppermute | solution.py:878
  15.2 7.0 %collective-permute-start.4 = (bf16[128,1280]{1,0:T(8,128)(2,1)S(1)}, bf16[128,1280]{1,0:T(8,128)(2,1)S(1)}, u32[]{:S(2)}, u32[]{:S(2)}) collective-permute-start(bf16[128,1280]{1,0:T(8,128)(2,1)S(1)} %get-tuple-element.103.refs_8_), channel_id=1, source_target_pairs={{4,8},{8,4},{5,9},{9,5},{6,10},{10,6},{7,11},{11,7},{20,24},{24,20... | collective-permute-start | bytes 983048 | tf_op jit(solution)/shard_map/ppermute | solution.py:844
  21.5 8.1 %collective-permute-start.3 = (bf16[128,1280]{1,0:T(8,128)(2,1)S(1)}, bf16[128,1280]{1,0:T(8,128)(2,1)S(1)}, u32[]{:S(2)}, u32[]{:S(2)}) collective-permute-start(bf16[128,1280]{1,0:T(8,128)(2,1)S(1)} %get-tuple-element.108._), channel_id=1, source_target_pairs={{4,8},{8,4},{5,9},{9,5},{6,10},{10,6},{7,11},{11,7},{20,24},{24,20... | collective-permute-start | bytes 983048 | tf_op jit(solution)/shard_map/ppermute | solution.py:844
  22.3 14.4 %collective-permute-start.5 = (bf16[128,1280]{1,0:T(8,128)(2,1)S(1)}, bf16[128,1280]{1,0:T(8,128)(2,1)S(1)}, u32[]{:S(2)}, u32[]{:S(2)}) collective-permute-start(bf16[128,1280]{1,0:T(8,128)(2,1)S(1)} %message.4.refs_8_), channel_id=1, source_target_pairs={{8,12},{4,0},{9,13},{5,1},{10,14},{6,2},{11,15},{7,3},{24,28},{20,... | collective-permute-start | bytes 983048 | tf_op jit(solution)/shard_map/ppermute | solution.py:844
  29.7 14.6 %collective-permute-start.6 = (bf16[128,1280]{1,0:T(8,128)(2,1)S(1)}, bf16[128,1280]{1,0:T(8,128)(2,1)S(1)}, u32[]{:S(2)}, u32[]{:S(2)}) collective-permute-start(bf16[128,1280]{1,0:T(8,128)(2,1)S(1)} %message.5.refs_8_), channel_id=1, source_target_pairs={{8,12},{4,0},{9,13},{5,1},{10,14},{6,2},{11,15},{7,3},{24,28},{20,... | collective-permute-start | bytes 983048 | tf_op jit(solution)/shard_map/ppermute | solution.py:844
  32.6 12.5 %collective-permute-start.8 = (bf16[8,1280]{1,0:T(8,128)(2,1)S(1)}, bf16[8,1280]{1,0:T(8,128)(2,1)S(1)}, u32[]{:S(2)}, u32[]{:S(2)}) collective-permute-start(bf16[8,1280]{1,0:T(8,128)(2,1)S(1)} %edge.1.refs_4_.edge_ref), channel_id=1, source_target_pairs={{4,0},{8,4},{12,8},{5,1},{9,5},{13,9},{6,2},{10,6},{14,10},{7,3},{... | collective-permute-start | bytes 61448 | tf_op jit(solution)/shard_map/ppermute | solution.py:1013
  45.0 1.2 %collective-permute-start.7 = (f32[8,384]{1,0:T(8,128)S(1)}, f32[8,384]{1,0:T(8,128)S(1)}, u32[]{:S(2)}, u32[]{:S(2)}) collective-permute-start(f32[8,384]{1,0:T(8,128)S(1)} %get-tuple-element.137.small_ref), channel_id=1, source_target_pairs={{0,1},{1,0},{2,3},{3,2},{4,5},{5,4},{6,7},{7,6},{8,9},{9,8},{10,11... | collective-permute-start | bytes 36872 | tf_op jit(solution)/shard_map/ppermute | solution.py:1069
  46.2 5.8 %collective-permute-start.10 = (bf16[272,256]{1,0:T(8,128)(2,1)S(1)}, bf16[272,256]{1,0:T(8,128)(2,1)S(1)}, u32[]{:S(2)}, u32[]{:S(2)}) collective-permute-start(bf16[272,256]{1,0:T(8,128)(2,1)S(1)} %get-tuple-element.138.refs_4_), channel_id=1, source_target_pairs={{0,2},{2,0},{1,3},{3,1},{4,6},{6,4},{5,7},{7,5},{8,10},{10,8},{9,1... | collective-permute-start | bytes 417800 | tf_op jit(solution)/shard_map/ppermute | solution.py:1072
  50.2 1.3 %collective-permute-start.9 = (f32[8,2560]{1,0:T(8,128)S(1)}, f32[8,2560]{1,0:T(8,128)S(1)}, u32[]{:S(2)}, u32[]{:S(2)}) collective-permute-start(f32[8,2560]{1,0:T(8,128)S(1)} %sums.1.refs_0_), channel_id=1, source_target_pairs={{0,1},{1,0},{2,3},{3,2},{4,5},{5,4},{6,7},{7,6},{8,9},{9,8},{10,11... | collective-permute-start | bytes 245768 | tf_op jit(solution)/shard_map/ppermute | solution.py:1082
  52.1 5.7 %collective-permute-start.11 = (bf16[8,1664]{1,0:T(8,128)(2,1)S(1)}, bf16[8,1664]{1,0:T(8,128)(2,1)S(1)}, u32[]{:S(2)}, u32[]{:S(2)}) collective-permute-start(bf16[8,1664]{1,0:T(8,128)(2,1)S(1)} %get-tuple-element.147._.refs_1_), channel_id=1, source_target_pairs={{0,4},{4,8},{8,12},{12,0},{1,5},{5,9},{9,13},{13,1},{2,6},{6,10},{... | collective-permute-start | bytes 79880 | tf_op jit(solution)/shard_map/ppermute | solution.py:1100
  52.1 5.6 %collective-permute-start.12 = (bf16[8,1664]{1,0:T(8,128)(2,1)S(1)}, bf16[8,1664]{1,0:T(8,128)(2,1)S(1)}, u32[]{:S(2)}, u32[]{:S(2)}) collective-permute-start(bf16[8,1664]{1,0:T(8,128)(2,1)S(1)} %get-tuple-element.147._.refs_1_), channel_id=1, source_target_pairs={{0,8},{4,12},{8,0},{12,4},{1,9},{5,13},{9,1},{13,5},{2,10},{6,14},... | collective-permute-start | bytes 79880 | tf_op jit(solution)/shard_map/ppermute | solution.py:1100
  54.9 3.8 %collective-permute-start.13 = (bf16[8,1664]{1,0:T(8,128)(2,1)S(1)}, bf16[8,1664]{1,0:T(8,128)(2,1)S(1)}, u32[]{:S(2)}, u32[]{:S(2)}) collective-permute-start(bf16[8,1664]{1,0:T(8,128)(2,1)S(1)} %get-tuple-element.147._.refs_1_), channel_id=1, source_target_pairs={{0,12},{4,0},{8,4},{12,8},{1,13},{5,1},{9,5},{13,9},{2,14},{6,2},{... | collective-permute-start | bytes 79880 | tf_op jit(solution)/shard_map/ppermute | solution.py:1100

commit v6 on v5

--- a/solution.py
+++ b/solution.py
@@ -594,8 +594,6 @@
     place_ref, x_ref, wx_ref, map_ref = refs[:4]
     blocks, refs = refs[5 : 5 + 4 * parts], refs[5 + 4 * parts :]
     came, refs = refs[:hops], refs[hops:]
-    if start:
-        refs = refs[2:]
     y_hbm, gx_hbm, taps_ref, end_ref, enter, grad, pad, y_ref, gx_ref, sems = refs
     rows = x_ref.shape[0]
     taps = wx_ref.shape[0]
@@ -641,6 +639,38 @@
         copy.wait()
 
 
+def finish_grad_kernel(count, start, spans, parts, *refs):
+    hops = count - 1
+    place_ref, x_ref, wx_ref, map_ref = refs[:4]
+    blocks, refs = refs[5 : 5 + 2 * parts], refs[5 + 2 * parts :]
+    came, (gx_ref, taps_ref, end_ref, grad, pad) = refs[:hops], refs[hops:]
+    rows = x_ref.shape[0]
+    taps = wx_ref.shape[0]
+    state = grad.shape[0]
+    b = map_ref[:, :state]
+    grad[...] = pick(place_ref[0], came, lambda hop: count - 2 - hop, state)
+    for q, (part, mine) in enumerate(spans):
+        dx_ref, q_ref = blocks[2 * part : 2 * part + 2]
+        lanes = slice(q * LANES, (q + 1) * LANES)
+        full = slice(start + q * LANES, start + (q + 1) * LANES)
+        one = pad.at[q]
+        inter = dot(b, grad[:, lanes])
+        one[0:rows, :] = dx_ref[:, mine] + q_ref[:, mine].astype(f32) * inter
+        one[rows : rows + HALO, :] = jnp.zeros((HALO, LANES), f32)
+        x = x_ref[:, full].astype(f32)
+        total = None
+        sums = []
+        for k, weight in enumerate(tap_rows(wx_ref, full)):
+            shifted = one[taps - 1 - k : taps - 1 - k + rows, :]
+            term = weight * shifted
+            total = term if total is None else total + term
+            sums.append(jnp.sum(shifted * x, axis=0, keepdims=True))
+        gx_ref[:, lanes] = total.astype(bf16)
+        end_ref[:, lanes] = total[rows - ROWS16 :]
+        sums = jnp.concatenate(sums + [jnp.zeros((8 - taps, LANES), f32)], axis=0)
+        taps_ref[:, lanes] = sums
+
+
 def sums_kernel(halo_ref, edge_ref, taps_a, taps_b, sums_ref, halo):
     taps, width = 4, taps_a.shape[1]
     edge = edge_ref[...].astype(f32)
@@ -657,10 +687,20 @@
             sums_ref[k : k + 1, lanes] += added
 
 
-def write_kernel(wx_ref, edge_ref, end_a, end_b, _, gx_in, gx_hbm, gx16, sem):
+def write_kernel(count, start, spans, parts, *refs):
+    hops = count - 1
+    place_ref, map_ref, wx_ref, edge_ref, end_a, end_b, gx_b = refs[:7]
+    blocks, refs = refs[8 : 8 + 2 * parts], refs[8 + 2 * parts :]
+    came, refs = refs[:hops], refs[hops + 2 :]
+    y_hbm, gx_hbm, enter, y_b, gx16, sems = refs
     taps = wx_ref.shape[0]
-    rows = gx_hbm.shape[0]
-    width = end_a.shape[1]
+    rows, width = gx_b.shape
+    state = enter.shape[0]
+    chunk = pl.ds(start, width)
+    body = pl.ds(0, rows - ROWS16)
+    tail = pl.ds(rows - ROWS16, ROWS16)
+    copies = [pltpu.make_async_copy(gx_b.at[body, :], gx_hbm.at[body, chunk], sems.at[0])]
+    copies[0].start()
     edge = edge_ref[...].astype(f32)
     row = lax.broadcasted_iota(jnp.int32, (ROWS16, width), 0)
     for c, end_ref in enumerate((end_a, end_b)):
@@ -672,8 +712,19 @@
                 here = wx_ref[k : k + 1, lanes] * edge[4 * c + j : 4 * c + j + 1]
                 end = end + jnp.where(row == at, here, 0.0)
         gx16[:, lanes] = end.astype(bf16)
-    tail = pl.ds(rows - ROWS16, ROWS16)
-    run_copies([pltpu.make_async_copy(gx16, gx_hbm.at[tail, :], sem.at[0])])
+    copies.append(pltpu.make_async_copy(gx16, gx_hbm.at[tail, :], sems.at[1]))
+    copies[1].start()
+    c = map_ref[:, state:]
+    enter[...] = pick(place_ref[0], came, lambda hop: hop + 1, state)
+    for q, (part, mine) in enumerate(spans):
+        y0_ref, ls_ref = blocks[2 * part : 2 * part + 2]
+        lanes = slice(q * LANES, (q + 1) * LANES)
+        inter = dot(c, enter[:, lanes])
+        y_b[:, lanes] = (y0_ref[:, mine] + ls_ref[:, mine].astype(f32) * inter).astype(bf16)
+    copies.append(pltpu.make_async_copy(y_b, y_hbm.at[:, chunk], sems.at[2]))
+    copies[2].start()
+    for copy in copies:
+        copy.wait()
 
 
 def pack_kernel(own_ref, small_ref, small_dp, _, small_out, head_ref):
@@ -812,7 +863,8 @@
     block = 640 if width % 640 == 0 else LANES
     per = width // block
     pairs = width // LANES
-    split = (pairs // 2, pairs + pairs // 5, pairs - pairs // 2 - pairs // 5)
+    split = (pairs // 2 + pairs // 10, pairs + pairs // 10)
+    split += (2 * pairs - sum(split),)
     spans = [
         (part, slice(at * LANES, (at + 1) * LANES))
         for part, size in enumerate(split)
@@ -1027,7 +1079,7 @@
         kernel = functools.partial(finish_bc_kernel, count, c == 0, where, len(used), scale)
         return call(kernel, "finish_bc", ins, outs, scratch)
 
-    def finish(c, after, kept_y):
+    def finish(c, after):
         start = c * width
         where, used = chunk_parts(c)
         pieces = (4, 4, 2) if pairs == 10 else (pairs - 1, 1)
@@ -1035,10 +1087,6 @@
         for made in used:
             ins += made[:4]
         ins += received[c]
-        kept = ()
-        if kept_y:
-            kept = ((len(ins), 0), (len(ins) + 1, 1))
-            ins += [(a, "hbm") for a in kept_y]
         made = call(
             functools.partial(finish_kernel, count, start, where, len(used), pieces),
             "finish",
@@ -1053,11 +1101,10 @@
                 vmem((rows, width), bf16),
                 pltpu.SemaphoreType.DMA((len(pieces), 2)),
             ],
-            kept=kept,
         )
         return made[:2], made[2], made[3]
 
-    outs, taps_a, end_a = finish(0, edge, None)
+    outs, taps_a, end_a = finish(0, edge)
     dbc = finish_bc(0, dsim, taps_a)[0]
     own, small = finish_bc(1, dbc, dbc)
 
@@ -1071,7 +1118,17 @@
     )
     others = [lax.ppermute(to_heads, "head", turn) for turn in turns]
 
-    (y, gx), taps_b, end_b = finish(1, to_heads, outs)
+    where, used = chunk_parts(1)
+    ins = [where_am_i, x, conv_x, mapped, (to_heads, "any")]
+    for made in used:
+        ins += made[1:3]
+    gx_b, taps_b, end_b = call(
+        functools.partial(finish_grad_kernel, count, width, where, len(used)),
+        "finish_grad",
+        ins + received[1],
+        [shape((rows, width), bf16), shape((8, width)), shape((ROWS16, width))],
+        [vmem((state, width), bf16), padded(pairs)],
+    )
     sums = call(
         sums_kernel,
         "sums",
@@ -1088,14 +1145,23 @@
         [shape((rows, bcw)), shape((8, send_width), bf16)],
         [vmem((8, send_width))],
     )
-    gx = call(
-        write_kernel,
+    ins = [where_am_i, mapped, conv_x, edges, end_a, end_b, gx_b, (to_seq, "any")]
+    for made in used:
+        ins += [made[0], made[3]]
+    ins += received[1]
+    y, gx = call(
+        functools.partial(write_kernel, count, width, where, len(used)),
         "write",
-        [conv_x, edges, end_a, end_b, (to_seq, "any"), (gx, "hbm")],
-        [(shape((rows, inner), bf16), "hbm")],
-        [vmem((ROWS16, inner), bf16), pltpu.SemaphoreType.DMA((1,))],
-        kept=((5, 0),),
-    )[0]
+        ins + [(outs[0], "hbm"), (outs[1], "hbm")],
+        [(shape((rows, inner), bf16), "hbm"), (shape((rows, inner), bf16), "hbm")],
+        [
+            vmem((state, width), bf16),
+            vmem((rows, width), bf16),
+            vmem((ROWS16, inner), bf16),
+            pltpu.SemaphoreType.DMA((3,)),
+        ],
+        kept=((len(ins), 0), (len(ins) + 1, 1)),
+    )
     from_seq = [
         lax.ppermute(to_seq, "seq", [(i, (i + k) % count) for i in range(count)])
         for k in range(1, count)

time: 59.8 us -> 59.4 us (level)
  Pallas kernels: 23.7 us -> 23.1 us
  starting transfers between devices: 16.6 us -> 17.2 us
    ppermute x3, waiting for transfers between devices: 1.82 us -> 0.5 us  [local(): lax.ppermute(to_seq, 'seq', [(i, (i + k) % count) for i in range(count)])]
    ppermute x1, waiting for transfers between devices: 0.52 us -> 1.55 us  [local(): others = [lax.ppermute(to_heads, 'head', turn) for turn in turns]]
    ppermute x3, starting transfers between devices: 4.02 us -> 4.69 us  [local(): lax.ppermute(to_seq, 'seq', [(i, (i + k) % count) for i in range(count)])]
    pallas_call x24, Pallas kernels: 23.7 us -> 23.1 us  [call(): pl.pallas_call(kernel, grid=grid, in_specs=[spec(i) for i in ins], out_sp...]
  transfers between devices with their start and end apart: 14 -> 14, of which waited for: 9 -> 8; matrix products, arithmetic and copies ran while one was open for 0% -> 0% of each run, Pallas kernels for 34% -> 33%
where the time goes in v6:
time: 59.4 us; the launch traced here: 59 us
  Pallas kernels  23.1 us (39%)
  waiting for transfers between devices  17.8 us (30%)
  starting transfers between devices  17.2 us (29%)
  between operations  0.9 us (2%)
    pallas_call x24, Pallas kernels, call(): pl.pallas_call(kernel, grid=grid, in_specs=[spec(i) for i in ins], out_sp...  23.1 us
    ppermute x6, waiting for transfers between devices, hop_on(): received[c].append(lax.ppermute(message, 'seq', routes))  13.4 us
    ppermute x6, starting transfers between devices, hop_on(): received[c].append(lax.ppermute(message, 'seq', routes))  8.88 us
    ppermute x3, starting transfers between devices, local(): lax.ppermute(to_seq, 'seq', [(i, (i + k) % count) for i in range(count)])  4.69 us
    ppermute x1, starting transfers between devices, local(): others = [lax.ppermute(to_heads, 'head', turn) for turn in turns]  1.56 us
    ppermute x1, waiting for transfers between devices, local(): others = [lax.ppermute(to_heads, 'head', turn) for turn in turns]  1.55 us
    ppermute x1, starting transfers between devices, local(): edges = lax.ppermute(edge, 'seq', [(i + 1, i) for i in range(count - 1)])  1.29 us
    ppermute x1, waiting for transfers between devices, local(): sums_dp = lax.ppermute(sums, 'dp', swap)  1.26 us
  transfers between devices with their start and end apart: 14, of which 8 were waited for; matrix products, arithmetic and copies ran while one was open for 0% of the time, Pallas kernels for 33%

profile of v6, /device:TPU:0, one launch (start us, length us, event | category | flops | bytes accessed | tf_op | source)
XLA Modules:
  0.0 59.0 jit_solution(16035427605803382873)
XLA Ops:
  0.6 1.4 %early_load.1 = (bf16[256,1280]{1,0:T(8,128)(2,1)S(1)}, bf16[256,1280]{1,0:T(8,128)(2,1)S(1)}, f32[40,256]{1,0:T(8,128)S(1)}, f32[4,2560]{1,0:T(4,128)S(1)}, bf1...) custom-call(s32[1]{0:T(128)} %bitcast.refs_0_.place_ref, bf16[256,2560]{1,0:T(8,128)(2,1)} %bitcast.10, ...), custom_call_target="tpu_custom_call" | custom-call | bytes 35000 | tf_op jit(solution)/shard_map/early_load/pallas_call | solution.py:823
  2.0 1.5 %first_state.1.refs_7_ = bf16[136,1280]{1,0:T(8,128)(2,1)S(1)} custom-call(s32[1]{0:T(128)} %bitcast.refs_0_.place_ref, f32[40,256]{1,0:T(8,128)S(1)} %get-tuple-element.82.refs_1_, bf16[256,1280]{1,0:T(8,128)(2,1)S(1)} %get-tuple-element.83.refs_2_, bf16[256,1280]{1,0:T(8,128)(2,1)S(1)} %get-tuple-element.84.refs_3_, ...), custom_call_target="tpu_custom_call" | custom-call | bytes 35000 | tf_op jit(solution)/shard_map/first_state/pallas_call | solution.py:823
  3.5 3.1 %collective-permute-start.1 = (bf16[136,1280]{1,0:T(8,128)(2,1)S(1)}, bf16[136,1280]{1,0:T(8,128)(2,1)S(1)}, u32[]{:S(2)}, u32[]{:S(2)}) collective-permute-start(bf16[136,1280]{1,0:T(8,128)(2,1)S(1)} %first_state.1.refs_7_), channel_id=1, source_target_pairs={{0,4},{12,8},{1,5},{13,9},{2,6},{14,10},{3,7},{15,11},{16,20},{28,... | collective-permute-start | bytes 1044488 | tf_op jit(solution)/shard_map/ppermute | solution.py:896
  6.6 1.8 %load.1 = (bf16[256,2560]{1,0:T(8,128)(2,1)S(1)}, bf16[256,256]{1,0:T(8,128)(2,1)S(1)}, bf16[256,2560]{1,0:T(8,128)(2,1)S(1)}, f32[40,256]{1,0:T(8,128)S(1)}, f3...) custom-call(bf16[256,2560]{1,0:T(8,128)(2,1)} %bitcast.11, bf16[256,256]{1,0:T(8,128)(2,1)} %bitcast.17, ...), custom_call_target="tpu_custom_call" | custom-call | bytes 35000 | tf_op jit(solution)/shard_map/load/pallas_call | solution.py:823
  9.9 1.7 %collective-permute-start.2 = (bf16[136,1280]{1,0:T(8,128)(2,1)S(1)}, bf16[136,1280]{1,0:T(8,128)(2,1)S(1)}, u32[]{:S(2)}, u32[]{:S(2)}) collective-permute-start(bf16[136,1280]{1,0:T(8,128)(2,1)S(1)} %end_state.1.refs_13_), channel_id=1, source_target_pairs={{0,4},{12,8},{1,5},{13,9},{2,6},{14,10},{3,7},{15,11},{16,20},{28,... | collective-permute-start | bytes 1044488 | tf_op jit(solution)/shard_map/ppermute | solution.py:896
  12.3 2.8 %collective-permute-done.1.refs_2_ = bf16[136,1280]{1,0:T(8,128)(2,1)S(1)} collective-permute-done((bf16[136,1280]{1,0:T(8,128)(2,1)S(1)}, bf16[136,1280]{1,0:T(8,128)(2,1)S(1)}, u32[]{:S(2)}, u32[]{:S(2)}) %collective-permute-start.1) | collective-permute-done | bytes 348192 | tf_op jit(solution)/shard_map/ppermute | solution.py:896
  15.9 2.6 %inside_block.3 = (f32[256,768]{1,0:T(8,128)S(1)}, f32[256,768]{1,0:T(8,128)S(1)}, bf16[256,768]{1,0:T(8,128)(2,1)S(1)}, bf16[256,768]{1,0:T(8,128)(2,1)S(1)}, b...) custom-call(bf16[256,2560]{1,0:T(8,128)(2,1)S(1)} %get-tuple-element., ...), custom_call_target="tpu_custom_call" | custom-call | bytes 9450000 | tf_op jit(solution)/shard_map/inside_block/pallas_call | solution.py:823
  18.5 2.9 %collective-permute-done.2.refs_4_ = bf16[136,1280]{1,0:T(8,128)(2,1)S(1)} collective-permute-done((bf16[136,1280]{1,0:T(8,128)(2,1)S(1)}, bf16[136,1280]{1,0:T(8,128)(2,1)S(1)}, u32[]{:S(2)}, u32[]{:S(2)}) %collective-permute-start.2) | collective-permute-done | bytes 348192 | tf_op jit(solution)/shard_map/ppermute | solution.py:896
  22.3 1.5 %collective-permute-start.6 = (bf16[128,1280]{1,0:T(8,128)(2,1)S(1)}, bf16[128,1280]{1,0:T(8,128)(2,1)S(1)}, u32[]{:S(2)}, u32[]{:S(2)}) collective-permute-start(bf16[128,1280]{1,0:T(8,128)(2,1)S(1)} %message.4.refs_8_), channel_id=1, source_target_pairs={{8,12},{4,0},{9,13},{5,1},{10,14},{6,2},{11,15},{7,3},{24,28},{20,... | collective-permute-start | bytes 983048 | tf_op jit(solution)/shard_map/ppermute | solution.py:896
  23.8 5.2 %inside_block.4 = (f32[256,1408]{1,0:T(8,128)S(1)}, f32[256,1408]{1,0:T(8,128)S(1)}, bf16[256,1408]{1,0:T(8,128)(2,1)S(1)}, bf16[256,1408]{1,0:T(8,128)(2,1)S(1)...) custom-call(bf16[256,2560]{1,0:T(8,128)(2,1)S(1)} %get-tuple-element, ...), custom_call_target="tpu_custom_call" | custom-call | bytes 9450000 | tf_op jit(solution)/shard_map/inside_block/pallas_call | solution.py:823
  29.1 1.3 %collective-permute-start.7 = (bf16[128,1280]{1,0:T(8,128)(2,1)S(1)}, bf16[128,1280]{1,0:T(8,128)(2,1)S(1)}, u32[]{:S(2)}, u32[]{:S(2)}) collective-permute-start(bf16[128,1280]{1,0:T(8,128)(2,1)S(1)} %message.5.refs_8_), channel_id=1, source_target_pairs={{8,12},{4,0},{9,13},{5,1},{10,14},{6,2},{11,15},{7,3},{24,28},{20,... | collective-permute-start | bytes 983048 | tf_op jit(solution)/shard_map/ppermute | solution.py:896
  30.4 1.3 %inside_block.5 = (f32[256,384]{1,0:T(8,128)S(1)}, f32[256,384]{1,0:T(8,128)S(1)}, bf16[256,384]{1,0:T(8,128)(2,1)S(1)}, bf16[256,384]{1,0:T(8,128)(2,1)S(1)}, b...) custom-call(bf16[256,2560]{1,0:T(8,128)(2,1)S(1)} %get-tuple-element., ...), custom_call_target="tpu_custom_call" | custom-call | bytes 9450000 | tf_op jit(solution)/shard_map/inside_block/pallas_call | solution.py:823
  32.0 1.3 %collective-permute-start.5 = (bf16[8,1280]{1,0:T(8,128)(2,1)S(1)}, bf16[8,1280]{1,0:T(8,128)(2,1)S(1)}, u32[]{:S(2)}, u32[]{:S(2)}) collective-permute-start(bf16[8,1280]{1,0:T(8,128)(2,1)S(1)} %edge.1.refs_4_.edge_ref), channel_id=1, source_target_pairs={{4,0},{8,4},{12,8},{5,1},{9,5},{13,9},{6,2},{10,6},{14,10},{7,3},{... | collective-permute-start | bytes 61448 | tf_op jit(solution)/shard_map/ppermute | solution.py:1065
  33.3 3.5 %collective-permute-done.6.refs_15_.refs_10_ = bf16[128,1280]{1,0:T(8,128)(2,1)S(1)} collective-permute-done((bf16[128,1280]{1,0:T(8,128)(2,1)S(1)}, bf16[128,1280]{1,0:T(8,128)(2,1)S(1)}, u32[]{:S(2)}, u32[]{:S(2)}) %collective-permute-start.6) | collective-permute-done | bytes 327712 | tf_op jit(solution)/shard_map/ppermute | solution.py:896
  36.8 2.3 %finish.1 = (bf16[256,2560]{1,0:T(8,128)(2,1)}, bf16[256,2560]{1,0:T(8,128)(2,1)}, f32[8,1280]{1,0:T(8,128)S(1)}, f32[16,1280]{1,0:T(8,128)S(1)}) custom-call(s32[1]{0:T(128)} %bitcast.refs_0_.place_ref, bf16[256,2560]{1,0:T(8,128)(2,1)S(1)} %get-tuple-element.88.refs_2_.refs_3_.refs_0_.refs_1_, ...), custom_call_target="tpu_custom_call" | custom-call | bytes 35000 | tf_op jit(solution)/shard_map/finish/pallas_call | solution.py:823
  39.8 4.1 %collective-permute-done.7.refs_10_.refs_11_.refs_14_ = bf16[128,1280]{1,0:T(8,128)(2,1)S(1)} collective-permute-done((bf16[128,1280]{1,0:T(8,128)(2,1)S(1)}, bf16[128,1280]{1,0:T(8,128)(2,1)S(1)}, u32[]{:S(2)}, u32[]{:S(2)}) %collective-permute-start.7) | collective-permute-done | bytes 327712 | tf_op jit(solution)/shard_map/ppermute | solution.py:896
  44.6 1.2 %collective-permute-done.8.small_dp = f32[8,384]{1,0:T(8,128)S(1)} collective-permute-done((f32[8,384]{1,0:T(8,128)S(1)}, f32[8,384]{1,0:T(8,128)S(1)}, u32[]{:S(2)}, u32[]{:S(2)}) %collective-permute-start.8) | collective-permute-done | bytes 12320 | tf_op jit(solution)/shard_map/ppermute | solution.py:1116
  45.8 1.6 %collective-permute-start.10 = (bf16[272,256]{1,0:T(8,128)(2,1)S(1)}, bf16[272,256]{1,0:T(8,128)(2,1)S(1)}, u32[]{:S(2)}, u32[]{:S(2)}) collective-permute-start(bf16[272,256]{1,0:T(8,128)(2,1)S(1)} %get-tuple-element.140.refs_4_), channel_id=1, source_target_pairs={{0,2},{2,0},{1,3},{3,1},{4,6},{6,4},{5,7},{7,5},{8,10},{10,8},{9,1... | collective-permute-start | bytes 417800 | tf_op jit(solution)/shard_map/ppermute | solution.py:1119
  47.3 1.3 %finish_grad.1 = (bf16[256,1280]{1,0:T(8,128)(2,1)S(1)}, f32[8,1280]{1,0:T(8,128)S(1)}, f32[16,1280]{1,0:T(8,128)S(1)}) custom-call(s32[1]{0:T(128)} %bitcast.refs_0_.place_ref, bf16[256,2560]{1,0:T(8,128)(2,1)S(1)} %get-tuple-element.88.refs_2_.refs_3_.refs_0_.refs_1_, f32[4,2560]{1,0:T(4,128)S(1)} %get-tuple-element.89.refs_4_.refs_5_.refs_3_.refs_2_, ...), custom_call_target="tpu_custom_call" | custom-call | bytes 35000 | tf_op jit(solution)/shard_map/finish_grad/pallas_call | solution.py:823
  48.8 1.3 %collective-permute-done.9.refs_1_ = f32[8,2560]{1,0:T(8,128)S(1)} collective-permute-done((f32[8,2560]{1,0:T(8,128)S(1)}, f32[8,2560]{1,0:T(8,128)S(1)}, u32[]{:S(2)}, u32[]{:S(2)}) %collective-permute-start.9) | collective-permute-done | bytes 81952 | tf_op jit(solution)/shard_map/ppermute | solution.py:1139
  50.0 1.6 %collective-permute-done.10.refs_4_ = bf16[272,256]{1,0:T(8,128)(2,1)S(1)} collective-permute-done((bf16[272,256]{1,0:T(8,128)(2,1)S(1)}, bf16[272,256]{1,0:T(8,128)(2,1)S(1)}, u32[]{:S(2)}, u32[]{:S(2)}) %collective-permute-start.10) | collective-permute-done | bytes 139296 | tf_op jit(solution)/shard_map/ppermute | solution.py:1119
  52.0 2.5 %collective-permute-start.12 = (bf16[8,1664]{1,0:T(8,128)(2,1)S(1)}, bf16[8,1664]{1,0:T(8,128)(2,1)S(1)}, u32[]{:S(2)}, u32[]{:S(2)}) collective-permute-start(bf16[8,1664]{1,0:T(8,128)(2,1)S(1)} %get-tuple-element.145.refs_7_._.refs_1_), channel_id=1, source_target_pairs={{0,8},{4,12},{8,0},{12,4},{1,9},{5,13},{9,1},{13,5},{2,10},{6,14},... | collective-permute-start | bytes 79880 | tf_op jit(solution)/shard_map/ppermute | solution.py:1166
  54.5 1.8 %collective-permute-start.13 = (bf16[8,1664]{1,0:T(8,128)(2,1)S(1)}, bf16[8,1664]{1,0:T(8,128)(2,1)S(1)}, u32[]{:S(2)}, u32[]{:S(2)}) collective-permute-start(bf16[8,1664]{1,0:T(8,128)(2,1)S(1)} %get-tuple-element.145.refs_7_._.refs_1_), channel_id=1, source_target_pairs={{0,12},{4,0},{8,4},{12,8},{1,13},{5,1},{9,5},{13,9},{2,14},{6,2},{... | collective-permute-start | bytes 79880 | tf_op jit(solution)/shard_map/ppermute | solution.py:1166
  56.5 1.4 %write.1 = (bf16[256,2560]{1,0:T(8,128)(2,1)}, bf16[256,2560]{1,0:T(8,128)(2,1)}) custom-call(s32[1]{0:T(128)} %bitcast.refs_0_.place_ref, bf16[256,256]{1,0:T(8,128)(2,1)S(1)} %get-tuple-element.101.refs_7_.refs_6_.refs_1_.refs_3_, f32[4,2560]{1,0:T(4,128)S(1)} %get-tuple-element.89.refs_4_.refs_5_.refs_3_.refs_2_, ...), custom_call_target="tpu_custom_call", output_to_operand_aliasing={{0}: (15, {}), {1}: (16, {})} | custom-call | bytes 2800000 | tf_op jit(solution)/shard_map/write/pallas_call | solution.py:823
  (28 shorter events, 7.3 us)
Async XLA Ops:
  3.5 11.6 %collective-permute-start.1 = (bf16[136,1280]{1,0:T(8,128)(2,1)S(1)}, bf16[136,1280]{1,0:T(8,128)(2,1)S(1)}, u32[]{:S(2)}, u32[]{:S(2)}) collective-permute-start(bf16[136,1280]{1,0:T(8,128)(2,1)S(1)} %first_state.1.refs_7_), channel_id=1, source_target_pairs={{0,4},{12,8},{1,5},{13,9},{2,6},{14,10},{3,7},{15,11},{16,20},{28,... | collective-permute-start | bytes 1044488 | tf_op jit(solution)/shard_map/ppermute | solution.py:896
  9.9 11.5 %collective-permute-start.2 = (bf16[136,1280]{1,0:T(8,128)(2,1)S(1)}, bf16[136,1280]{1,0:T(8,128)(2,1)S(1)}, u32[]{:S(2)}, u32[]{:S(2)}) collective-permute-start(bf16[136,1280]{1,0:T(8,128)(2,1)S(1)} %end_state.1.refs_13_), channel_id=1, source_target_pairs={{0,4},{12,8},{1,5},{13,9},{2,6},{14,10},{3,7},{15,11},{16,20},{28,... | collective-permute-start | bytes 1044488 | tf_op jit(solution)/shard_map/ppermute | solution.py:896
  11.6 0.7 %collective-permute-start = (bf16[8,2816]{1,0:T(8,128)(2,1)S(1)}, bf16[8,2816]{1,0:T(8,128)(2,1)S(1)}, u32[]{:S(2)}, u32[]{:S(2)}) collective-permute-start(bf16[8,2816]{1,0:T(8,128)(2,1)S(1)} %get-tuple-element.81.refs_7_), channel_id=1, source_target_pairs={{4,8},{8,12},{5,9},{9,13},{6,10},{10,14},{7,11},{11,15},{20,24},{2... | collective-permute-start | bytes 135176 | tf_op jit(solution)/shard_map/ppermute | solution.py:930
  15.2 7.0 %collective-permute-start.4 = (bf16[128,1280]{1,0:T(8,128)(2,1)S(1)}, bf16[128,1280]{1,0:T(8,128)(2,1)S(1)}, u32[]{:S(2)}, u32[]{:S(2)}) collective-permute-start(bf16[128,1280]{1,0:T(8,128)(2,1)S(1)} %get-tuple-element.104.refs_8_), channel_id=1, source_target_pairs={{4,8},{8,4},{5,9},{9,5},{6,10},{10,6},{7,11},{11,7},{20,24},{24,20... | collective-permute-start | bytes 983048 | tf_op jit(solution)/shard_map/ppermute | solution.py:896
  21.5 7.5 %collective-permute-start.3 = (bf16[128,1280]{1,0:T(8,128)(2,1)S(1)}, bf16[128,1280]{1,0:T(8,128)(2,1)S(1)}, u32[]{:S(2)}, u32[]{:S(2)}) collective-permute-start(bf16[128,1280]{1,0:T(8,128)(2,1)S(1)} %get-tuple-element.109._), channel_id=1, source_target_pairs={{4,8},{8,4},{5,9},{9,5},{6,10},{10,6},{7,11},{11,7},{20,24},{24,20... | collective-permute-start | bytes 983048 | tf_op jit(solution)/shard_map/ppermute | solution.py:896
  22.3 14.5 %collective-permute-start.6 = (bf16[128,1280]{1,0:T(8,128)(2,1)S(1)}, bf16[128,1280]{1,0:T(8,128)(2,1)S(1)}, u32[]{:S(2)}, u32[]{:S(2)}) collective-permute-start(bf16[128,1280]{1,0:T(8,128)(2,1)S(1)} %message.4.refs_8_), channel_id=1, source_target_pairs={{8,12},{4,0},{9,13},{5,1},{10,14},{6,2},{11,15},{7,3},{24,28},{20,... | collective-permute-start | bytes 983048 | tf_op jit(solution)/shard_map/ppermute | solution.py:896
  29.1 14.8 %collective-permute-start.7 = (bf16[128,1280]{1,0:T(8,128)(2,1)S(1)}, bf16[128,1280]{1,0:T(8,128)(2,1)S(1)}, u32[]{:S(2)}, u32[]{:S(2)}) collective-permute-start(bf16[128,1280]{1,0:T(8,128)(2,1)S(1)} %message.5.refs_8_), channel_id=1, source_target_pairs={{8,12},{4,0},{9,13},{5,1},{10,14},{6,2},{11,15},{7,3},{24,28},{20,... | collective-permute-start | bytes 983048 | tf_op jit(solution)/shard_map/ppermute | solution.py:896
  32.0 12.6 %collective-permute-start.5 = (bf16[8,1280]{1,0:T(8,128)(2,1)S(1)}, bf16[8,1280]{1,0:T(8,128)(2,1)S(1)}, u32[]{:S(2)}, u32[]{:S(2)}) collective-permute-start(bf16[8,1280]{1,0:T(8,128)(2,1)S(1)} %edge.1.refs_4_.edge_ref), channel_id=1, source_target_pairs={{4,0},{8,4},{12,8},{5,1},{9,5},{13,9},{6,2},{10,6},{14,10},{7,3},{... | collective-permute-start | bytes 61448 | tf_op jit(solution)/shard_map/ppermute | solution.py:1065
  44.5 1.2 %collective-permute-start.8 = (f32[8,384]{1,0:T(8,128)S(1)}, f32[8,384]{1,0:T(8,128)S(1)}, u32[]{:S(2)}, u32[]{:S(2)}) collective-permute-start(f32[8,384]{1,0:T(8,128)S(1)} %get-tuple-element.139.small_ref), channel_id=1, source_target_pairs={{0,1},{1,0},{2,3},{3,2},{4,5},{5,4},{6,7},{7,6},{8,9},{9,8},{10,11... | collective-permute-start | bytes 36872 | tf_op jit(solution)/shard_map/ppermute | solution.py:1116
  45.8 5.8 %collective-permute-start.10 = (bf16[272,256]{1,0:T(8,128)(2,1)S(1)}, bf16[272,256]{1,0:T(8,128)(2,1)S(1)}, u32[]{:S(2)}, u32[]{:S(2)}) collective-permute-start(bf16[272,256]{1,0:T(8,128)(2,1)S(1)} %get-tuple-element.140.refs_4_), channel_id=1, source_target_pairs={{0,2},{2,0},{1,3},{3,1},{4,6},{6,4},{5,7},{7,5},{8,10},{10,8},{9,1... | collective-permute-start | bytes 417800 | tf_op jit(solution)/shard_map/ppermute | solution.py:1119
  48.7 1.3 %collective-permute-start.9 = (f32[8,2560]{1,0:T(8,128)S(1)}, f32[8,2560]{1,0:T(8,128)S(1)}, u32[]{:S(2)}, u32[]{:S(2)}) collective-permute-start(f32[8,2560]{1,0:T(8,128)S(1)} %sums.1.refs_0_), channel_id=1, source_target_pairs={{0,1},{1,0},{2,3},{3,2},{4,5},{5,4},{6,7},{7,6},{8,9},{9,8},{10,11... | collective-permute-start | bytes 245768 | tf_op jit(solution)/shard_map/ppermute | solution.py:1139
  51.6 6.2 %collective-permute-start.11 = (bf16[8,1664]{1,0:T(8,128)(2,1)S(1)}, bf16[8,1664]{1,0:T(8,128)(2,1)S(1)}, u32[]{:S(2)}, u32[]{:S(2)}) collective-permute-start(bf16[8,1664]{1,0:T(8,128)(2,1)S(1)} %get-tuple-element.145.refs_7_._.refs_1_), channel_id=1, source_target_pairs={{0,4},{4,8},{8,12},{12,0},{1,5},{5,9},{9,13},{13,1},{2,6},{6,10},{... | collective-permute-start | bytes 79880 | tf_op jit(solution)/shard_map/ppermute | solution.py:1166
  52.0 5.9 %collective-permute-start.12 = (bf16[8,1664]{1,0:T(8,128)(2,1)S(1)}, bf16[8,1664]{1,0:T(8,128)(2,1)S(1)}, u32[]{:S(2)}, u32[]{:S(2)}) collective-permute-start(bf16[8,1664]{1,0:T(8,128)(2,1)S(1)} %get-tuple-element.145.refs_7_._.refs_1_), channel_id=1, source_target_pairs={{0,8},{4,12},{8,0},{12,4},{1,9},{5,13},{9,1},{13,5},{2,10},{6,14},... | collective-permute-start | bytes 79880 | tf_op jit(solution)/shard_map/ppermute | solution.py:1166
  54.5 3.8 %collective-permute-start.13 = (bf16[8,1664]{1,0:T(8,128)(2,1)S(1)}, bf16[8,1664]{1,0:T(8,128)(2,1)S(1)}, u32[]{:S(2)}, u32[]{:S(2)}) collective-permute-start(bf16[8,1664]{1,0:T(8,128)(2,1)S(1)} %get-tuple-element.145.refs_7_._.refs_1_), channel_id=1, source_target_pairs={{0,12},{4,0},{8,4},{12,8},{1,13},{5,1},{9,5},{13,9},{2,14},{6,2},{... | collective-permute-start | bytes 79880 | tf_op jit(solution)/shard_map/ppermute | solution.py:1166

commit v7 on v6

--- a/solution.py
+++ b/solution.py
@@ -109,19 +109,23 @@
         pltpu.make_async_copy(bc_hbm.at[last, :], bc16, sems.at[small + 3]),
     ]
     copies = [pltpu.make_async_copy(sources[i], kept[i], sems.at[i]) for i in range(small)]
-    for copy in tails:
-        copy.start()
-
-    @pl.when(place == 0)
-    def _():
-        run_copies(copies + [pltpu.make_async_copy(x_hbm.at[:, chunk], xa, sems.at[small])])
-
-    @pl.when(place == count - 1)
-    def _():
-        run_copies(copies + [pltpu.make_async_copy(g_hbm.at[:, chunk], ga, sems.at[small + 1])])
-
-    for copy in tails:
-        copy.wait()
+    first = [pltpu.make_async_copy(x_hbm.at[:, chunk], xa, sems.at[small])] + copies
+    last_ones = [pltpu.make_async_copy(g_hbm.at[:, chunk], ga, sems.at[small + 1])]
+    last_ones += copies[:1] + copies[2:]
+
+    def start(found):
+        for copy in found:
+            copy.start()
+
+    def wait(found):
+        for copy in found:
+            copy.wait()
+
+    pl.when(place == 0)(lambda: start(first))
+    pl.when(place == count - 1)(lambda: start(last_ones))
+    run_copies(tails)
+    pl.when(place == 0)(lambda: wait(first))
+    pl.when(place == count - 1)(lambda: wait(last_ones))
     tails_ref[:, :width] = x16[...].astype(f32)[ROWS16 - HALO :].astype(bf16)
     tails_ref[:, width:] = bc16[...].astype(f32)[ROWS16 - HALO :].astype(bf16)
 

time: 59.4 us -> 59.3 us (level)
  no operation moved by 1% of the time
where the time goes in v7:
time: 59.3 us; the launch traced here: 58.9 us
  Pallas kernels  23 us (39%)
  waiting for transfers between devices  17.7 us (30%)
  starting transfers between devices  17.3 us (29%)
  between operations  0.9 us (2%)
    pallas_call x24, Pallas kernels, call(): pl.pallas_call(kernel, grid=grid, in_specs=[spec(i) for i in ins], out_sp...  23 us
    ppermute x6, waiting for transfers between devices, hop_on(): received[c].append(lax.ppermute(message, 'seq', routes))  13.2 us
    ppermute x6, starting transfers between devices, hop_on(): received[c].append(lax.ppermute(message, 'seq', routes))  8.99 us
    ppermute x3, starting transfers between devices, local(): lax.ppermute(to_seq, 'seq', [(i, (i + k) % count) for i in range(count)])  4.69 us
    ppermute x1, waiting for transfers between devices, local(): others = [lax.ppermute(to_heads, 'head', turn) for turn in turns]  1.56 us
    ppermute x1, starting transfers between devices, local(): others = [lax.ppermute(to_heads, 'head', turn) for turn in turns]  1.56 us
    ppermute x1, starting transfers between devices, local(): edges = lax.ppermute(edge, 'seq', [(i + 1, i) for i in range(count - 1)])  1.29 us
    ppermute x1, waiting for transfers between devices, local(): sums_dp = lax.ppermute(sums, 'dp', swap)  1.26 us
  transfers between devices with their start and end apart: 14, of which 8 were waited for; matrix products, arithmetic and copies ran while one was open for 0% of the time, Pallas kernels for 33%

profile of v7, /device:TPU:0, one launch (start us, length us, event | category | flops | bytes accessed | tf_op | source)
XLA Modules:
  0.0 58.9 jit_solution(14894692389844159998)
XLA Ops:
  0.6 1.3 %early_load.1 = (bf16[256,1280]{1,0:T(8,128)(2,1)S(1)}, bf16[256,1280]{1,0:T(8,128)(2,1)S(1)}, f32[40,256]{1,0:T(8,128)S(1)}, f32[4,2560]{1,0:T(4,128)S(1)}, bf1...) custom-call(s32[1]{0:T(128)} %bitcast.refs_0_.place_ref, bf16[256,2560]{1,0:T(8,128)(2,1)} %bitcast.10, ...), custom_call_target="tpu_custom_call" | custom-call | bytes 35000 | tf_op jit(solution)/shard_map/early_load/pallas_call | solution.py:827
  1.9 1.5 %first_state.1.refs_7_ = bf16[136,1280]{1,0:T(8,128)(2,1)S(1)} custom-call(s32[1]{0:T(128)} %bitcast.refs_0_.place_ref, f32[40,256]{1,0:T(8,128)S(1)} %get-tuple-element.82.refs_1_, bf16[256,1280]{1,0:T(8,128)(2,1)S(1)} %get-tuple-element.83.refs_2_, bf16[256,1280]{1,0:T(8,128)(2,1)S(1)} %get-tuple-element.84.refs_3_, ...), custom_call_target="tpu_custom_call" | custom-call | bytes 35000 | tf_op jit(solution)/shard_map/first_state/pallas_call | solution.py:827
  3.4 3.2 %collective-permute-start.1 = (bf16[136,1280]{1,0:T(8,128)(2,1)S(1)}, bf16[136,1280]{1,0:T(8,128)(2,1)S(1)}, u32[]{:S(2)}, u32[]{:S(2)}) collective-permute-start(bf16[136,1280]{1,0:T(8,128)(2,1)S(1)} %first_state.1.refs_7_), channel_id=1, source_target_pairs={{0,4},{12,8},{1,5},{13,9},{2,6},{14,10},{3,7},{15,11},{16,20},{28,... | collective-permute-start | bytes 1044488 | tf_op jit(solution)/shard_map/ppermute | solution.py:900
  6.6 1.8 %load.1 = (bf16[256,2560]{1,0:T(8,128)(2,1)S(1)}, bf16[256,256]{1,0:T(8,128)(2,1)S(1)}, bf16[256,2560]{1,0:T(8,128)(2,1)S(1)}, f32[40,256]{1,0:T(8,128)S(1)}, f3...) custom-call(bf16[256,2560]{1,0:T(8,128)(2,1)} %bitcast.11, bf16[256,256]{1,0:T(8,128)(2,1)} %bitcast.17, ...), custom_call_target="tpu_custom_call" | custom-call | bytes 35000 | tf_op jit(solution)/shard_map/load/pallas_call | solution.py:827
  9.9 1.7 %collective-permute-start.2 = (bf16[136,1280]{1,0:T(8,128)(2,1)S(1)}, bf16[136,1280]{1,0:T(8,128)(2,1)S(1)}, u32[]{:S(2)}, u32[]{:S(2)}) collective-permute-start(bf16[136,1280]{1,0:T(8,128)(2,1)S(1)} %end_state.1.refs_13_), channel_id=1, source_target_pairs={{0,4},{12,8},{1,5},{13,9},{2,6},{14,10},{3,7},{15,11},{16,20},{28,... | collective-permute-start | bytes 1044488 | tf_op jit(solution)/shard_map/ppermute | solution.py:900
  12.3 2.8 %collective-permute-done.1.refs_2_ = bf16[136,1280]{1,0:T(8,128)(2,1)S(1)} collective-permute-done((bf16[136,1280]{1,0:T(8,128)(2,1)S(1)}, bf16[136,1280]{1,0:T(8,128)(2,1)S(1)}, u32[]{:S(2)}, u32[]{:S(2)}) %collective-permute-start.1) | collective-permute-done | bytes 348192 | tf_op jit(solution)/shard_map/ppermute | solution.py:900
  15.9 2.7 %inside_block.3 = (f32[256,768]{1,0:T(8,128)S(1)}, f32[256,768]{1,0:T(8,128)S(1)}, bf16[256,768]{1,0:T(8,128)(2,1)S(1)}, bf16[256,768]{1,0:T(8,128)(2,1)S(1)}, b...) custom-call(bf16[256,2560]{1,0:T(8,128)(2,1)S(1)} %get-tuple-element., ...), custom_call_target="tpu_custom_call" | custom-call | bytes 9450000 | tf_op jit(solution)/shard_map/inside_block/pallas_call | solution.py:827
  18.6 2.9 %collective-permute-done.2.refs_4_ = bf16[136,1280]{1,0:T(8,128)(2,1)S(1)} collective-permute-done((bf16[136,1280]{1,0:T(8,128)(2,1)S(1)}, bf16[136,1280]{1,0:T(8,128)(2,1)S(1)}, u32[]{:S(2)}, u32[]{:S(2)}) %collective-permute-start.2) | collective-permute-done | bytes 348192 | tf_op jit(solution)/shard_map/ppermute | solution.py:900
  22.3 1.5 %collective-permute-start.6 = (bf16[128,1280]{1,0:T(8,128)(2,1)S(1)}, bf16[128,1280]{1,0:T(8,128)(2,1)S(1)}, u32[]{:S(2)}, u32[]{:S(2)}) collective-permute-start(bf16[128,1280]{1,0:T(8,128)(2,1)S(1)} %message.4.refs_8_), channel_id=1, source_target_pairs={{8,12},{4,0},{9,13},{5,1},{10,14},{6,2},{11,15},{7,3},{24,28},{20,... | collective-permute-start | bytes 983048 | tf_op jit(solution)/shard_map/ppermute | solution.py:900
  23.8 5.2 %inside_block.4 = (f32[256,1408]{1,0:T(8,128)S(1)}, f32[256,1408]{1,0:T(8,128)S(1)}, bf16[256,1408]{1,0:T(8,128)(2,1)S(1)}, bf16[256,1408]{1,0:T(8,128)(2,1)S(1)...) custom-call(bf16[256,2560]{1,0:T(8,128)(2,1)S(1)} %get-tuple-element, ...), custom_call_target="tpu_custom_call" | custom-call | bytes 9450000 | tf_op jit(solution)/shard_map/inside_block/pallas_call | solution.py:827
  29.1 1.3 %collective-permute-start.7 = (bf16[128,1280]{1,0:T(8,128)(2,1)S(1)}, bf16[128,1280]{1,0:T(8,128)(2,1)S(1)}, u32[]{:S(2)}, u32[]{:S(2)}) collective-permute-start(bf16[128,1280]{1,0:T(8,128)(2,1)S(1)} %message.5.refs_8_), channel_id=1, source_target_pairs={{8,12},{4,0},{9,13},{5,1},{10,14},{6,2},{11,15},{7,3},{24,28},{20,... | collective-permute-start | bytes 983048 | tf_op jit(solution)/shard_map/ppermute | solution.py:900
  30.4 1.3 %inside_block.5 = (f32[256,384]{1,0:T(8,128)S(1)}, f32[256,384]{1,0:T(8,128)S(1)}, bf16[256,384]{1,0:T(8,128)(2,1)S(1)}, bf16[256,384]{1,0:T(8,128)(2,1)S(1)}, b...) custom-call(bf16[256,2560]{1,0:T(8,128)(2,1)S(1)} %get-tuple-element., ...), custom_call_target="tpu_custom_call" | custom-call | bytes 9450000 | tf_op jit(solution)/shard_map/inside_block/pallas_call | solution.py:827
  32.0 1.3 %collective-permute-start.5 = (bf16[8,1280]{1,0:T(8,128)(2,1)S(1)}, bf16[8,1280]{1,0:T(8,128)(2,1)S(1)}, u32[]{:S(2)}, u32[]{:S(2)}) collective-permute-start(bf16[8,1280]{1,0:T(8,128)(2,1)S(1)} %edge.1.refs_4_.edge_ref), channel_id=1, source_target_pairs={{4,0},{8,4},{12,8},{5,1},{9,5},{13,9},{6,2},{10,6},{14,10},{7,3},{... | collective-permute-start | bytes 61448 | tf_op jit(solution)/shard_map/ppermute | solution.py:1069
  33.3 3.4 %collective-permute-done.6.refs_15_.refs_10_ = bf16[128,1280]{1,0:T(8,128)(2,1)S(1)} collective-permute-done((bf16[128,1280]{1,0:T(8,128)(2,1)S(1)}, bf16[128,1280]{1,0:T(8,128)(2,1)S(1)}, u32[]{:S(2)}, u32[]{:S(2)}) %collective-permute-start.6) | collective-permute-done | bytes 327712 | tf_op jit(solution)/shard_map/ppermute | solution.py:900
  36.7 2.3 %finish.1 = (bf16[256,2560]{1,0:T(8,128)(2,1)}, bf16[256,2560]{1,0:T(8,128)(2,1)}, f32[8,1280]{1,0:T(8,128)S(1)}, f32[16,1280]{1,0:T(8,128)S(1)}) custom-call(s32[1]{0:T(128)} %bitcast.refs_0_.place_ref, bf16[256,2560]{1,0:T(8,128)(2,1)S(1)} %get-tuple-element.88.refs_2_.refs_3_.refs_0_.refs_1_, ...), custom_call_target="tpu_custom_call" | custom-call | bytes 35000 | tf_op jit(solution)/shard_map/finish/pallas_call | solution.py:827
  39.7 4.1 %collective-permute-done.7.refs_10_.refs_11_.refs_14_ = bf16[128,1280]{1,0:T(8,128)(2,1)S(1)} collective-permute-done((bf16[128,1280]{1,0:T(8,128)(2,1)S(1)}, bf16[128,1280]{1,0:T(8,128)(2,1)S(1)}, u32[]{:S(2)}, u32[]{:S(2)}) %collective-permute-start.7) | collective-permute-done | bytes 327712 | tf_op jit(solution)/shard_map/ppermute | solution.py:900
  44.5 1.2 %collective-permute-done.8.small_dp = f32[8,384]{1,0:T(8,128)S(1)} collective-permute-done((f32[8,384]{1,0:T(8,128)S(1)}, f32[8,384]{1,0:T(8,128)S(1)}, u32[]{:S(2)}, u32[]{:S(2)}) %collective-permute-start.8) | collective-permute-done | bytes 12320 | tf_op jit(solution)/shard_map/ppermute | solution.py:1120
  45.7 1.6 %collective-permute-start.10 = (bf16[272,256]{1,0:T(8,128)(2,1)S(1)}, bf16[272,256]{1,0:T(8,128)(2,1)S(1)}, u32[]{:S(2)}, u32[]{:S(2)}) collective-permute-start(bf16[272,256]{1,0:T(8,128)(2,1)S(1)} %get-tuple-element.140.refs_4_), channel_id=1, source_target_pairs={{0,2},{2,0},{1,3},{3,1},{4,6},{6,4},{5,7},{7,5},{8,10},{10,8},{9,1... | collective-permute-start | bytes 417800 | tf_op jit(solution)/shard_map/ppermute | solution.py:1123
  47.2 1.3 %finish_grad.1 = (bf16[256,1280]{1,0:T(8,128)(2,1)S(1)}, f32[8,1280]{1,0:T(8,128)S(1)}, f32[16,1280]{1,0:T(8,128)S(1)}) custom-call(s32[1]{0:T(128)} %bitcast.refs_0_.place_ref, bf16[256,2560]{1,0:T(8,128)(2,1)S(1)} %get-tuple-element.88.refs_2_.refs_3_.refs_0_.refs_1_, f32[4,2560]{1,0:T(4,128)S(1)} %get-tuple-element.89.refs_4_.refs_5_.refs_3_.refs_2_, ...), custom_call_target="tpu_custom_call" | custom-call | bytes 35000 | tf_op jit(solution)/shard_map/finish_grad/pallas_call | solution.py:827
  48.6 1.3 %collective-permute-done.9.refs_1_ = f32[8,2560]{1,0:T(8,128)S(1)} collective-permute-done((f32[8,2560]{1,0:T(8,128)S(1)}, f32[8,2560]{1,0:T(8,128)S(1)}, u32[]{:S(2)}, u32[]{:S(2)}) %collective-permute-start.9) | collective-permute-done | bytes 81952 | tf_op jit(solution)/shard_map/ppermute | solution.py:1143
  49.9 1.6 %collective-permute-done.10.refs_4_ = bf16[272,256]{1,0:T(8,128)(2,1)S(1)} collective-permute-done((bf16[272,256]{1,0:T(8,128)(2,1)S(1)}, bf16[272,256]{1,0:T(8,128)(2,1)S(1)}, u32[]{:S(2)}, u32[]{:S(2)}) %collective-permute-start.10) | collective-permute-done | bytes 139296 | tf_op jit(solution)/shard_map/ppermute | solution.py:1123
  51.8 2.5 %collective-permute-start.12 = (bf16[8,1664]{1,0:T(8,128)(2,1)S(1)}, bf16[8,1664]{1,0:T(8,128)(2,1)S(1)}, u32[]{:S(2)}, u32[]{:S(2)}) collective-permute-start(bf16[8,1664]{1,0:T(8,128)(2,1)S(1)} %get-tuple-element.145.refs_7_._.refs_1_), channel_id=1, source_target_pairs={{0,8},{4,12},{8,0},{12,4},{1,9},{5,13},{9,1},{13,5},{2,10},{6,14},... | collective-permute-start | bytes 79880 | tf_op jit(solution)/shard_map/ppermute | solution.py:1170
  54.4 1.8 %collective-permute-start.13 = (bf16[8,1664]{1,0:T(8,128)(2,1)S(1)}, bf16[8,1664]{1,0:T(8,128)(2,1)S(1)}, u32[]{:S(2)}, u32[]{:S(2)}) collective-permute-start(bf16[8,1664]{1,0:T(8,128)(2,1)S(1)} %get-tuple-element.145.refs_7_._.refs_1_), channel_id=1, source_target_pairs={{0,12},{4,0},{8,4},{12,8},{1,13},{5,1},{9,5},{13,9},{2,14},{6,2},{... | collective-permute-start | bytes 79880 | tf_op jit(solution)/shard_map/ppermute | solution.py:1170
  56.3 1.4 %write.1 = (bf16[256,2560]{1,0:T(8,128)(2,1)}, bf16[256,2560]{1,0:T(8,128)(2,1)}) custom-call(s32[1]{0:T(128)} %bitcast.refs_0_.place_ref, bf16[256,256]{1,0:T(8,128)(2,1)S(1)} %get-tuple-element.101.refs_7_.refs_6_.refs_1_.refs_3_, f32[4,2560]{1,0:T(4,128)S(1)} %get-tuple-element.89.refs_4_.refs_5_.refs_3_.refs_2_, ...), custom_call_target="tpu_custom_call", output_to_operand_aliasing={{0}: (15, {}), {1}: (16, {})} | custom-call | bytes 2800000 | tf_op jit(solution)/shard_map/write/pallas_call | solution.py:827
  (28 shorter events, 7.3 us)
Async XLA Ops:
  3.4 11.7 %collective-permute-start.1 = (bf16[136,1280]{1,0:T(8,128)(2,1)S(1)}, bf16[136,1280]{1,0:T(8,128)(2,1)S(1)}, u32[]{:S(2)}, u32[]{:S(2)}) collective-permute-start(bf16[136,1280]{1,0:T(8,128)(2,1)S(1)} %first_state.1.refs_7_), channel_id=1, source_target_pairs={{0,4},{12,8},{1,5},{13,9},{2,6},{14,10},{3,7},{15,11},{16,20},{28,... | collective-permute-start | bytes 1044488 | tf_op jit(solution)/shard_map/ppermute | solution.py:900
  9.9 11.5 %collective-permute-start.2 = (bf16[136,1280]{1,0:T(8,128)(2,1)S(1)}, bf16[136,1280]{1,0:T(8,128)(2,1)S(1)}, u32[]{:S(2)}, u32[]{:S(2)}) collective-permute-start(bf16[136,1280]{1,0:T(8,128)(2,1)S(1)} %end_state.1.refs_13_), channel_id=1, source_target_pairs={{0,4},{12,8},{1,5},{13,9},{2,6},{14,10},{3,7},{15,11},{16,20},{28,... | collective-permute-start | bytes 1044488 | tf_op jit(solution)/shard_map/ppermute | solution.py:900
  11.6 0.7 %collective-permute-start = (bf16[8,2816]{1,0:T(8,128)(2,1)S(1)}, bf16[8,2816]{1,0:T(8,128)(2,1)S(1)}, u32[]{:S(2)}, u32[]{:S(2)}) collective-permute-start(bf16[8,2816]{1,0:T(8,128)(2,1)S(1)} %get-tuple-element.81.refs_7_), channel_id=1, source_target_pairs={{4,8},{8,12},{5,9},{9,13},{6,10},{10,14},{7,11},{11,15},{20,24},{2... | collective-permute-start | bytes 135176 | tf_op jit(solution)/shard_map/ppermute | solution.py:934
  15.2 7.0 %collective-permute-start.4 = (bf16[128,1280]{1,0:T(8,128)(2,1)S(1)}, bf16[128,1280]{1,0:T(8,128)(2,1)S(1)}, u32[]{:S(2)}, u32[]{:S(2)}) collective-permute-start(bf16[128,1280]{1,0:T(8,128)(2,1)S(1)} %get-tuple-element.104.refs_8_), channel_id=1, source_target_pairs={{4,8},{8,4},{5,9},{9,5},{6,10},{10,6},{7,11},{11,7},{20,24},{24,20... | collective-permute-start | bytes 983048 | tf_op jit(solution)/shard_map/ppermute | solution.py:900
  21.5 7.5 %collective-permute-start.3 = (bf16[128,1280]{1,0:T(8,128)(2,1)S(1)}, bf16[128,1280]{1,0:T(8,128)(2,1)S(1)}, u32[]{:S(2)}, u32[]{:S(2)}) collective-permute-start(bf16[128,1280]{1,0:T(8,128)(2,1)S(1)} %get-tuple-element.109._), channel_id=1, source_target_pairs={{4,8},{8,4},{5,9},{9,5},{6,10},{10,6},{7,11},{11,7},{20,24},{24,20... | collective-permute-start | bytes 983048 | tf_op jit(solution)/shard_map/ppermute | solution.py:900
  22.3 14.4 %collective-permute-start.6 = (bf16[128,1280]{1,0:T(8,128)(2,1)S(1)}, bf16[128,1280]{1,0:T(8,128)(2,1)S(1)}, u32[]{:S(2)}, u32[]{:S(2)}) collective-permute-start(bf16[128,1280]{1,0:T(8,128)(2,1)S(1)} %message.4.refs_8_), channel_id=1, source_target_pairs={{8,12},{4,0},{9,13},{5,1},{10,14},{6,2},{11,15},{7,3},{24,28},{20,... | collective-permute-start | bytes 983048 | tf_op jit(solution)/shard_map/ppermute | solution.py:900
  29.1 14.7 %collective-permute-start.7 = (bf16[128,1280]{1,0:T(8,128)(2,1)S(1)}, bf16[128,1280]{1,0:T(8,128)(2,1)S(1)}, u32[]{:S(2)}, u32[]{:S(2)}) collective-permute-start(bf16[128,1280]{1,0:T(8,128)(2,1)S(1)} %message.5.refs_8_), channel_id=1, source_target_pairs={{8,12},{4,0},{9,13},{5,1},{10,14},{6,2},{11,15},{7,3},{24,28},{20,... | collective-permute-start | bytes 983048 | tf_op jit(solution)/shard_map/ppermute | solution.py:900
  32.0 12.5 %collective-permute-start.5 = (bf16[8,1280]{1,0:T(8,128)(2,1)S(1)}, bf16[8,1280]{1,0:T(8,128)(2,1)S(1)}, u32[]{:S(2)}, u32[]{:S(2)}) collective-permute-start(bf16[8,1280]{1,0:T(8,128)(2,1)S(1)} %edge.1.refs_4_.edge_ref), channel_id=1, source_target_pairs={{4,0},{8,4},{12,8},{5,1},{9,5},{13,9},{6,2},{10,6},{14,10},{7,3},{... | collective-permute-start | bytes 61448 | tf_op jit(solution)/shard_map/ppermute | solution.py:1069
  44.4 1.2 %collective-permute-start.8 = (f32[8,384]{1,0:T(8,128)S(1)}, f32[8,384]{1,0:T(8,128)S(1)}, u32[]{:S(2)}, u32[]{:S(2)}) collective-permute-start(f32[8,384]{1,0:T(8,128)S(1)} %get-tuple-element.139.small_ref), channel_id=1, source_target_pairs={{0,1},{1,0},{2,3},{3,2},{4,5},{5,4},{6,7},{7,6},{8,9},{9,8},{10,11... | collective-permute-start | bytes 36872 | tf_op jit(solution)/shard_map/ppermute | solution.py:1120
  45.7 5.8 %collective-permute-start.10 = (bf16[272,256]{1,0:T(8,128)(2,1)S(1)}, bf16[272,256]{1,0:T(8,128)(2,1)S(1)}, u32[]{:S(2)}, u32[]{:S(2)}) collective-permute-start(bf16[272,256]{1,0:T(8,128)(2,1)S(1)} %get-tuple-element.140.refs_4_), channel_id=1, source_target_pairs={{0,2},{2,0},{1,3},{3,1},{4,6},{6,4},{5,7},{7,5},{8,10},{10,8},{9,1... | collective-permute-start | bytes 417800 | tf_op jit(solution)/shard_map/ppermute | solution.py:1123
  48.6 1.3 %collective-permute-start.9 = (f32[8,2560]{1,0:T(8,128)S(1)}, f32[8,2560]{1,0:T(8,128)S(1)}, u32[]{:S(2)}, u32[]{:S(2)}) collective-permute-start(f32[8,2560]{1,0:T(8,128)S(1)} %sums.1.refs_0_), channel_id=1, source_target_pairs={{0,1},{1,0},{2,3},{3,2},{4,5},{5,4},{6,7},{7,6},{8,9},{9,8},{10,11... | collective-permute-start | bytes 245768 | tf_op jit(solution)/shard_map/ppermute | solution.py:1143
  51.5 6.2 %collective-permute-start.11 = (bf16[8,1664]{1,0:T(8,128)(2,1)S(1)}, bf16[8,1664]{1,0:T(8,128)(2,1)S(1)}, u32[]{:S(2)}, u32[]{:S(2)}) collective-permute-start(bf16[8,1664]{1,0:T(8,128)(2,1)S(1)} %get-tuple-element.145.refs_7_._.refs_1_), channel_id=1, source_target_pairs={{0,4},{4,8},{8,12},{12,0},{1,5},{5,9},{9,13},{13,1},{2,6},{6,10},{... | collective-permute-start | bytes 79880 | tf_op jit(solution)/shard_map/ppermute | solution.py:1170
  51.8 5.9 %collective-permute-start.12 = (bf16[8,1664]{1,0:T(8,128)(2,1)S(1)}, bf16[8,1664]{1,0:T(8,128)(2,1)S(1)}, u32[]{:S(2)}, u32[]{:S(2)}) collective-permute-start(bf16[8,1664]{1,0:T(8,128)(2,1)S(1)} %get-tuple-element.145.refs_7_._.refs_1_), channel_id=1, source_target_pairs={{0,8},{4,12},{8,0},{12,4},{1,9},{5,13},{9,1},{13,5},{2,10},{6,14},... | collective-permute-start | bytes 79880 | tf_op jit(solution)/shard_map/ppermute | solution.py:1170
  54.4 3.8 %collective-permute-start.13 = (bf16[8,1664]{1,0:T(8,128)(2,1)S(1)}, bf16[8,1664]{1,0:T(8,128)(2,1)S(1)}, u32[]{:S(2)}, u32[]{:S(2)}) collective-permute-start(bf16[8,1664]{1,0:T(8,128)(2,1)S(1)} %get-tuple-element.145.refs_7_._.refs_1_), channel_id=1, source_target_pairs={{0,12},{4,0},{8,4},{12,8},{1,13},{5,1},{9,5},{13,9},{2,14},{6,2},{... | collective-permute-start | bytes 79880 | tf_op jit(solution)/shard_map/ppermute | solution.py:1170
